TPU v7x, 32 devices: a whole 2x2x4 slice. The times are simulated.
32 devices in a mesh: img: 8 (over z, y), grp: 4 (over x, core).
Axes of the slice: x: 2, y: 2, z: 4, core: 2. Of those that a mesh axis runs over, the one named last changes fastest.
Arguments:
- image_in: bfloat16 [1024, 1792], P('img', 'grp'), may hold values from -6 to 6
- text_in: bfloat16 [1024, 1152], P('img', 'grp'), may hold values from -6 to 6
- image_gain: float32 [1792], replicated, may hold values from 0.25 to 1.75
- text_gain: float32 [1152], replicated, may hold values from 0.25 to 1.75
- image_up: bfloat16 [1792, 7680], P('img', 'grp'), may hold values from -0.125 to 0.125
- image_down: bfloat16 [7680, 1792], P('grp', 'img'), may hold values from -0.0625 to 0.0625
- text_up: bfloat16 [1152, 2560], P(None, 'grp'), may hold values from -0.1875 to 0.1875
- text_down: bfloat16 [2560, 1152], P('grp'), may hold values from -0.125 to 0.125
- image_head: bfloat16 [1792, 1152], P('grp'), may hold values from -0.041666667 to 2
- log_scale: float32 [1], replicated, may hold values from 2.4 to 2.9
- bias: float32 [1], replicated, may hold values from -9 to -6
Outputs:
- image_grad: bfloat16 [1024, 1792], P('img', 'grp')
- text_grad: bfloat16 [1024, 1152], P('img', 'grp')
All inputs are finite; a program needn't handle non-finite values.
Results may differ from a plain program's by a relative error of at most 0.0082.
Values may be sent and summed in bfloat16 or wider, within the bound.
No kernel may reach another device: no remote copies, remote signals or barrier semaphores. Data moves between devices by JAX's collectives and lax.ppermute only.
A program may use at most 128 MiB of HBM per device.

v0:
```python
import jax
import jax.numpy as jnp
from jax import lax
from jax.sharding import PartitionSpec as P

EPS = 1e-06


def layer_norm(rows, gain):
    rows = rows.astype(jnp.float32)
    mean = jnp.mean(rows, axis=1, keepdims=True)
    centered = rows - mean
    inverse = lax.rsqrt(jnp.mean(centered * centered, axis=1, keepdims=True) + EPS)
    normed = centered * inverse
    return (normed, inverse, (normed * gain).astype(jnp.bfloat16))


def tower_forward(local_in, gain, up_weight, down_weight):
    whole_in = lax.all_gather(local_in, "grp", axis=1, tiled=True)
    normed, inverse, scaled = layer_norm(whole_in, gain)
    before = jnp.dot(scaled, up_weight, preferred_element_type=jnp.float32)
    hidden = jax.nn.gelu(before, approximate=True).astype(jnp.bfloat16)
    branch = jnp.dot(hidden, down_weight, preferred_element_type=jnp.float32)
    return (whole_in, normed, inverse, before, branch)


def tower_backward(upstream, normed, inverse, before, gain, up_weight, down_weight, local_cols):
    grad_hidden = jnp.einsum("rd,fd->rf", upstream, down_weight, preferred_element_type=jnp.float32)
    _, gelu_back = jax.vjp(lambda value: jax.nn.gelu(value, approximate=True), before)
    grad_before = gelu_back(grad_hidden)[0].astype(jnp.bfloat16)
    grad_scaled = jnp.einsum(
        "rf,df->rd", grad_before, up_weight, preferred_element_type=jnp.float32
    )
    col_start = lax.axis_index("grp") * local_cols
    summed = lax.psum(grad_scaled, "grp")
    scaled_grad = summed * gain
    first = jnp.mean(scaled_grad, axis=1, keepdims=True)
    second = jnp.mean(scaled_grad * normed, axis=1, keepdims=True)
    back = inverse * (scaled_grad - first - normed * second)
    return lax.dynamic_slice_in_dim(back, col_start, local_cols, 1)


def unit_rows(embed):
    inv = lax.rsqrt(jnp.sum(embed * embed, axis=1, keepdims=True) + EPS)
    return (inv, (embed * inv).astype(jnp.bfloat16))


def unit_back(embed, inv, grad):
    along = jnp.sum(embed * grad, axis=1, keepdims=True)
    return inv * (grad - embed * (inv * inv) * along)


def shards(
    image_in,
    text_in,
    image_gain,
    text_gain,
    image_up,
    image_down,
    text_up,
    text_down,
    image_head,
    log_scale,
    bias,
):
    member = lax.axis_index("grp")
    groups = lax.axis_size("grp")
    rows = image_in.shape[0]
    quarter = rows // groups
    image_cols = image_in.shape[1]
    text_cols = text_in.shape[1]
    full_up, full_down = (
        lax.all_gather(image_up, "img", axis=0, tiled=True),
        lax.all_gather(image_down, "img", axis=1, tiled=True),
    )
    img_whole, img_normed, img_inverse, img_before, img_branch = tower_forward(
        image_in, image_gain, full_up, full_down
    )
    image_mid = image_in.astype(jnp.float32) + lax.psum_scatter(
        img_branch, "grp", scatter_dimension=1, tiled=True
    )
    head_part = jnp.dot(
        image_mid.astype(jnp.bfloat16), image_head, preferred_element_type=jnp.float32
    )
    image_embed = lax.psum(head_part, "grp")
    img_inv, image_unit = unit_rows(image_embed)
    txt_whole, txt_normed, txt_inverse, txt_before, txt_branch = tower_forward(
        text_in, text_gain, text_up, text_down
    )
    text_rows = lax.psum_scatter(txt_branch, "grp", scatter_dimension=0, tiled=True)
    own_rows = lax.dynamic_slice_in_dim(txt_whole, member * quarter, quarter, 0).astype(jnp.float32)
    text_embed = own_rows + text_rows
    txt_inv, text_unit = unit_rows(text_embed)
    scale = jnp.exp(log_scale[0])
    shift = bias[0]
    image_ids = lax.axis_index("img") * rows + jnp.arange(rows, dtype=jnp.int32)
    every_text = lax.all_gather(text_unit, "img", axis=0, tiled=True)
    cosine = jnp.einsum("re,ke->rk", image_unit, every_text, preferred_element_type=jnp.float32)
    logits = scale * cosine + shift
    position = jnp.arange(every_text.shape[0], dtype=jnp.int32)
    text_ids = position // quarter * rows + member * quarter + position % quarter
    same = (image_ids[:, None] == text_ids[None, :]).astype(jnp.float32)
    pull = (jax.nn.sigmoid(logits) - same).astype(jnp.bfloat16)
    grad_image_unit = scale * jnp.dot(pull, every_text, preferred_element_type=jnp.float32)
    grad_text_unit = lax.psum_scatter(
        scale * jnp.einsum("rk,re->ke", pull, image_unit, preferred_element_type=jnp.float32),
        "img",
        scatter_dimension=0,
        tiled=True,
    )
    grad_image_unit = lax.psum(grad_image_unit, "grp")
    grad_img_embed16 = unit_back(image_embed, img_inv, grad_image_unit).astype(jnp.bfloat16)
    grad_mid = jnp.einsum(
        "re,de->rd", grad_img_embed16, image_head, preferred_element_type=jnp.float32
    )
    grad_mid_whole = lax.all_gather(grad_mid.astype(jnp.bfloat16), "grp", axis=1, tiled=True)
    img_back = tower_backward(
        grad_mid_whole,
        img_normed,
        img_inverse,
        img_before,
        image_gain,
        full_up,
        full_down,
        image_cols,
    )
    image_grad = (grad_mid + img_back).astype(jnp.bfloat16)
    grad_txt_embed16 = unit_back(text_embed, txt_inv, grad_text_unit).astype(jnp.bfloat16)
    grad_txt_whole = lax.all_gather(grad_txt_embed16, "grp", axis=0, tiled=True)
    txt_back = tower_backward(
        grad_txt_whole,
        txt_normed,
        txt_inverse,
        txt_before,
        text_gain,
        text_up,
        text_down,
        text_cols,
    )
    residual_cols = lax.dynamic_slice_in_dim(
        grad_txt_whole, member * text_cols, text_cols, 1
    ).astype(jnp.float32)
    text_grad = (residual_cols + txt_back).astype(jnp.bfloat16)
    return (image_grad, text_grad)


def solution(mesh):
    in_specs = (
        P("img", "grp"),
        P("img", "grp"),
        P(),
        P(),
        P("img", "grp"),
        P("grp", "img"),
        P(None, "grp"),
        P("grp", None),
        P("grp", None),
        P(),
        P(),
    )
    out_specs = (P("img", "grp"), P("img", "grp"))
    return jax.shard_map(shards, mesh=mesh, in_specs=in_specs, out_specs=out_specs, check_vma=False)
```

profile of v0, /device:TPU:0, one launch (start us, length us, event | category | flops | bytes accessed | tf_op | source)
XLA Modules:
  0.0 431.6 jit_solution(12416112755434285134)
XLA Ops:
  9.6 7.4 %all_gather.24 = bf16[128,1152]{0,1:T(8,128)(2,1)S(1)} all-gather(bf16[128,288]{0,1:T(8,128)(2,1)S(1)} %copy-done.12), channel_id=1, replica_groups=mesh['img'=8,'grp'=4] {'grp'}, dimensions={1}, use_global_device_ids=true | all-gather | bytes 368640 | tf_op jit(solution)/shard_map/all_gather | solution.py:19
  17.6 1.8 fusion.42
  19.4 1.3 fusion.57
  20.8 6.9 %all_gather.21 = bf16[128,1792]{0,1:T(8,128)(2,1)S(1)} all-gather(bf16[128,448]{0,1:T(8,128)(2,1)S(1)} %copy-done.10), channel_id=1, replica_groups=mesh['img'=8,'grp'=4] {'grp'}, dimensions={1}, use_global_device_ids=true | all-gather | bytes 573440 | tf_op jit(solution)/shard_map/all_gather | solution.py:19
  28.3 91.9 %all-gather.3.cloned.1.call-done = bf16[1792,1920]{1,0:T(8,128)(2,1)} async-done(((bf16[224,1920]{1,0:T(8,128)(2,1)}), bf16[1792,1920]{1,0:T(8,128)(2,1)}) %all-gather.3.cloned.1.call-update) | async-done | bytes 6881296 | tf_op jit(solution)/shard_map/all_gather | solution.py:73
  120.2 4.2 fusion.33
  124.4 102.5 %all-gather.5.cloned.1.call-done = bf16[1920,1792]{0,1:T(8,128)(2,1)} async-done(((bf16[1920,224]{0,1:T(8,128)(2,1)}), bf16[1920,1792]{0,1:T(8,128)(2,1)}) %all-gather.5.cloned.1.call-update) | async-done | bytes 6881296 | tf_op jit(solution)/shard_map/all_gather | solution.py:74
  226.9 5.9 %fusion.20 = f32[128,1792]{0,1:T(8,128)} fusion(bf16[1920,1792]{0,1:T(8,128)(2,1)} %all-gather.5.cloned.1.call-done, f32[128,1920]{1,0:T(8,128)S(1)} %fusion.33), kind=kOutput, calls=%fused_computation.38 | convolution fusion | flops 883015680 | bytes 8781824 | tf_op jit(solution)/shard_map/dot_general | solution.py:23
  235.5 1.1 multiply_reduce_fusion.5
  237.1 18.1 %reduce-scatter.4.cloned.1.call-done = f32[128,448]{0,1:T(8,128)} async-done(((f32[128,1792]{0,1:T(8,128)}), f32[128,448]{0,1:T(8,128)}) %reduce-scatter.4.cloned.1.call-update) | async-done | bytes 229392 | tf_op jit(solution)/shard_map/reduce_scatter | solution.py:79
  255.2 2.1 fusion.70
  257.5 31.6 %all_gather.25 = bf16[256,1152]{1,0:T(8,128)(2,1)S(1)} all-gather(bf16[32,1152]{1,0:T(8,128)(2,1)S(1)} %multiply_convert_fusion.12), channel_id=1, replica_groups=mesh['img'=8,'grp'=4] {'img'}, dimensions={0}, use_global_device_ids=true | all-gather | bytes 663552 | tf_op jit(solution)/shard_map/all_gather | solution.py:97
  289.1 2.2 all-reduce.5.cloned.1.call-done
  291.2 1.2 multiply_reduce_fusion.3
  293.6 1.5 fusion.6
  295.8 1.1 convolution_multiply_fusion.1
  296.9 2.2 convolution_multiply_fusion
  299.2 31.4 %all-reduce.7.cloned.1.call-done = f32[128,1152]{1,0:T(8,128)} async-done(((f32[128,1152]{1,0:T(8,128)}), f32[128,1152]{1,0:T(8,128)}) %all-reduce.7.cloned.1.call-update) | async-done | bytes 589840 | tf_op jit(solution)/shard_map/psum | solution.py:111
  330.7 1.3 multiply_reduce_fusion.2
  332.1 1.6 fusion.101
  333.7 6.3 %all_gather.26 = bf16[128,1792]{0,1:T(8,128)(2,1)S(1)} all-gather(bf16[128,448]{0,1:T(8,128)(2,1)S(1)} %get-tuple-element.20), channel_id=1, replica_groups=mesh['img'=8,'grp'=4] {'grp'}, dimensions={1}, use_global_device_ids=true | all-gather | bytes 573440 | tf_op jit(solution)/shard_map/all_gather | solution.py:116
  340.0 9.6 %fusion.21 = f32[128,1792]{0,1:T(8,128)} fusion(bf16[1792,1920]{1,0:T(8,128)(2,1)} %all-gather.3.cloned.1.call-done, f32[128,1920]{1,0:T(8,128)} %copy-done.4, bf16[128,1792]{0,1:T(8,128)(2,1)S(1)} %all_gather.26, bf16[1920,1792]{0,1:T(8,128)(2,1)} %all-gather.5.cloned.1.call-done), kind=kOutput, calls=%fused_computation.39 | convolution fusion | flops 1766522880 | bytes 16121856 | tf_op jit(solution)/shard_map/rf,df->rd/dot_general | solution.py:31
  349.7 16.0 %reduce-scatter.8.cloned.1.call-done = f32[32,1152]{1,0:T(8,128)} async-done(((f32[256,1152]{1,0:T(8,128)}), f32[32,1152]{1,0:T(8,128)}) %reduce-scatter.8.cloned.1.call-update) | async-done | bytes 147472 | tf_op jit(solution)/shard_map/reduce_scatter | solution.py:105
  365.7 1.0 multiply_reduce_fusion.4
  366.8 1.0 multiply_convert_fusion.11
  367.8 6.0 %all_gather.27 = bf16[128,1152]{1,0:T(8,128)(2,1)S(1)} all-gather(bf16[32,1152]{1,0:T(8,128)(2,1)S(1)} %multiply_convert_fusion.11), channel_id=1, replica_groups=mesh['img'=8,'grp'=4] {'grp'}, dimensions={0}, use_global_device_ids=true | all-gather | bytes 368640 | tf_op jit(solution)/shard_map/all_gather | solution.py:129
  373.7 3.4 fusion.58
  377.1 40.8 %all-reduce.9.cloned.1.call-done = (f32[128,1792]{0,1:T(8,128)}, f32[128,1152]{1,0:T(8,128)}) async-done(((f32[128,1792]{0,1:T(8,128)}, f32[128,1152]{1,0:T(8,128)}), (f32[128,1792]{0,1:T(8,128)}, f32[128,1152]{1,0:T(8,128)})) %all-reduce.9.cloned.1.call-update) | async-done | bytes 1507344 | tf_op jit(solution)/shard_map/psum | solution.py:35
  418.0 2.5 fusion.99
  420.7 1.2 fusion.56
  421.9 0.7 copy.19
  422.6 1.6 fusion.52
  (96 shorter events, 6.9 us)
Async XLA Ops:
  8.0 11.4 %copy-start = (bf16[640,1152]{1,0:T(8,128)(2,1)S(1)}, bf16[640,1152]{1,0:T(8,128)(2,1)}, u32[]{:S(2)}) copy-start(bf16[640,1152]{1,0:T(8,128)(2,1)} %param.18) | copy-start | bytes 4423684
  8.0 9.5 %copy-start.15 = (f32[1152]{0:T(1024)S(1)}, f32[1152]{0:T(1024)}, u32[]{:S(2)}) copy-start(f32[1152]{0:T(1024)} %param.14) | copy-start | bytes 13828
  8.0 112.1 %all-gather.3.cloned.1.call-start = ((), (), s32[]{:S(2)}) async-start(), calls=%async_computation.3 | async-start | bytes 7741440 | tf_op jit(solution)/shard_map/all_gather | solution.py:73
  8.8 218.2 %all-gather.5.cloned.1.call-start = ((), (), s32[]{:S(2)}) async-start(), calls=%async_computation.4 | async-start | bytes 7741440 | tf_op jit(solution)/shard_map/all_gather | solution.py:74
  9.5 225.9 %reduce-scatter.6.cloned.1.call-start = ((), (), s32[]{:S(2)}) async-start(), calls=%async_computation.7 | async-start | bytes 737280 | tf_op jit(solution)/shard_map/reduce_scatter | solution.py:90
  17.3 3.4 copy-start.21
  17.5 3.2 copy-start.17
  20.7 99.4 %copy-start.13 = (f32[1792]{0:T(1024)S(1)}, f32[1792]{0:T(1024)}, u32[]{:S(2)}) copy-start(f32[1792]{0:T(1024)} %param.13) | copy-start | bytes 21508
  20.8 234.4 %reduce-scatter.4.cloned.1.call-start = ((), (), s32[]{:S(2)}) async-start(), calls=%async_computation.5 | async-start | bytes 1146880 | tf_op jit(solution)/shard_map/reduce_scatter | solution.py:79
  28.0 96.3 %copy-start.23 = (f32[128]{0:T(128)}, f32[128]{0:T(128)S(1)}, u32[]{:S(2)}) copy-start(f32[128]{0:T(128)S(1)} %broadcast_multiply_fusion.7) | copy-start | bytes 1540
  28.3 96.1 %copy-start.19 = (f32[128]{0:T(128)}, f32[128]{0:T(128)S(1)}, u32[]{:S(2)}) copy-start(f32[128]{0:T(128)S(1)} %add_rsqrt_fusion.3) | copy-start | bytes 1540
  124.4 102.6 %copy-start.4 = (f32[128,1920]{1,0:T(8,128)}, f32[128,1920]{1,0:T(8,128)S(1)}, u32[]{:S(2)}) copy-start(f32[128,1920]{1,0:T(8,128)S(1)} %fusion.33) | copy-start | bytes 2949124
  232.9 22.3 %copy-start.2 = (bf16[448,1152]{1,0:T(8,128)(2,1)S(1)}, bf16[448,1152]{1,0:T(8,128)(2,1)}, u32[]{:S(2)}) copy-start(bf16[448,1152]{1,0:T(8,128)(2,1)} %param.19) | copy-start | bytes 3096580
  232.9 58.4 %all-reduce.5.cloned.1.call-start = ((), (), s32[]{:S(2)}) async-start(), calls=%async_computation.6 | async-start | bytes 1179648 | tf_op jit(solution)/shard_map/psum | solution.py:85
  235.5 22.0 %copy-start.5 = (f32[32,1152]{1,0:T(8,128)S(1)}, f32[32,1152]{1,0:T(8,128)}, u32[]{:S(2)}) copy-start(f32[32,1152]{1,0:T(8,128)} %reduce-scatter.6.cloned.1.call-done) | copy-start | bytes 442372
  237.1 20.3 %copy-start.25 = (f32[32]{0:T(128)}, f32[32]{0:T(128)S(1)}, u32[]{:S(2)}) copy-start(f32[32]{0:T(128)S(1)} %get-tuple-element.17) | copy-start | bytes 388
  257.4 73.3 %all-reduce.7.cloned.1.call-start = ((), (), s32[]{:S(2)}) async-start(), calls=%async_computation.8 | async-start | bytes 1179648 | tf_op jit(solution)/shard_map/psum | solution.py:111
  293.6 3.3 copy-start.1
  296.9 68.8 %reduce-scatter.8.cloned.1.call-start = ((), (), s32[]{:S(2)}) async-start(), calls=%async_computation.9 | async-start | bytes 1327104 | tf_op jit(solution)/shard_map/reduce_scatter | solution.py:105
  299.2 32.8 %copy-start.28 = (f32[128]{0:T(128)S(1)}, f32[128]{0:T(128)}, u32[]{:S(2)}) copy-start(f32[128]{0:T(128)} %copy-done.27) | copy-start | bytes 1540
  299.2 32.8 %copy-start.30 = (f32[128]{0:T(128)S(1)}, f32[128]{0:T(128)}, u32[]{:S(2)}) copy-start(f32[128]{0:T(128)} %get-tuple-element.18) | copy-start | bytes 1540
  299.2 118.7 %all-reduce.9.cloned.1.call-start = ((), (), s32[]{:S(2)}) async-start(), calls=%async_computation.10 | async-start | bytes 3014656 | tf_op jit(solution)/shard_map/psum | solution.py:35
  340.0 26.7 %copy-start.26 = (f32[32]{0:T(128)S(1)}, f32[32]{0:T(128)}, u32[]{:S(2)}) copy-start(f32[32]{0:T(128)} %copy-done.25) | copy-start | bytes 388
  340.0 26.7 %copy-start.29 = (f32[32]{0:T(128)S(1)}, f32[32]{0:T(128)}, u32[]{:S(2)}) copy-start(f32[32]{0:T(128)} %get-tuple-element.16) | copy-start | bytes 388
  340.0 33.7 %copy-start.7 = (f32[128,640]{1,0:T(8,128)S(1)}, f32[128,640]{1,0:T(8,128)}, u32[]{:S(2)}) copy-start(f32[128,640]{1,0:T(8,128)} %copy-done.6) | copy-start | bytes 983044
  373.7 3.4 copy-start.9
  377.1 40.8 %copy-start.14 = (f32[1792]{0:T(1024)S(1)}, f32[1792]{0:T(1024)}, u32[]{:S(2)}) copy-start(f32[1792]{0:T(1024)} %param.13) | copy-start | bytes 21508
  377.1 40.8 %copy-start.20 = (f32[128]{0:T(128)S(1)}, f32[128]{0:T(128)}, u32[]{:S(2)}) copy-start(f32[128]{0:T(128)} %copy-done.19) | copy-start | bytes 1540
  377.1 40.8 %copy-start.24 = (f32[128]{0:T(128)S(1)}, f32[128]{0:T(128)}, u32[]{:S(2)}) copy-start(f32[128]{0:T(128)} %copy-done.23) | copy-start | bytes 1540
  417.9 2.5 copy-start.8
  417.9 2.5 copy-start.16
  417.9 2.5 copy-start.18
  (7 other events, 9.4 us)
Sparse Core Ops, SparseCore 0:
  11.1 109.0 all-gather.2
  122.3 104.5 all-gather.4
  301.5 64.1 reduce-scatter.7
Sparse Core Ops, SparseCore 1:
  20.8 23.2 reduce-scatter.5
  233.0 22.1 reduce-scatter.3
  257.5 33.7 all-reduce.4
  296.9 33.7 all-reduce.6
  377.2 40.6 all-reduce.8
where the time goes:
time: 432 us
  waiting for transfers between devices  304 us (70%)
  blocking collectives  58.2 us (13%)
  matrix products  34.8 us (8%)
  between operations  17.2 us (4%)
  other arithmetic  14.4 us (3%)
    all_gather x1, waiting for transfers between devices, shards(): lax.all_gather(image_down, 'img', axis=1, tiled=True)  103 us
    all_gather x1, waiting for transfers between devices, shards(): lax.all_gather(image_up, 'img', axis=0, tiled=True)  91.9 us
    psum x1, waiting for transfers between devices, tower_backward(): summed = lax.psum(grad_scaled, 'grp')  40.8 us
    all_gather x1, blocking collectives, shards(): every_text = lax.all_gather(text_unit, 'img', axis=0, tiled=True)  31.6 us
    psum x1, waiting for transfers between devices, shards(): grad_image_unit = lax.psum(grad_image_unit, 'grp')  31.4 us
    reduce_scatter x1, waiting for transfers between devices, shards(): lax.psum_scatter(img_branch, 'grp', scatter_dimension=1, tiled=True)  18.1 us
    reduce_scatter x1, waiting for transfers between devices, shards(): lax.psum_scatter(scale * jnp.einsum('rk,re->ke', pull, image_unit, prefer...  16 us
    all_gather x2, blocking collectives, tower_forward(): whole_in = lax.all_gather(local_in, 'grp', axis=1, tiled=True)  14.3 us
  transfers between devices with their start and end apart: 8, of which 7 were waited for; matrix products, arithmetic and copies ran while one was open for 7% of the time, Pallas kernels for 0%

commit v1 on v0

v1 whole, which is shorter than its diff:
```python
import jax
import jax.numpy as jnp
from jax import lax
from jax.sharding import PartitionSpec as P

EPS = 1e-06
BF16 = jnp.bfloat16
F32 = jnp.float32


def swap(value, axis, flip):
    return lax.ppermute(value, axis, [(i, i ^ flip) for i in range(lax.axis_size(axis))])


def pick(index, options):
    chosen = options[0]
    for at, option in enumerate(options[1:], 1):
        chosen = jnp.where(index == at, option, chosen)
    return chosen


def place(parts, index, flips):
    whole = jnp.zeros((len(flips),) + parts[0].shape, parts[0].dtype)
    for part, flip in zip(parts, flips):
        whole = lax.dynamic_update_index_in_dim(whole, part, index ^ flip, 0)
    return whole


def dot(left, right, left_dim, right_dim):
    dims = (((left_dim,), (right_dim,)), ((), ()))
    return lax.dot_general(left, right, dims, preferred_element_type=F32)


def gather_hidden(shard, img):
    members = lax.axis_size("img")
    top = members // 2
    half = shard.shape[1] // 2
    low, high = shard[:, :half], shard[:, half:]
    upper = img >= top
    own = jnp.where(upper, high, low)
    other = swap(jnp.where(upper, low, high), "img", top)
    held, flips = jnp.stack([own, other]), [0, top]
    bit = top // 2
    while bit > 2:
        held = jnp.concatenate([held, swap(held, "img", bit)])
        flips = flips + [flip ^ bit for flip in flips]
        bit //= 2
    middle = len(flips) // 2
    by_one, by_two = swap(held, "img", 1), swap(held, "img", 2)
    both = [swap(by_one[:middle], "img", 2), swap(by_two[middle:], "img", 1)]
    blocks, places = [], []
    for array, extra in ((held, 0), (by_one, 1), (by_two, 2)):
        blocks += [array[at] for at in range(len(flips))]
        places += [flip ^ extra for flip in flips]
    blocks += [array[at] for array in both for at in range(middle)]
    places += [flip ^ 3 for flip in flips]
    return place(blocks, img, places).reshape(members * shard.shape[0], half)


def stats(rows):
    rows = rows.astype(F32)
    mean = jnp.mean(rows, axis=-1, keepdims=True)
    centered = rows - mean
    inverse = lax.rsqrt(jnp.mean(centered * centered, axis=-1, keepdims=True) + EPS)
    return mean, inverse


def scatter_rows(partial, grp):
    x, core = grp // 2, grp % 2
    lead = partial.shape[:-3]
    split = partial.reshape(lead + (2, 2) + partial.shape[-2:])
    axis = len(lead) + 1
    keep = lax.dynamic_index_in_dim(split, core, axis, False)
    send = lax.dynamic_index_in_dim(split, 1 - core, axis, False)
    total = keep + swap(send.astype(BF16), "grp", 1).astype(F32)
    keep = lax.dynamic_index_in_dim(total, x, axis - 1, False)
    send = lax.dynamic_index_in_dim(total, 1 - x, axis - 1, False)
    return keep + swap(send.astype(BF16), "grp", 2).astype(F32)


def packed(data, sums):
    high = lax.reduce_precision(sums, 8, 7)
    columns = [data.astype(BF16), high.astype(BF16), (sums - high).astype(BF16)]
    used = data.shape[-1] + 4
    columns.append(jnp.zeros(data.shape[:-1] + (-used % 128,), BF16))
    return jnp.concatenate(columns, axis=-1)


def unpacked(payload, cols):
    payload = payload.astype(F32)
    high, low = payload[..., cols : cols + 2], payload[..., cols + 2 : cols + 4]
    return payload[..., :cols], high + low


def scatter_cols(partial, gain, normed, grp, upper, top):
    x, core = grp // 2, grp % 2
    cols = partial.shape[-1] // 4
    scaled_grad = partial * gain
    sums = jnp.stack([jnp.sum(scaled_grad, -1), jnp.sum(scaled_grad * normed, -1)], -1)
    blocks = [partial[..., at * cols : (at + 1) * cols] for at in range(4)]
    keep = [jnp.where(core == 1, blocks[at + 1], blocks[at]) for at in (0, 2)]
    send = [jnp.where(core == 1, blocks[at], blocks[at + 1]) for at in (0, 2)]
    got = swap(jnp.stack([packed(part, sums) for part in send]), "grp", 1)
    pairs = [unpacked(got[at], cols) for at in (0, 1)]
    keep = [part + pair[0] for part, pair in zip(keep, pairs)]
    sums = sums + pairs[0][1]
    send = jnp.where(x == 1, keep[0], keep[1])
    keep = jnp.where(x == 1, keep[1], keep[0])
    data, more = unpacked(swap(packed(send, sums), "grp", 2), cols)
    keep, sums = keep + data, sums + more
    if top:
        rows = keep.shape[0] // 2
        keep, sums = keep.reshape(2, rows, cols), sums.reshape(2, rows, 2)
        send = jnp.where(upper, packed(keep[0], sums[0]), packed(keep[1], sums[1]))
        data, more = unpacked(swap(send, "img", top), cols)
        keep = jnp.where(upper, keep[1], keep[0]) + data
        sums = jnp.where(upper, sums[1], sums[0]) + more
    return keep, sums


def norm_back(grad, sums, rows, mean, inverse, gain, grp, features):
    cols = rows.shape[1]
    own_gain = lax.dynamic_slice_in_dim(gain, grp * cols, cols, 0)
    normed = (rows.astype(F32) - mean) * inverse
    first, second = sums[:, 0:1] / features, sums[:, 1:2] / features
    return inverse * (grad * own_gain - first - normed * second)


def unit_rows(embed):
    inv = lax.rsqrt(jnp.sum(embed * embed, axis=1, keepdims=True) + EPS)
    return inv, (embed * inv).astype(BF16)


def unit_back(embed, inv, grad):
    along = jnp.sum(embed * grad, axis=1, keepdims=True)
    return inv * (grad - embed * (inv * inv) * along)


def gelu16(before):
    return jax.nn.gelu(before, approximate=True).astype(BF16)


def gelu_back16(before, grad):
    _, back = jax.vjp(lambda value: jax.nn.gelu(value, approximate=True), before)
    return back(grad)[0].astype(BF16)


def shards(
    image_in,
    text_in,
    image_gain,
    text_gain,
    image_up,
    image_down,
    text_up,
    text_down,
    image_head,
    log_scale,
    bias,
):
    img, grp = lax.axis_index("img"), lax.axis_index("grp")
    members = lax.axis_size("img")
    top = members // 2
    upper = img >= top
    rows, image_cols = image_in.shape
    quarter = rows // 4
    text_cols = text_in.shape[1]
    image_features, text_features = image_cols * 4, text_cols * 4
    embed_width = image_head.shape[1]
    scale = jnp.exp(log_scale[0])
    shift = bias[0]

    with jax.named_scope("weights"):
        up = gather_hidden(image_up, img)
        down = gather_hidden(image_down.T, img)

    with jax.named_scope("image_rows"):
        far_in = swap(image_in, "img", top)
        near = lax.all_gather(image_in, "grp", axis=1, tiled=True)
        far = lax.all_gather(far_in, "grp", axis=1, tiled=True)
        whole = jnp.concatenate([jnp.where(upper, far, near), jnp.where(upper, near, far)])
        mean, inverse = stats(whole)
        normed = (whole.astype(F32) - mean) * inverse
        scaled = (normed * image_gain).astype(BF16)

    with jax.named_scope("text_forward"):
        text_whole = lax.all_gather(text_in, "grp", axis=1, tiled=True)
        text_mean, text_inverse = stats(text_whole)
        text_normed = (text_whole.astype(F32) - text_mean) * text_inverse
        text_before = dot((text_normed * text_gain).astype(BF16), text_up, 1, 0)
        text_branch = dot(gelu16(text_before), text_down, 1, 0)
        text_sum = scatter_rows(text_branch.reshape(4, quarter, text_features), grp)
        own_rows = lax.dynamic_slice_in_dim(text_whole, grp * quarter, quarter, 0)
        text_embed = own_rows.astype(F32) + text_sum
        text_inv, text_unit = unit_rows(text_embed)

    with jax.named_scope("text_units"):
        held, flips, bit = text_unit[None], [0], 1
        while bit < members:
            held = jnp.concatenate([held, swap(held, "img", bit)])
            flips = flips + [flip ^ bit for flip in flips]
            bit *= 2
        share = place([held[at] for at in range(members)], img, flips)
        share = share.reshape(members * quarter, embed_width)
        pair = jnp.stack([share, swap(share, "grp", 2)])
        every = jnp.concatenate([pair, swap(pair, "grp", 1)])
        every_flips = [0, 2, 1, 3]
        every_text = every.reshape(4 * members * quarter, embed_width)
        at = jnp.arange(members * quarter, dtype=jnp.int32)
        share_ids = at // quarter * rows + at % quarter
        text_ids = jnp.concatenate([share_ids + (grp ^ flip) * quarter for flip in every_flips])

    with jax.named_scope("head"):
        pair = jnp.stack([image_head, swap(image_head, "grp", 2)])
        pairs = [pair, swap(pair, "grp", 1)]
        blocks = [block[at] for block in pairs for at in (0, 1)]
        head = place(blocks, grp, every_flips).reshape(image_features, embed_width)

    with jax.named_scope("image_forward"):
        before = dot(scaled, up, 1, 0)
        branch = dot(gelu16(before), down, 1, 1)
        branch = scatter_rows(branch.reshape(2, 4, quarter, image_features), grp)
        send = jnp.where(upper, branch[0], branch[1]).astype(BF16)
        branch = jnp.where(upper, branch[1], branch[0]) + swap(send, "img", top).astype(F32)
        start = upper.astype(jnp.int32) * rows + grp * quarter
        image_mid = lax.dynamic_slice_in_dim(whole, start, quarter, 0).astype(F32) + branch
        image_embed = dot(image_mid.astype(BF16), head, 1, 0)
        image_inv, image_unit = unit_rows(image_embed)

    with jax.named_scope("image_loss"):
        image_ids = img * rows + grp * quarter + jnp.arange(quarter, dtype=jnp.int32)
        logits = scale * dot(image_unit, every_text, 1, 1) + shift
        same = (image_ids[:, None] == text_ids[None, :]).astype(F32)
        pull = (jax.nn.sigmoid(logits) - same).astype(BF16)
        grad_image_unit = scale * dot(pull, every_text, 1, 0)
        grad_embed16 = unit_back(image_embed, image_inv, grad_image_unit).astype(BF16)
        grad_mid16 = dot(grad_embed16, head, 1, 1).astype(BF16)

    with jax.named_scope("image_backward"):
        far_grad = swap(grad_mid16, "img", top)
        near = lax.all_gather(grad_mid16, "grp", axis=0, tiled=True)
        far = lax.all_gather(far_grad, "grp", axis=0, tiled=True)
        upstream = jnp.concatenate([jnp.where(upper, far, near), jnp.where(upper, near, far)])
        grad_before = gelu_back16(before, dot(upstream, down, 1, 0))
        partial = dot(grad_before, up, 1, 1)
        grad, sums = scatter_cols(partial, image_gain, normed, grp, upper, top)
        own_mean = jnp.where(upper, mean[rows:], mean[:rows])
        own_inverse = jnp.where(upper, inverse[rows:], inverse[:rows])
        back = norm_back(
            grad, sums, image_in, own_mean, own_inverse, image_gain, grp, image_features
        )
        own_grad = pick(grp, [near[:, at * image_cols : (at + 1) * image_cols] for at in range(4)])
        image_grad = (own_grad.astype(F32) + back).astype(BF16)

    with jax.named_scope("text_loss"):
        image_units = lax.all_gather(image_unit, "grp", axis=0, tiled=True)
        logits = scale * dot(image_units, share, 1, 1) + shift
        group_ids = img * rows + jnp.arange(rows, dtype=jnp.int32)
        same = (group_ids[:, None] == (share_ids + grp * quarter)[None, :]).astype(F32)
        pull = (jax.nn.sigmoid(logits) - same).astype(BF16)
        partial = (scale * dot(pull, image_units, 0, 0)).astype(BF16)
        partial = partial.reshape(members, quarter, embed_width)
        parts = lax.all_to_all(partial, "img", split_axis=0, concat_axis=0, tiled=True)
        grad_text_unit = jnp.sum(parts.astype(F32), axis=0)
        grad_text16 = unit_back(text_embed, text_inv, grad_text_unit).astype(BF16)

    with jax.named_scope("text_backward"):
        upstream = lax.all_gather(grad_text16, "grp", axis=0, tiled=True)
        grad_before = gelu_back16(text_before, dot(upstream, text_down, 1, 1))
        partial = dot(grad_before, text_up, 1, 1)
        grad, sums = scatter_cols(partial, text_gain, text_normed, grp, upper, 0)
        back = norm_back(
            grad, sums, text_in, text_mean, text_inverse, text_gain, grp, text_features
        )
        own_grad = pick(
            grp, [upstream[:, at * text_cols : (at + 1) * text_cols] for at in range(4)]
        )
        text_grad = (own_grad.astype(F32) + back).astype(BF16)
    return (image_grad, text_grad)


def solution(mesh):
    in_specs = (
        P("img", "grp"),
        P("img", "grp"),
        P(),
        P(),
        P("img", "grp"),
        P("grp", "img"),
        P(None, "grp"),
        P("grp", None),
        P("grp", None),
        P(),
        P(),
    )
    out_specs = (P("img", "grp"), P("img", "grp"))
    return jax.shard_map(shards, mesh=mesh, in_specs=in_specs, out_specs=out_specs, check_vma=False)
```

time: 432 us -> 329 us (0.76)
  waiting for transfers between devices: 304 us -> 82.5 us
  local copies, waits for them, and re-layouts: 2.37 us -> 60.8 us
  starting transfers between devices: 0.34 us -> 46.9 us
  other arithmetic: 14.4 us -> 34.2 us
  between operations: 17.2 us -> 3.05 us
  blocking collectives: 58.2 us -> 65.6 us
    all_gather x2 -> x0, waiting for transfers between devices: 194 us -> none  [the longest x1 103 us: shards(): lax.all_gather(image_down, 'img', axis=1, tiled=True)]
    psum x3 -> x0, waiting for transfers between devices: 74.4 us -> none  [the longest x1 40.8 us: tower_backward(): summed = lax.psum(grad_scaled, 'grp')]
    ppermute x0 -> x29, waiting for transfers between devices: none -> 68.3 us  [swap(): lax.ppermute(value, axis, [(i, i ^ flip) for i in range(lax.axis_size(axi...]
    ppermute x0 -> x29, starting transfers between devices: none -> 42 us  [swap(): lax.ppermute(value, axis, [(i, i ^ flip) for i in range(lax.axis_size(axi...]
    reduce_scatter x3 -> x0, waiting for transfers between devices: 34.1 us -> none  [the longest x1 18.1 us: shards(): lax.psum_scatter(img_branch, 'grp', scatter_dimension=1, tiled=True)]
    unnamed x63 -> x126, local copies, waits for them, and re-layouts: 2.16 us -> 24.8 us
    dynamic_update_slice x0 -> x21, local copies, waits for them, and re-layouts: none -> 15.1 us  [place(): whole = lax.dynamic_update_index_in_dim(whole, part, index ^ flip, 0)]
    all_to_all x0 -> x1, waiting for transfers between devices: none -> 14.2 us  [shards(): lax.all_to_all(partial, 'img', split_axis=0, concat_axis=0, tiled=True)]
  transfers between devices with their start and end apart: 8 -> 30, of which waited for: 7 -> 10; matrix products, arithmetic and copies ran while one was open for 7% -> 26% of each run, Pallas kernels for 0% -> 0%
where the time goes in v1:
time: 329 us; the launch traced here: 327 us
  waiting for transfers between devices  82.5 us (25%)
  blocking collectives  65.6 us (20%)
  local copies, waits for them, and re-layouts  60.8 us (18%)
  starting transfers between devices  46.9 us (14%)
  other arithmetic  34.2 us (10%)
  matrix products  34.1 us (10%)
    ppermute x29, waiting for transfers between devices, swap(): lax.ppermute(value, axis, [(i, i ^ flip) for i in range(lax.axis_size(axi...  68.3 us
    ppermute x29, starting transfers between devices, swap(): lax.ppermute(value, axis, [(i, i ^ flip) for i in range(lax.axis_size(axi...  42 us
    dot_general x10, matrix products, dot(): return lax.dot_general(left, right, dims, preferred_element_type=F32)  34.1 us
    all_gather x1, blocking collectives, shards(): text_whole = lax.all_gather(text_in, 'grp', axis=1, tiled=True)  24.8 us
    unnamed x126, local copies, waits for them, and re-layouts  24.8 us
    dynamic_update_slice x21, local copies, waits for them, and re-layouts, place(): whole = lax.dynamic_update_index_in_dim(whole, part, index ^ flip, 0)  15.1 us
    all_to_all x1, waiting for transfers between devices, shards(): lax.all_to_all(partial, 'img', split_axis=0, concat_axis=0, tiled=True)  14.2 us
    all_gather x1, blocking collectives, shards(): far = lax.all_gather(far_grad, 'grp', axis=0, tiled=True)  7.5 us
  transfers between devices with their start and end apart: 30, of which 10 were waited for; matrix products, arithmetic and copies ran while one was open for 26% of the time, Pallas kernels for 0%

profile of v1, /device:TPU:0, one launch (start us, length us, event | category | flops | bytes accessed | tf_op | source)
XLA Modules:
  0.0 327.1 jit_solution(13392182779689233603)
XLA Ops:
  0.7 4.1 %collective-permute-start = (bf16[128,448]{0,1:T(8,128)(2,1)}, bf16[128,448]{0,1:T(8,128)(2,1)}, u32[]{:S(2)}, u32[]{:S(2)}) collective-permute-start(bf16[128,448]{0,1:T(8,128)(2,1)} %param.11), channel_id=1, source_target_pairs={{0,16},{4,20},{8,24},{12,28},{16,0},{20,4},{24,8},{28,12},{1,17},{... | collective-permute-start | bytes 344072 | tf_op jit(solution)/shard_map/image_rows/ppermute | solution.py:12
  9.2 2.7 collective-permute-start.6
  13.4 24.8 %all_gather.23 = bf16[128,1152]{0,1:T(8,128)(2,1)S(1)} all-gather(bf16[128,288]{0,1:T(8,128)(2,1)S(1)} %copy-done.24), channel_id=1, replica_groups=mesh['img'=8,'grp'=4] {'grp'}, dimensions={1}, use_global_device_ids=true | all-gather | bytes 368640 | tf_op jit(solution)/shard_map/text_forward/all_gather | solution.py:187
  41.1 6.8 %all_gather.22 = bf16[128,1792]{0,1:T(8,128)(2,1)S(1)} all-gather(bf16[128,448]{0,1:T(8,128)(2,1)S(1)} %copy-done.22), channel_id=1, replica_groups=mesh['img'=8,'grp'=4] {'grp'}, dimensions={1}, use_global_device_ids=true | all-gather | bytes 573440 | tf_op jit(solution)/shard_map/image_rows/all_gather | solution.py:179
  51.8 2.3 broadcast.222.clone.1
  55.4 2.3 broadcast_in_dim.74
  65.1 7.4 %all_gather.21 = bf16[128,1792]{0,1:T(8,128)(2,1)S(1)} all-gather(bf16[128,448]{0,1:T(8,128)(2,1)} %collective-permute-done), channel_id=1, replica_groups=mesh['img'=8,'grp'=4] {'grp'}, dimensions={1}, use_global_device_ids=true | all-gather | bytes 573440 | tf_op jit(solution)/shard_map/image_rows/all_gather | solution.py:180
  76.9 3.2 collective-permute-done.17
  96.5 37.8 %collective-permute-done.20 = bf16[4,32,1152]{2,1,0:T(8,128)(2,1)S(1)} collective-permute-done((bf16[4,32,1152]{2,1,0:T(8,128)(2,1)S(1)}, bf16[4,32,1152]{2,1,0:T(8,128)(2,1)S(1)}, u32[]{:S(2)}, u32[]{:S(2)}) %collective-permute-start.20) | collective-permute-done | bytes 294944 | tf_op jit(solution)/shard_map/text_units/ppermute | solution.py:12
  137.4 2.4 collective-permute-start.4
  140.0 14.8 %collective-permute-done.7 = bf16[2,224,960]{2,1,0:T(8,128)(2,1)S(1)} collective-permute-done((bf16[2,224,960]{2,1,0:T(8,128)(2,1)S(1)}, bf16[2,224,960]{2,1,0:T(8,128)(2,1)S(1)}, u32[]{:S(2)}, u32[]{:S(2)}) %collective-permute-start.7) | collective-permute-done | bytes 860192 | tf_op jit(solution)/shard_map/weights/ppermute | solution.py:12
  158.2 2.5 collective-permute-start.9
  167.2 2.8 multiply_convert_fusion
  175.7 3.4 %fusion.190 = f32[2,2,2,32,1792]{4,3,2,1,0:T(8,128)S(1)} fusion(bf16[2,2,2,32,960]{4,3,2,1,0:T(8,128)(2,1)} %bitcast.127, bf16[1792,960,1,1,1]{1,0,4,3,2:T(8,128)(2,1)} %bitcast.8), kind=kOutput, calls=%fused_computation.330 | convolution fusion | flops 880803840 | bytes 5767168 | tf_op jit(solution)/shard_map/image_forward/dot_general | solution.py:31
  186.6 4.4 %collective-permute-done.12 = bf16[2,32,1792]{2,1,0:T(8,128)(2,1)S(1)} collective-permute-done((bf16[2,32,1792]{2,1,0:T(8,128)(2,1)S(1)}, bf16[2,32,1792]{2,1,0:T(8,128)(2,1)S(1)}, u32[]{:S(2)}, u32[]{:S(2)}) %collective-permute-start.12) | collective-permute-done | bytes 229408 | tf_op jit(solution)/shard_map/image_forward/ppermute | solution.py:12
  191.0 6.5 %collective-permute-start.13 = (bf16[32,1792]{1,0:T(8,128)(2,1)S(1)}, bf16[32,1792]{1,0:T(8,128)(2,1)S(1)}, u32[]{:S(2)}, u32[]{:S(2)}) collective-permute-start(bf16[32,1792]{1,0:T(8,128)(2,1)S(1)} %fusion.110), channel_id=1, source_target_pairs={{0,16},{4,20},{8,24},{12,28},{16,0},{20,4},{24,8},{28,12},{1,17},{... | collective-permute-start | bytes 344072 | tf_op jit(solution)/shard_map/image_forward/ppermute | solution.py:12
  197.5 2.8 pad_maximum_fusion
  203.0 3.8 %multiply_reduce_fusion.5 = (f32[32]{0:T(128)S(1)}, f32[32,1152]{1,0:T(8,128)}) fusion(bf16[1792,1152]{1,0:T(8,128)(2,1)} %bitcast.17, bf16[32,1792]{1,0:T(8,128)(2,1)S(1)} %collective-permute-done.13, f32[2,32,1792]{2,1,0:T(8,128)S(1)} %bitcast_add_fusion.1, s32[]{:T(128)S(6)} %select_n.336, bf16[128,1792]{1,0:T(8,128)(2,1)S(1)} %get-tuple-element.39, ...), kind=kOutput, calls=%fused_computation.180 | convolution fusion | flops 132710368 | bytes 5767301 | tf_op jit(solution)/shard_map/image_forward/dot_general | solution.py:31
  206.8 4.4 %multiply_reduce_fusion.3 = (f32[32]{0:T(128)S(1)}, f32[32,1152]{1,0:T(8,128)}) fusion(f32[32,1152]{1,0:T(8,128)} %get-tuple-element.85, bf16[1024,1152]{1,0:T(8,128)(2,1)} %bitcast.115, s32[1024]{0:T(1024)S(1)} %pad_add_fusion, f32[]{:T(128)} %bitcast.113, f32[]{:T(128)} %bitcast.18, s32[32]{0:T(128)S(1)} %iota_add_fusion.1, f32[32]{0:T(128)S(1)} %get-tuple-element.81), kind=kOutput, calls=%fused_computation.175 | convolution fusion | flops 151474144 | bytes 2658696 | tf_op jit(solution)/shard_map/image_loss/dot_general | solution.py:31
  211.2 4.2 %convolution_convert_fusion = bf16[32,1792]{1,0:T(8,128)(2,1)} fusion(bf16[1792,1152]{1,0:T(8,128)(2,1)} %bitcast.17, f32[32,1152]{1,0:T(8,128)} %get-tuple-element.87, f32[32,1152]{1,0:T(8,128)} %get-tuple-element.85, f32[32]{0:T(128)S(1)} %get-tuple-element.86, f32[32]{0:T(128)S(1)} %get-tuple-element.80, f32[32]{0:T(128)S(1)} %get-tuple-element.81), kind=kOutput, calls=%fused_computation.6 | convolution fusion | flops 132362240 | bytes 4538752 | tf_op jit(solution)/shard_map/image_loss/dot_general | solution.py:31
  215.7 6.8 %all_gather.24 = bf16[128,1792]{1,0:T(8,128)(2,1)S(1)} all-gather(bf16[32,1792]{1,0:T(8,128)(2,1)} %convolution_convert_fusion), channel_id=1, replica_groups=mesh['img'=8,'grp'=4] {'grp'}, dimensions={0}, use_global_device_ids=true | all-gather | bytes 573440 | tf_op jit(solution)/shard_map/image_backward/all_gather | solution.py:241
  230.0 7.5 %all_gather.25 = bf16[128,1792]{1,0:T(8,128)(2,1)S(1)} all-gather(bf16[32,1792]{1,0:T(8,128)(2,1)} %collective-permute-done.23), channel_id=1, replica_groups=mesh['img'=8,'grp'=4] {'grp'}, dimensions={0}, use_global_device_ids=true | all-gather | bytes 573440 | tf_op jit(solution)/shard_map/image_backward/all_gather | solution.py:242
  239.6 9.2 %multiply_reduce_fusion = (f32[256]{0:T(256)S(1)}, f32[256]{0:T(256)S(1)}, f32[256,1792]{1,0:T(8,128)}) fusion(f32[1792]{0:T(1024)S(1)} %copy-done.53, f32[256]{0:T(256)S(1)} %copy-done.42, f32[256]{0:T(256)S(1)} %copy-done.34, bf16[128,1792]{1,0:T(8,128)(2,1)S(1)} %get-tuple-element.39, bf16[128,1792]{1,0:T(8,128)(2,1)S(1)} %get-tuple-element.38, ...), kind=kOutput, calls=%fused_computation.15 | convolution fusion | flops 1772944896 | bytes 11545600 | tf_op jit(solution)/shard_map/image_backward/dot_general | solution.py:31
  248.8 3.0 fusion.177
  259.2 6.3 %all_gather.26 = bf16[128,1152]{1,0:T(8,128)(2,1)} all-gather(bf16[32,1152]{1,0:T(8,128)(2,1)S(1)} %multiply_convert_fusion.6), channel_id=1, replica_groups=mesh['img'=8,'grp'=4] {'grp'}, dimensions={0}, use_global_device_ids=true | all-gather | bytes 368640 | tf_op jit(solution)/shard_map/text_loss/all_gather | solution.py:256
  268.5 2.8 fusion
  271.3 4.9 %all-to-all-start = ((bf16[8,32,1152]{2,1,0:T(8,128)(2,1)}), bf16[8,32,1152]{2,1,0:T(8,128)(2,1)}, u32[]{:S(2)}, u32[]{:S(2)}) async-start(bf16[8,32,1152]{2,1,0:T(8,128)(2,1)} %bitcast.126), calls=%async_computation | async-start | bytes 1179648 | tf_op jit(solution)/shard_map/text_loss/all_to_all | solution.py:263
  279.5 2.7 collective-permute-start.26
  282.2 14.2 %all-to-all-done = bf16[8,32,1152]{2,1,0:T(8,128)(2,1)} async-done(((bf16[8,32,1152]{2,1,0:T(8,128)(2,1)}), bf16[8,32,1152]{2,1,0:T(8,128)(2,1)}, u32[]{:S(2)}, u32[]{:S(2)}) %all-to-all-start) | async-done | bytes 589856 | tf_op jit(solution)/shard_map/text_loss/all_to_all | solution.py:263
  297.8 5.9 %all_gather.27 = bf16[128,1152]{1,0:T(8,128)(2,1)S(1)} all-gather(bf16[32,1152]{1,0:T(8,128)(2,1)S(1)} %multiply_convert_fusion.3), channel_id=1, replica_groups=mesh['img'=8,'grp'=4] {'grp'}, dimensions={0}, use_global_device_ids=true | all-gather | bytes 368640 | tf_op jit(solution)/shard_map/text_backward/all_gather | solution.py:268
  303.7 2.5 multiply_reduce_fusion.1
  322.4 3.0 collective-permute-done.28
  (291 shorter events, 111.6 us)
Async XLA Ops:
  0.7 64.4 %collective-permute-start = (bf16[128,448]{0,1:T(8,128)(2,1)}, bf16[128,448]{0,1:T(8,128)(2,1)}, u32[]{:S(2)}, u32[]{:S(2)}) collective-permute-start(bf16[128,448]{0,1:T(8,128)(2,1)} %param.11), channel_id=1, source_target_pairs={{0,16},{4,20},{8,24},{12,28},{16,0},{20,4},{24,8},{28,12},{1,17},{... | collective-permute-start | bytes 344072 | tf_op jit(solution)/shard_map/image_rows/ppermute | solution.py:12
  6.9 80.1 %collective-permute-start.1 = (bf16[224,960]{1,0:T(8,128)(2,1)}, bf16[224,960]{1,0:T(8,128)(2,1)}, u32[]{:S(2)}, u32[]{:S(2)}) collective-permute-start(bf16[224,960]{1,0:T(8,128)(2,1)} %broadcast_select_fusion.1), channel_id=1, source_target_pairs={{0,16},{4,20},{8,24},{12,28},{16,0},{20,4},{24,8},{28,12},{1,17},{... | collective-permute-start | bytes 1290248 | tf_op jit(solution)/shard_map/weights/ppermute | solution.py:12
  9.2 81.0 %collective-permute-start.6 = (bf16[224,960]{1,0:T(8,128)(2,1)}, bf16[224,960]{1,0:T(8,128)(2,1)}, u32[]{:S(2)}, u32[]{:S(2)}) collective-permute-start(bf16[224,960]{1,0:T(8,128)(2,1)} %broadcast_select_fusion), channel_id=1, source_target_pairs={{0,16},{4,20},{8,24},{12,28},{16,0},{20,4},{24,8},{28,12},{1,17},{... | collective-permute-start | bytes 1290248 | tf_op jit(solution)/shard_map/weights/ppermute | solution.py:12
  11.9 167.2 %collective-permute-start.14 = (bf16[448,1152]{1,0:T(8,128)(2,1)}, bf16[448,1152]{1,0:T(8,128)(2,1)}, u32[]{:S(2)}, u32[]{:S(2)}) collective-permute-start(bf16[448,1152]{1,0:T(8,128)(2,1)} %param.19), channel_id=1, source_target_pairs={{0,2},{1,3},{2,0},{3,1},{4,6},{5,7},{6,4},{7,5},{8,10},{9,11},{10,... | collective-permute-start | bytes 3096584 | tf_op jit(solution)/shard_map/head/ppermute | solution.py:12
  40.7 34.6 %collective-permute-start.16 = (bf16[2,32,1152]{2,1,0:T(8,128)(2,1)}, bf16[2,32,1152]{2,1,0:T(8,128)(2,1)S(1)}, u32[]{:S(2)}, u32[]{:S(2)}) collective-permute-start(bf16[2,32,1152]{2,1,0:T(8,128)(2,1)} %fusion.97), channel_id=1, source_target_pairs={{0,1},{1,0},{2,3},{3,2},{4,5},{5,4},{6,7},{7,6},{8,9},{9,8},{10,11... | collective-permute-start | bytes 442376 | tf_op jit(solution)/shard_map/text_forward/ppermute | solution.py:12
  75.0 90.3 %copy-start.33 = (f32[256]{0:T(256)}, f32[256]{0:T(256)S(1)}, u32[]{:S(2)}) copy-start(f32[256]{0:T(256)S(1)} %broadcast_multiply_fusion) | copy-start | bytes 3076
  75.5 4.6 %collective-permute-start.17 = (bf16[32,1152]{1,0:T(8,128)(2,1)S(1)}, bf16[32,1152]{1,0:T(8,128)(2,1)S(1)}, u32[]{:S(2)}, u32[]{:S(2)}) collective-permute-start(bf16[32,1152]{1,0:T(8,128)(2,1)S(1)} %fusion.119), channel_id=1, source_target_pairs={{0,2},{1,3},{2,0},{3,1},{4,6},{5,7},{6,4},{7,5},{8,10},{9,11},{10,... | collective-permute-start | bytes 221192 | tf_op jit(solution)/shard_map/text_forward/ppermute | solution.py:12
  76.9 88.4 %copy-start.41 = (f32[256]{0:T(256)}, f32[256]{0:T(256)S(1)}, u32[]{:S(2)}) copy-start(f32[256]{0:T(256)S(1)} %add_rsqrt_fusion) | copy-start | bytes 3076
  80.9 4.4 %collective-permute-start.18 = (bf16[1,32,1152]{2,1,0:T(8,128)(2,1)S(1)}, bf16[1,32,1152]{2,1,0:T(8,128)(2,1)S(1)}, u32[]{:S(2)}, u32[]{:S(2)}) collective-permute-start(bf16[1,32,1152]{2,1,0:T(8,128)(2,1)S(1)} %get-tuple-element.21), channel_id=1, source_target_pairs={{0,4},{4,0},{8,12},{12,8},{16,20},{20,16},{24,28},{28,24},{1,5},{5... | collective-permute-start | bytes 221192 | tf_op jit(solution)/shard_map/text_units/ppermute | solution.py:12
  85.4 10.4 %collective-permute-start.19 = (bf16[2,32,1152]{2,1,0:T(8,128)(2,1)S(1)}, bf16[2,32,1152]{2,1,0:T(8,128)(2,1)S(1)}, u32[]{:S(2)}, u32[]{:S(2)}) collective-permute-start(bf16[2,32,1152]{2,1,0:T(8,128)(2,1)S(1)} %pad_maximum_fusion.13), channel_id=1, source_target_pairs={{0,8},{4,12},{8,0},{12,4},{16,24},{20,28},{24,16},{28,20},{1,9},{5... | collective-permute-start | bytes 442376 | tf_op jit(solution)/shard_map/text_units/ppermute | solution.py:12
  88.1 49.3 %collective-permute-start.3 = (bf16[2,224,960]{2,1,0:T(8,128)(2,1)S(1)}, bf16[2,224,960]{2,1,0:T(8,128)(2,1)S(1)}, u32[]{:S(2)}, u32[]{:S(2)}) collective-permute-start(bf16[2,224,960]{2,1,0:T(8,128)(2,1)S(1)} %pad_maximum_fusion.4), channel_id=1, source_target_pairs={{0,8},{4,12},{8,0},{12,4},{16,24},{20,28},{24,16},{28,20},{1,9},{5... | collective-permute-start | bytes 2580488 | tf_op jit(solution)/shard_map/weights/ppermute | solution.py:12
  88.7 47.2 %collective-permute-start.2 = (bf16[2,224,960]{2,1,0:T(8,128)(2,1)S(1)}, bf16[2,224,960]{2,1,0:T(8,128)(2,1)S(1)}, u32[]{:S(2)}, u32[]{:S(2)}) collective-permute-start(bf16[2,224,960]{2,1,0:T(8,128)(2,1)S(1)} %pad_maximum_fusion.4), channel_id=1, source_target_pairs={{0,4},{4,0},{8,12},{12,8},{16,20},{20,16},{24,28},{28,24},{1,5},{5... | collective-permute-start | bytes 2580488 | tf_op jit(solution)/shard_map/weights/ppermute | solution.py:12
  91.3 66.9 %collective-permute-start.8 = (bf16[2,224,960]{2,1,0:T(8,128)(2,1)S(1)}, bf16[2,224,960]{2,1,0:T(8,128)(2,1)S(1)}, u32[]{:S(2)}, u32[]{:S(2)}) collective-permute-start(bf16[2,224,960]{2,1,0:T(8,128)(2,1)S(1)} %pad_maximum_fusion.5), channel_id=1, source_target_pairs={{0,8},{4,12},{8,0},{12,4},{16,24},{20,28},{24,16},{28,20},{1,9},{5... | collective-permute-start | bytes 2580488 | tf_op jit(solution)/shard_map/weights/ppermute | solution.py:12
  95.8 38.5 %collective-permute-start.20 = (bf16[4,32,1152]{2,1,0:T(8,128)(2,1)S(1)}, bf16[4,32,1152]{2,1,0:T(8,128)(2,1)S(1)}, u32[]{:S(2)}, u32[]{:S(2)}) collective-permute-start(bf16[4,32,1152]{2,1,0:T(8,128)(2,1)S(1)} %pad_maximum_fusion.11), channel_id=1, source_target_pairs={{0,16},{4,20},{8,24},{12,28},{16,0},{20,4},{24,8},{28,12},{1,17},{... | collective-permute-start | bytes 884744 | tf_op jit(solution)/shard_map/text_units/ppermute | solution.py:12
  134.3 20.5 %collective-permute-start.7 = (bf16[2,224,960]{2,1,0:T(8,128)(2,1)S(1)}, bf16[2,224,960]{2,1,0:T(8,128)(2,1)S(1)}, u32[]{:S(2)}, u32[]{:S(2)}) collective-permute-start(bf16[2,224,960]{2,1,0:T(8,128)(2,1)S(1)} %pad_maximum_fusion.5), channel_id=1, source_target_pairs={{0,4},{4,0},{8,12},{12,8},{16,20},{20,16},{24,28},{28,24},{1,5},{5... | collective-permute-start | bytes 2580488 | tf_op jit(solution)/shard_map/weights/ppermute | solution.py:12
  135.9 45.6 %collective-permute-start.21 = (bf16[256,1152]{1,0:T(8,128)(2,1)S(1)}, bf16[256,1152]{1,0:T(8,128)(2,1)}, u32[]{:S(2)}, u32[]{:S(2)}) collective-permute-start(bf16[256,1152]{1,0:T(8,128)(2,1)S(1)} %bitcast.116), channel_id=1, source_target_pairs={{0,2},{1,3},{2,0},{3,1},{4,6},{5,7},{6,4},{7,5},{8,10},{9,11},{10,... | collective-permute-start | bytes 1769480 | tf_op jit(solution)/shard_map/text_units/ppermute | solution.py:12
  137.4 25.2 %collective-permute-start.4 = (bf16[1,224,960]{2,1,0:T(8,128)(2,1)S(1)}, bf16[1,224,960]{2,1,0:T(8,128)(2,1)S(1)}, u32[]{:S(2)}, u32[]{:S(2)}) collective-permute-start(bf16[1,224,960]{2,1,0:T(8,128)(2,1)S(1)} %get-tuple-element.42), channel_id=1, source_target_pairs={{0,8},{4,12},{8,0},{12,4},{16,24},{20,28},{24,16},{28,20},{1,9},{5... | collective-permute-start | bytes 1290248 | tf_op jit(solution)/shard_map/weights/ppermute | solution.py:12
  154.8 10.4 %collective-permute-start.5 = (bf16[1,224,960]{2,1,0:T(8,128)(2,1)S(1)}, bf16[1,224,960]{2,1,0:T(8,128)(2,1)S(1)}, u32[]{:S(2)}, u32[]{:S(2)}) collective-permute-start(bf16[1,224,960]{2,1,0:T(8,128)(2,1)S(1)} %get-tuple-element.40), channel_id=1, source_target_pairs={{0,4},{4,0},{8,12},{12,8},{16,20},{20,16},{24,28},{28,24},{1,5},{5... | collective-permute-start | bytes 1290248 | tf_op jit(solution)/shard_map/weights/ppermute | solution.py:12
  158.2 13.9 %collective-permute-start.9 = (bf16[1,224,960]{2,1,0:T(8,128)(2,1)}, bf16[1,224,960]{2,1,0:T(8,128)(2,1)}, u32[]{:S(2)}, u32[]{:S(2)}) collective-permute-start(bf16[1,224,960]{2,1,0:T(8,128)(2,1)} %get-tuple-element.36), channel_id=1, source_target_pairs={{0,8},{4,12},{8,0},{12,4},{16,24},{20,28},{24,16},{28,20},{1,9},{5... | collective-permute-start | bytes 1290248 | tf_op jit(solution)/shard_map/weights/ppermute | solution.py:12
  162.6 11.3 %collective-permute-start.10 = (bf16[1,224,960]{2,1,0:T(8,128)(2,1)}, bf16[1,224,960]{2,1,0:T(8,128)(2,1)}, u32[]{:S(2)}, u32[]{:S(2)}) collective-permute-start(bf16[1,224,960]{2,1,0:T(8,128)(2,1)} %get-tuple-element.34), channel_id=1, source_target_pairs={{0,4},{4,0},{8,12},{12,8},{16,20},{20,16},{24,28},{28,24},{1,5},{5... | collective-permute-start | bytes 1290248 | tf_op jit(solution)/shard_map/weights/ppermute | solution.py:12
  179.1 3.7 %collective-permute-start.11 = (bf16[2,2,32,1792]{3,2,1,0:T(8,128)(2,1)S(1)}, bf16[2,2,32,1792]{3,2,1,0:T(8,128)(2,1)S(1)}, u32[]{:S(2)}, u32[]{:S(2)}) collective-permute-start(bf16[2,2,32,1792]{3,2,1,0:T(8,128)(2,1)S(1)} %fusion.57), channel_id=1, source_target_pairs={{0,1},{1,0},{2,3},{3,2},{4,5},{5,4},{6,7},{7,6},{8,9},{9,8},{10,11... | collective-permute-start | bytes 1376264 | tf_op jit(solution)/shard_map/image_forward/ppermute | solution.py:12
  180.9 19.4 %collective-permute-start.15 = (bf16[2,448,1152]{2,1,0:T(8,128)(2,1)S(1)}, bf16[2,448,1152]{2,1,0:T(8,128)(2,1)S(1)}, u32[]{:S(2)}, u32[]{:S(2)}) collective-permute-start(bf16[2,448,1152]{2,1,0:T(8,128)(2,1)S(1)} %pad_maximum_fusion.1), channel_id=1, source_target_pairs={{0,1},{1,0},{2,3},{3,2},{4,5},{5,4},{6,7},{7,6},{8,9},{9,8},{10,11... | collective-permute-start | bytes 6193160 | tf_op jit(solution)/shard_map/head/ppermute | solution.py:12
  182.7 14.9 %collective-permute-start.22 = (bf16[2,256,1152]{2,1,0:T(8,128)(2,1)S(1)}, bf16[2,256,1152]{2,1,0:T(8,128)(2,1)S(1)}, u32[]{:S(2)}, u32[]{:S(2)}) collective-permute-start(bf16[2,256,1152]{2,1,0:T(8,128)(2,1)S(1)} %pad_maximum_fusion.2), channel_id=1, source_target_pairs={{0,1},{1,0},{2,3},{3,2},{4,5},{5,4},{6,7},{7,6},{8,9},{9,8},{10,11... | collective-permute-start | bytes 3538952 | tf_op jit(solution)/shard_map/text_units/ppermute | solution.py:12
  182.9 8.1 %collective-permute-start.12 = (bf16[2,32,1792]{2,1,0:T(8,128)(2,1)S(1)}, bf16[2,32,1792]{2,1,0:T(8,128)(2,1)S(1)}, u32[]{:S(2)}, u32[]{:S(2)}) collective-permute-start(bf16[2,32,1792]{2,1,0:T(8,128)(2,1)S(1)} %fusion.75), channel_id=1, source_target_pairs={{0,2},{1,3},{2,0},{3,1},{4,6},{5,7},{6,4},{7,5},{8,10},{9,11},{10,... | collective-permute-start | bytes 688136 | tf_op jit(solution)/shard_map/image_forward/ppermute | solution.py:12
  191.0 12.0 %collective-permute-start.13 = (bf16[32,1792]{1,0:T(8,128)(2,1)S(1)}, bf16[32,1792]{1,0:T(8,128)(2,1)S(1)}, u32[]{:S(2)}, u32[]{:S(2)}) collective-permute-start(bf16[32,1792]{1,0:T(8,128)(2,1)S(1)} %fusion.110), channel_id=1, source_target_pairs={{0,16},{4,20},{8,24},{12,28},{16,0},{20,4},{24,8},{28,12},{1,17},{... | collective-permute-start | bytes 344072 | tf_op jit(solution)/shard_map/image_forward/ppermute | solution.py:12
  215.5 14.6 %collective-permute-start.23 = (bf16[32,1792]{1,0:T(8,128)(2,1)}, bf16[32,1792]{1,0:T(8,128)(2,1)}, u32[]{:S(2)}, u32[]{:S(2)}) collective-permute-start(bf16[32,1792]{1,0:T(8,128)(2,1)} %convolution_convert_fusion), channel_id=1, source_target_pairs={{0,16},{4,20},{8,24},{12,28},{16,0},{20,4},{24,8},{28,12},{1,17},{... | collective-permute-start | bytes 344072 | tf_op jit(solution)/shard_map/image_backward/ppermute | solution.py:12
  258.7 6.8 %collective-permute-start.24 = (bf16[2,256,512]{1,2,0:T(8,128)(2,1)S(1)}, bf16[2,256,512]{1,2,0:T(8,128)(2,1)S(1)}, u32[]{:S(2)}, u32[]{:S(2)}) collective-permute-start(bf16[2,256,512]{1,2,0:T(8,128)(2,1)S(1)} %pad_maximum_fusion.6), channel_id=1, source_target_pairs={{0,1},{1,0},{2,3},{3,2},{4,5},{5,4},{6,7},{7,6},{8,9},{9,8},{10,11... | collective-permute-start | bytes 1572872 | tf_op jit(solution)/shard_map/image_backward/ppermute | solution.py:12
  267.5 8.9 %collective-permute-start.25 = (bf16[256,512]{0,1:T(8,128)(2,1)}, bf16[256,512]{0,1:T(8,128)(2,1)}, u32[]{:S(2)}, u32[]{:S(2)}) collective-permute-start(bf16[256,512]{0,1:T(8,128)(2,1)} %maximum_maximum_fusion), channel_id=1, source_target_pairs={{0,2},{1,3},{2,0},{3,1},{4,6},{5,7},{6,4},{7,5},{8,10},{9,11},{10,... | collective-permute-start | bytes 786440 | tf_op jit(solution)/shard_map/image_backward/ppermute | solution.py:12
  271.3 25.1 %all-to-all-start = ((bf16[8,32,1152]{2,1,0:T(8,128)(2,1)}), bf16[8,32,1152]{2,1,0:T(8,128)(2,1)}, u32[]{:S(2)}, u32[]{:S(2)}) async-start(bf16[8,32,1152]{2,1,0:T(8,128)(2,1)} %bitcast.126), calls=%async_computation | async-start | bytes 1179648 | tf_op jit(solution)/shard_map/text_loss/all_to_all | solution.py:263
  279.5 38.7 %collective-permute-start.26 = (bf16[128,512]{0,1:T(8,128)(2,1)}, bf16[128,512]{0,1:T(8,128)(2,1)}, u32[]{:S(2)}, u32[]{:S(2)}) collective-permute-start(bf16[128,512]{0,1:T(8,128)(2,1)} %maximum_select_fusion), channel_id=1, source_target_pairs={{0,16},{4,20},{8,24},{12,28},{16,0},{20,4},{24,8},{28,12},{1,17},{... | collective-permute-start | bytes 393224 | tf_op jit(solution)/shard_map/image_backward/ppermute | solution.py:12
  311.4 7.8 %collective-permute-start.27 = (bf16[2,128,384]{1,2,0:T(8,128)(2,1)}, bf16[2,128,384]{1,2,0:T(8,128)(2,1)}, u32[]{:S(2)}, u32[]{:S(2)}) collective-permute-start(bf16[2,128,384]{1,2,0:T(8,128)(2,1)} %pad_maximum_fusion.12), channel_id=1, source_target_pairs={{0,1},{1,0},{2,3},{3,2},{4,5},{5,4},{6,7},{7,6},{8,9},{9,8},{10,11... | collective-permute-start | bytes 589832 | tf_op jit(solution)/shard_map/text_backward/ppermute | solution.py:12
  320.4 4.9 %collective-permute-start.28 = (bf16[128,384]{0,1:T(8,128)(2,1)S(1)}, bf16[128,384]{0,1:T(8,128)(2,1)S(1)}, u32[]{:S(2)}, u32[]{:S(2)}) collective-permute-start(bf16[128,384]{0,1:T(8,128)(2,1)S(1)} %maximum_maximum_fusion.1), channel_id=1, source_target_pairs={{0,2},{1,3},{2,0},{3,1},{4,6},{5,7},{6,4},{7,5},{8,10},{9,11},{10,... | collective-permute-start | bytes 294920 | tf_op jit(solution)/shard_map/text_backward/ppermute | solution.py:12
  (53 other events, 569.6 us)

commit v2 on v1

v2 whole, which is shorter than its diff:
```python
import jax
import jax.numpy as jnp
from jax import lax
from jax.experimental import pallas as pl
from jax.experimental.pallas import tpu as pltpu
from jax.sharding import PartitionSpec as P

EPS = 1e-06
BF16 = jnp.bfloat16
F32 = jnp.float32
FLIPS = (0, 2, 1, 3)
GELU_C = 0.7978845608028654
GELU_A = 0.044715
VMEM = pl.BlockSpec(memory_space=pltpu.VMEM)
SMEM = pl.BlockSpec(memory_space=pltpu.SMEM)
PARAMS = pltpu.CompilerParams(vmem_limit_bytes=40 * 1024 * 1024)


def swap(value, axis, flip):
    return lax.ppermute(value, axis, [(i, i ^ flip) for i in range(lax.axis_size(axis))])


def place(parts, index, flips):
    whole = jnp.zeros((len(flips),) + parts[0].shape, parts[0].dtype)
    for part, flip in zip(parts, flips):
        whole = lax.dynamic_update_index_in_dim(whole, part, index ^ flip, 0)
    return whole


def dot(left, right, left_dim, right_dim):
    dims = (((left_dim,), (right_dim,)), ((), ()))
    return lax.dot_general(left, right, dims, preferred_element_type=F32)


def take(array, index, axis=0):
    return lax.dynamic_index_in_dim(array, index, axis, False)


def halves(shard, img):
    half = shard.shape[1] // 2
    low, high = shard[:, :half], shard[:, half:]
    upper = img >= lax.axis_size("img") // 2
    return jnp.where(upper, high, low), jnp.where(upper, low, high)


def widen(block, img):
    members = lax.axis_size("img")
    held, flips, bit = block[None], [0], 4
    while bit < members // 2:
        held = jnp.concatenate([held, swap(held, "img", bit)])
        flips = flips + [flip ^ (bit // 4) for flip in flips]
        bit *= 2
    if len(flips) > 1:
        middle = img // 4 % (members // 8)
        held = place([held[at] for at in range(len(flips))], middle, flips)
    return held.reshape(-1, block.shape[1])


def blocked(natural):
    members, rows, width = natural.shape
    if members == 8:
        return natural
    split = natural.reshape(2, members // 8, 4, rows, width)
    return split.transpose(0, 2, 3, 1, 4).reshape(8, rows, members // 8 * width)


def in_order(blocks, members):
    if members == 8:
        return blocks
    rows, width = blocks.shape[1], blocks.shape[2] * 8 // members
    split = blocks.reshape(2, 4, rows, members // 8, width)
    return split.transpose(0, 3, 1, 2, 4).reshape(members, rows, width)


def up_kernel(ids, scaled, *refs):
    weights, before, hidden, gains = refs[:8], refs[8], refs[9], refs[10]
    rows = before.shape[0]
    total = jnp.zeros((scaled.shape[1], before.shape[1]), F32)
    for at in range(8):
        total = total + dot(scaled[ids[0] ^ at], weights[at][...], 1, 0)
    value = total[:rows]
    before[...] = value
    bend = jnp.tanh(GELU_C * (value + GELU_A * value * value * value))
    hidden[...] = (0.5 * value * (1.0 + bend)).astype(BF16)
    gains[...] = jnp.sum(total[rows:], axis=0, keepdims=True)


def down_kernel(ids, hidden, *refs):
    weights, keep, send = refs[:8], refs[8], refs[9]
    _, pairs, quarter, width = keep.shape
    for at in range(8):
        block = ids[0] ^ at
        value = dot(hidden[...], weights[at][...], 1, 1).reshape(pairs, 2, quarter, width)
        odd = ids[1] == 1
        keep[block] = jnp.where(odd, value[:, 1], value[:, 0])
        send[block] = jnp.where(odd, value[:, 0], value[:, 1]).astype(BF16)


def back_kernel(ids, near, far, before, gains, *refs):
    downs, ups, outs, first, second = refs[:8], refs[8:16], refs[16], refs[17], refs[18]
    rows, hidden = before.shape
    half = rows // 2
    total = jnp.zeros((rows, hidden), F32)
    for at in range(8):
        block = ids[0] ^ at
        width = downs[at].shape[0]
        upstream = jnp.concatenate(
            [near[:, block].reshape(half, width), far[:, block].reshape(half, width)]
        )
        total = total + dot(upstream, downs[at][...], 1, 0)
    value = before[...]
    square = value * value
    bend = jnp.tanh(GELU_C * value * (1.0 + GELU_A * square))
    slope = 0.5 * (1.0 + bend) + 0.5 * GELU_C * value * (1.0 - bend * bend) * (
        1.0 + 3.0 * GELU_A * square
    )
    grad16 = (total * slope).astype(BF16)
    grad = grad16.astype(F32)
    first[...] = jnp.sum(grad * gains[...], axis=1, keepdims=True)
    second[...] = jnp.sum(grad * value, axis=1, keepdims=True)
    for at in range(8):
        outs[ids[0] ^ at] = dot(grad16, ups[at][...], 1, 1)


def call(kernel, name, shapes, *operands):
    flops = 2 * 256 * 1792 * 960 * (2 if name == "back" else 1)
    return pl.pallas_call(
        kernel,
        out_shape=shapes,
        in_specs=[SMEM] + [VMEM] * (len(operands) - 1),
        out_specs=tuple(VMEM for _ in shapes),
        compiler_params=PARAMS,
        cost_estimate=pl.CostEstimate(flops=flops, bytes_accessed=6 << 20, transcendentals=0),
        name=name,
    )(*operands)


def norm_stats(rows, axes):
    mean = jnp.mean(rows, axis=axes, keepdims=True)
    centered = rows - mean
    return mean, lax.rsqrt(jnp.mean(centered * centered, axis=axes, keepdims=True) + EPS)


def packed(data, sums):
    high = lax.reduce_precision(sums, 8, 7)
    tail = jnp.concatenate([high, sums - high], -1).astype(BF16)
    return jnp.concatenate([data.astype(BF16), jnp.broadcast_to(tail, data.shape[:-1] + (4,))], -1)


def unpacked(payload, cols):
    payload = payload.astype(F32)
    sums = payload[0, :, cols : cols + 2] + payload[0, :, cols + 2 : cols + 4]
    return payload[..., :cols], sums


def norm_back(grad, sums, rows, mean, inverse, gain, features):
    normed = (rows - mean) * inverse
    first, second = sums[:, 0:1] / features, sums[:, 1:2] / features
    return inverse * (grad * gain - first - normed * second)


def unit_rows(embed):
    inv = lax.rsqrt(jnp.sum(embed * embed, axis=1, keepdims=True) + EPS)
    return inv, (embed * inv).astype(BF16)


def unit_back(embed, inv, grad):
    along = jnp.sum(embed * grad, axis=1, keepdims=True)
    return inv * (grad - embed * (inv * inv) * along)


def gelu16(before):
    return jax.nn.gelu(before, approximate=True).astype(BF16)


def gelu_back16(before, grad):
    _, back = jax.vjp(lambda value: jax.nn.gelu(value, approximate=True), before)
    return back(grad)[0].astype(BF16)


def shards(
    image_in,
    text_in,
    image_gain,
    text_gain,
    image_up,
    image_down,
    text_up,
    text_down,
    image_head,
    log_scale,
    bias,
):
    img, grp = lax.axis_index("img"), lax.axis_index("grp")
    x, core = grp // 2, grp % 2
    members = lax.axis_size("img")
    top = members // 2
    rows, image_cols = image_in.shape
    quarter = rows // 4
    text_cols = text_in.shape[1]
    image_features, text_features = image_cols * 4, text_cols * 4
    width = image_features // members
    share_count = members // 4
    hidden_half = image_up.shape[1] // 2
    embed_width = image_head.shape[1]
    scale = jnp.exp(log_scale[0])
    shift = bias[0]
    ids = jnp.stack([img // top * 4 + img % 4, core]).astype(jnp.int32)

    with jax.named_scope("weights"):
        near_up, far_up = halves(image_up, img)
        far_up = swap(far_up, "img", top)
        near_down, far_down = halves(image_down.T, img)
        far_down = swap(far_down, "img", top)
        ups, downs = [], []
        for near, far in ((near_up, far_up), (near_down, far_down)):
            groups = []
            for block in (near, far):
                block = widen(block, img)
                by_two = swap(block, "img", 2)
                groups += [block, swap(block, "img", 1), by_two, swap(by_two, "img", 1)]
            (downs if ups else ups).extend(groups)

    with jax.named_scope("image_rows"):
        own_in = image_in.reshape(rows, share_count, width).transpose(1, 0, 2)
        both = jnp.stack([own_in, swap(own_in, "img", top)], 1)
        both = jnp.stack([both, swap(both, "grp", 2)])
        both = jnp.concatenate([both, swap(both, "grp", 1)])
        whole = place([both[at] for at in range(4)], grp, FLIPS)
        whole = whole.reshape(members, 2 * rows, width)
        whole32 = whole.astype(F32)
        mean, inverse = norm_stats(whole32, (0, 2))
        gain = image_gain.reshape(members, 1, width)
        scaled = ((whole32 - mean) * inverse * gain).astype(BF16)
        parts, rest = [], gain
        for _ in range(3):
            part = lax.reduce_precision(rest, 8, 7)
            parts.append(part.astype(BF16))
            rest = rest - part
        parts.append(jnp.zeros((members, 13, width), BF16))
        scaled = blocked(jnp.concatenate([scaled] + parts, 1))

    with jax.named_scope("text_forward"):
        pair = jnp.stack([text_in, swap(text_in, "grp", 2)])
        parts = jnp.concatenate([pair, swap(pair, "grp", 1)])
        parts = place([parts[at] for at in range(4)], grp, FLIPS)
        text_whole = parts.transpose(1, 0, 2).reshape(rows, text_features).astype(F32)
        text_mean, text_inverse = norm_stats(text_whole, 1)
        text_normed = (text_whole - text_mean) * text_inverse
        text_before = dot((text_normed * text_gain).astype(BF16), text_up, 1, 0)
        text_branch = dot(gelu16(text_before), text_down, 1, 0)
        text_branch = text_branch.reshape(2, 2, quarter, text_features)
        send = take(text_branch, 1 - core, 1).astype(BF16)
        total = take(text_branch, core, 1) + swap(send, "grp", 1).astype(F32)
        send = take(total, 1 - x).astype(BF16)
        total = take(total, x) + swap(send, "grp", 2).astype(F32)
        text_embed = lax.dynamic_slice_in_dim(text_whole, grp * quarter, quarter, 0) + total
        text_inv, text_unit = unit_rows(text_embed)
        text_gains = jnp.sum(text_up.astype(F32) * text_gain[:, None], axis=0)

    with jax.named_scope("text_units"):
        held, flips, bit = text_unit[None], [0], 1
        while bit < members:
            held = jnp.concatenate([held, swap(held, "img", bit)])
            flips = flips + [flip ^ bit for flip in flips]
            bit *= 2
        share = place([held[at] for at in range(members)], img, flips)
        share = share.reshape(members * quarter, embed_width)
        pair = jnp.stack([share, swap(share, "grp", 2)])
        every = jnp.concatenate([pair, swap(pair, "grp", 1)])
        every_text = every.reshape(4 * members * quarter, embed_width)
        at = jnp.arange(members * quarter, dtype=jnp.int32)
        share_ids = at // quarter * rows + at % quarter
        text_ids = jnp.concatenate([share_ids + (grp ^ flip) * quarter for flip in FLIPS])

    with jax.named_scope("head"):
        pair = jnp.stack([image_head, swap(image_head, "grp", 2)])
        pairs = jnp.concatenate([pair, swap(pair, "grp", 1)])
        head = place([pairs[at] for at in range(4)], grp, FLIPS)
        head = head.reshape(members, width, embed_width)

    with jax.named_scope("image_forward"):
        before, hidden, gains = call(
            up_kernel,
            "up",
            (
                jax.ShapeDtypeStruct((2 * rows, hidden_half), F32),
                jax.ShapeDtypeStruct((2 * rows, hidden_half), BF16),
                jax.ShapeDtypeStruct((1, hidden_half), F32),
            ),
            ids,
            scaled,
            *ups,
        )
        shape = (8, 4, quarter, image_features // 8)
        keep, send = call(
            down_kernel,
            "down",
            (jax.ShapeDtypeStruct(shape, F32), jax.ShapeDtypeStruct(shape, BF16)),
            ids,
            hidden,
            *downs,
        )
        total = (keep + swap(send, "grp", 1).astype(F32)).reshape(8, 2, 2, quarter, -1)
        send = take(total, 1 - x, 2).astype(BF16)
        total = take(total, x, 2) + swap(send, "grp", 2).astype(F32)
        branch = total[:, 0] + swap(total[:, 1].astype(BF16), "img", top).astype(F32)
        own_rows = lax.dynamic_slice_in_dim(whole, grp * quarter, quarter, 1).astype(F32)
        image_mid16 = (own_rows + in_order(branch, members)).astype(BF16)
        image_mid16 = image_mid16.transpose(1, 0, 2).reshape(quarter, image_features)
        image_embed = dot(image_mid16, head.reshape(image_features, embed_width), 1, 0)
        image_inv, image_unit = unit_rows(image_embed)

    with jax.named_scope("image_loss"):
        image_ids = img * rows + grp * quarter + jnp.arange(quarter, dtype=jnp.int32)
        logits = scale * dot(image_unit, every_text, 1, 1) + shift
        same = (image_ids[:, None] == text_ids[None, :]).astype(F32)
        pull = (jax.nn.sigmoid(logits) - same).astype(BF16)
        grad_image_unit = scale * dot(pull, every_text, 1, 0)
        grad_embed16 = unit_back(image_embed, image_inv, grad_image_unit).astype(BF16)
        grad_mid16 = dot(grad_embed16, head.reshape(image_features, embed_width), 1, 1)
        grad_mid16 = grad_mid16.astype(BF16).reshape(quarter, members, width)
        grad_mid16 = blocked(grad_mid16.transpose(1, 0, 2))

    with jax.named_scope("image_backward"):
        far_grad = swap(grad_mid16, "img", top)
        near_whole = lax.all_gather(grad_mid16, "grp")
        far_whole = lax.all_gather(far_grad, "grp")
        partial, first, second = call(
            back_kernel,
            "back",
            (
                jax.ShapeDtypeStruct((8, 2 * rows, image_features // 8), F32),
                jax.ShapeDtypeStruct((2 * rows, 1), F32),
                jax.ShapeDtypeStruct((2 * rows, 1), F32),
            ),
            ids,
            near_whole,
            far_whole,
            before,
            gains,
            *downs,
            *ups,
        )
        sums = jnp.concatenate([first, second], 1)
        partial = in_order(partial, members).reshape(2, 2, share_count, 2 * rows, width)
        send = packed(take(partial, 1 - core, 1), sums)
        got = swap(send, "grp", 1).reshape(2 * share_count, 2 * rows, width + 4)
        data, more = unpacked(got, width)
        total = take(partial, core, 1) + data.reshape(2, share_count, 2 * rows, width)
        sums = sums + more
        data, more = unpacked(swap(packed(take(total, 1 - x), sums), "grp", 2), width)
        total, sums = take(total, x) + data, sums + more
        send = packed(total[:, rows:], sums[rows:])
        data, more = unpacked(swap(send, "img", top), width)
        total, sums = total[:, :rows] + data, sums[:rows] + more
        back = norm_back(
            total,
            sums,
            own_in.astype(F32),
            mean[0, :rows],
            inverse[0, :rows],
            take(gain.reshape(4, share_count, 1, width), grp),
            image_features,
        )
        own_grad = in_order(near_whole.transpose(1, 0, 2, 3).reshape(8, rows, -1), members)
        own_grad = take(own_grad.reshape(4, share_count, rows, width), grp)
        image_grad = (own_grad.astype(F32) + back).astype(BF16)
        image_grad = image_grad.transpose(1, 0, 2).reshape(rows, image_cols)

    with jax.named_scope("text_loss"):
        pair = jnp.stack([image_unit, swap(image_unit, "grp", 2)])
        image_units = jnp.concatenate([pair, swap(pair, "grp", 1)]).reshape(rows, embed_width)
        logits = scale * dot(image_units, share, 1, 1) + shift
        at = jnp.arange(quarter, dtype=jnp.int32)
        group_ids = jnp.concatenate([img * rows + (grp ^ flip) * quarter + at for flip in FLIPS])
        same = (group_ids[:, None] == (share_ids + grp * quarter)[None, :]).astype(F32)
        pull = (jax.nn.sigmoid(logits) - same).astype(BF16)
        partial = (scale * dot(pull, image_units, 0, 0)).astype(BF16)
        partial = partial.reshape(members, quarter, embed_width)
        parts = lax.all_to_all(partial, "img", split_axis=0, concat_axis=0, tiled=True)
        grad_text_unit = jnp.sum(parts.astype(F32), axis=0)
        grad_text16 = unit_back(text_embed, text_inv, grad_text_unit).astype(BF16)

    with jax.named_scope("text_backward"):
        pair = jnp.stack([grad_text16, swap(grad_text16, "grp", 2)])
        parts = jnp.concatenate([pair, swap(pair, "grp", 1)])
        upstream = place([parts[at] for at in range(4)], grp, FLIPS).reshape(rows, text_features)
        grad_before = gelu_back16(text_before, dot(upstream, text_down, 1, 1))
        grad32 = grad_before.astype(F32)
        sums = jnp.stack([jnp.sum(grad32 * text_gains, 1), jnp.sum(grad32 * text_before, 1)], 1)
        blocks = text_up.reshape(4, text_cols, -1)
        partial = {flip: dot(grad_before, take(blocks, grp ^ flip), 1, 1) for flip in FLIPS}
        send = jnp.stack([packed(partial[flip], sums) for flip in (1, 3)])
        data, more = unpacked(swap(send, "grp", 1), text_cols)
        sums = sums + more
        send = packed(partial[2] + data[1], sums)[None]
        more_data, more = unpacked(swap(send, "grp", 2), text_cols)
        total, sums = partial[0] + data[0] + more_data[0], sums + more
        own_gain = lax.dynamic_slice_in_dim(text_gain, grp * text_cols, text_cols, 0)
        back = norm_back(
            total, sums, text_in.astype(F32), text_mean, text_inverse, own_gain, text_features
        )
        own_grad = lax.dynamic_slice_in_dim(upstream, grp * text_cols, text_cols, 1)
        text_grad = (own_grad.astype(F32) + back).astype(BF16)
    return (image_grad, text_grad)


def solution(mesh):
    in_specs = (
        P("img", "grp"),
        P("img", "grp"),
        P(),
        P(),
        P("img", "grp"),
        P("grp", "img"),
        P(None, "grp"),
        P("grp", None),
        P("grp", None),
        P(),
        P(),
    )
    out_specs = (P("img", "grp"), P("img", "grp"))
    return jax.shard_map(shards, mesh=mesh, in_specs=in_specs, out_specs=out_specs, check_vma=False)
```

time: 329 us -> 310 us (0.942)
  blocking collectives: 65.6 us -> 14.4 us
  waiting for transfers between devices: 82.5 us -> 118 us
  matrix products: 34.1 us -> 15.9 us
  Pallas kernels: 0 us -> 9.76 us
  starting transfers between devices: 46.9 us -> 40.9 us
  other arithmetic: 34.2 us -> 40.1 us
  local copies, waits for them, and re-layouts: 60.8 us -> 66.1 us
    all_gather x7 -> x2, blocking collectives: 65.6 us -> 14.4 us  [the longest x1 7.23 us: shards(): near_whole = lax.all_gather(grad_mid16, 'grp')]
    ppermute x29 -> x41, waiting for transfers between devices: 68.3 us -> 118 us  [swap(): lax.ppermute(value, axis, [(i, i ^ flip) for i in range(lax.axis_size(axi...]
    dot_general x10 -> x11, matrix products: 34.1 us -> 15.9 us  [dot(): return lax.dot_general(left, right, dims, preferred_element_type=F32)]
    all_to_all x1, waiting for transfers between devices: 14.2 us -> 0.01 us  [shards(): lax.all_to_all(partial, 'img', split_axis=0, concat_axis=0, tiled=True)]
    unnamed x126 -> x131, local copies, waits for them, and re-layouts: 24.8 us -> 14 us
    pallas_call x0 -> x3, Pallas kernels: none -> 9.76 us  [call(): pl.pallas_call(kernel, out_shape=shapes, in_specs=[SMEM] + [VMEM] * (len(...]
    dynamic_update_slice x21 -> x22, local copies, waits for them, and re-layouts: 15.1 us -> 21.6 us  [place(): whole = lax.dynamic_update_index_in_dim(whole, part, index ^ flip, 0)]
    select_n x6 -> x2, other arithmetic: 9 us -> 3.32 us  [halves(): return (jnp.where(upper, high, low), jnp.where(upper, low, high))]
  transfers between devices with their start and end apart: 30 -> 42, of which waited for: 10 -> 20; matrix products, arithmetic and copies ran while one was open for 26% -> 28% of each run, Pallas kernels for 0% -> 3%
where the time goes in v2:
time: 310 us; the launch traced here: 308 us
  waiting for transfers between devices  118 us (38%)
  local copies, waits for them, and re-layouts  66.1 us (21%)
  starting transfers between devices  40.9 us (13%)
  other arithmetic  40.1 us (13%)
  matrix products  15.9 us (5%)
  blocking collectives  14.4 us (5%)
  Pallas kernels  9.76 us (3%)
  between operations  3.21 us (1%)
    ppermute x41, waiting for transfers between devices, swap(): lax.ppermute(value, axis, [(i, i ^ flip) for i in range(lax.axis_size(axi...  118 us
    ppermute x41, starting transfers between devices, swap(): lax.ppermute(value, axis, [(i, i ^ flip) for i in range(lax.axis_size(axi...  37.3 us
    dynamic_update_slice x22, local copies, waits for them, and re-layouts, place(): whole = lax.dynamic_update_index_in_dim(whole, part, index ^ flip, 0)  21.6 us
    dot_general x11, matrix products, dot(): return lax.dot_general(left, right, dims, preferred_element_type=F32)  15.9 us
    unnamed x131, local copies, waits for them, and re-layouts  14 us
    pallas_call x3, Pallas kernels, call(): pl.pallas_call(kernel, out_shape=shapes, in_specs=[SMEM] + [VMEM] * (len(...  9.76 us
    all_gather x1, blocking collectives, shards(): near_whole = lax.all_gather(grad_mid16, 'grp')  7.23 us
    all_gather x1, blocking collectives, shards(): far_whole = lax.all_gather(far_grad, 'grp')  7.21 us
  transfers between devices with their start and end apart: 42, of which 20 were waited for; matrix products, arithmetic and copies ran while one was open for 28% of the time, Pallas kernels for 3%

profile of v2, /device:TPU:0, one launch (start us, length us, event | category | flops | bytes accessed | tf_op | source)
XLA Modules:
  0.0 308.1 jit_solution(5659492283452477965)
XLA Ops:
  3.0 3.0 collective-permute-start.3
  7.5 2.6 collective-permute-start
  54.6 4.0 %collective-permute-done.26 = bf16[1,32,1152]{2,1,0:T(8,128)(2,1)S(1)} collective-permute-done((bf16[1,32,1152]{2,1,0:T(8,128)(2,1)S(1)}, bf16[1,32,1152]{2,1,0:T(8,128)(2,1)S(1)}, u32[]{:S(2)}, u32[]{:S(2)}) %collective-permute-start.26) | collective-permute-done | bytes 73760 | tf_op jit(solution)/shard_map/text_units/ppermute | solution.py:20
  61.0 2.9 collective-permute-done.27
  66.0 2.6 collective-permute-start.28
  78.2 4.8 %concatenate.65.scaled = bf16[8,272,224]{2,1,0:T(8,128)(2,1)S(1)} concatenate(bf16[8,256,224]{2,1,0:T(8,128)(2,1)} %multiply_convert_fusion, bf16[8,1,224]{2,1,0:T(2,128)(2,1)S(1)} %get-tuple-element.41, bf16[8,1,224]{2,1,0:T(2,128)(2,1)S(1)} %get-tuple-element.40, bf16[8,1,224]{2,1,0:T(2,128)(2,1)S(1)} %get-tuple-element.39, bf16[8,13,224]{2,1,0:T(8,128)(2,1)} %broadcast_in_dim.99), dimensions={1} | concatenate | bytes 1949696 | tf_op jit(solution)/shard_map/image_rows/concatenate | solution.py:241
  88.6 18.1 %collective-permute-done.13.refs_4_ = bf16[224,960]{1,0:T(8,128)(2,1)S(1)} collective-permute-done((bf16[224,960]{1,0:T(8,128)(2,1)}, bf16[224,960]{1,0:T(8,128)(2,1)S(1)}, u32[]{:S(2)}, u32[]{:S(2)}) %collective-permute-start.13) | collective-permute-done | bytes 430112 | tf_op jit(solution)/shard_map/weights/ppermute | solution.py:20
  112.3 6.3 %collective-permute-done.15.refs_6_ = bf16[224,960]{1,0:T(8,128)(2,1)S(1)} collective-permute-done((bf16[224,960]{1,0:T(8,128)(2,1)S(1)}, bf16[224,960]{1,0:T(8,128)(2,1)S(1)}, u32[]{:S(2)}, u32[]{:S(2)}) %collective-permute-start.15) | collective-permute-done | bytes 430112 | tf_op jit(solution)/shard_map/weights/ppermute | solution.py:20
  122.3 2.8 up.1
  126.2 4.0 %collective-permute-done.10.refs_1_ = bf16[224,960]{1,0:T(8,128)(2,1)S(1)} collective-permute-done((bf16[224,960]{1,0:T(8,128)(2,1)S(1)}, bf16[224,960]{1,0:T(8,128)(2,1)S(1)}, u32[]{:S(2)}, u32[]{:S(2)}) %collective-permute-start.10) | collective-permute-done | bytes 430112 | tf_op jit(solution)/shard_map/weights/ppermute | solution.py:20
  130.1 19.7 %collective-permute-done.12.refs_3_ = bf16[224,960]{1,0:T(8,128)(2,1)S(1)} collective-permute-done((bf16[224,960]{1,0:T(8,128)(2,1)}, bf16[224,960]{1,0:T(8,128)(2,1)S(1)}, u32[]{:S(2)}, u32[]{:S(2)}) %collective-permute-start.12) | collective-permute-done | bytes 430112 | tf_op jit(solution)/shard_map/weights/ppermute | solution.py:20
  149.8 8.2 %collective-permute-done.16.refs_7_ = bf16[224,960]{1,0:T(8,128)(2,1)S(1)} collective-permute-done((bf16[224,960]{1,0:T(8,128)(2,1)S(1)}, bf16[224,960]{1,0:T(8,128)(2,1)S(1)}, u32[]{:S(2)}, u32[]{:S(2)}) %collective-permute-start.16) | collective-permute-done | bytes 430112 | tf_op jit(solution)/shard_map/weights/ppermute | solution.py:20
  158.0 2.5 down.1
  166.2 12.3 %collective-permute-done.29 = bf16[256,1152]{1,0:T(8,128)(2,1)S(1)} collective-permute-done((bf16[256,1152]{1,0:T(8,128)(2,1)}, bf16[256,1152]{1,0:T(8,128)(2,1)S(1)}, u32[]{:S(2)}, u32[]{:S(2)}) %collective-permute-start.29) | collective-permute-done | bytes 589856 | tf_op jit(solution)/shard_map/text_units/ppermute | solution.py:20
  178.5 2.4 pad_maximum_fusion.2
  181.0 2.8 collective-permute-done.18
  183.9 2.5 collective-permute-start.19
  187.4 5.3 %collective-permute-done.19 = bf16[8,32,224]{2,1,0:T(8,128)(2,1)S(1)} collective-permute-done((bf16[8,32,224]{2,1,0:T(8,128)(2,1)S(1)}, bf16[8,32,224]{2,1,0:T(8,128)(2,1)S(1)}, u32[]{:S(2)}, u32[]{:S(2)}) %collective-permute-start.19) | collective-permute-done | bytes 114720 | tf_op jit(solution)/shard_map/image_forward/ppermute | solution.py:20
  194.0 3.3 %pad_maximum_fusion = bf16[4,256,1152]{2,1,0:T(8,128)(2,1)} fusion(bf16[2,256,1152]{2,1,0:T(8,128)(2,1)} %collective-permute-done.30, bf16[1,256,1152]{2,1,0:T(8,128)(2,1)} %bitcast.238, bf16[1,256,1152]{2,1,0:T(8,128)(2,1)} %bitcast.34), kind=kLoop, calls=%fused_computation.5 | loop fusion | flops 2359296 | bytes 4718592 | tf_op jit(solution)/shard_map/text_units/concatenate | solution.py:270
  201.8 3.1 %multiply_reduce_fusion.5 = (f32[32]{0:T(128)S(1)}, f32[32,1152]{1,0:T(8,128)S(1)}) fusion(bf16[32,1792]{1,0:T(8,128)(2,1)S(1)} %reshape.277, bf16[1792,1152]{1,0:T(8,128)(2,1)} %bitcast.21), kind=kOutput, calls=%fused_computation.134 | convolution fusion | flops 132194272 | bytes 4391040 | tf_op jit(solution)/shard_map/image_forward/dot_general | solution.py:32
  205.0 3.7 %multiply_reduce_fusion.3 = (f32[32]{0:T(128)S(1)}, f32[32,1152]{1,0:T(8,128)S(1)}) fusion(f32[32,1152]{1,0:T(8,128)S(1)} %get-tuple-element.63, bf16[1024,1152]{1,0:T(8,128)(2,1)} %bitcast.221, s32[1024]{0:T(1024)S(1)} %pad_add_fusion, f32[]{:T(128)} %bitcast.214, f32[]{:T(128)} %bitcast.22, s32[32]{0:T(128)S(1)} %copy-done.55, f32[32]{0:T(128)S(1)} %get-tuple-element.61), kind=kOutput, calls=%fused_computation.129 | convolution fusion | flops 151474144 | bytes 2658696 | tf_op jit(solution)/shard_map/image_loss/dot_general | solution.py:32
  208.7 3.4 %convolution_convert_fusion = bf16[32,1792]{1,0:T(8,128)(2,1)S(1)} fusion(bf16[1792,1152]{1,0:T(8,128)(2,1)} %bitcast.21, f32[32,1152]{1,0:T(8,128)S(1)} %get-tuple-element.65, f32[32,1152]{1,0:T(8,128)S(1)} %get-tuple-element.63, f32[32]{0:T(128)S(1)} %get-tuple-element.64, f32[32]{0:T(128)S(1)} %get-tuple-element.60, f32[32]{0:T(128)S(1)} %get-tuple-element.61), kind=kOutput, calls=%fused_computation.7 | convolution fusion | flops 132362240 | bytes 4538752 | tf_op jit(solution)/shard_map/image_loss/dot_general | solution.py:32
  212.4 7.2 %all-gather = bf16[32,32,224]{2,1,0:T(8,128)(2,1)S(1)} all-gather(bf16[8,32,224]{2,1,0:T(8,128)(2,1)S(1)} %bitcast.245), channel_id=2, replica_groups=mesh['img'=8,'grp'=4] {'grp'}, dimensions={0}, use_global_device_ids=true | all-gather | bytes 573440 | tf_op jit(solution)/shard_map/image_backward/all_gather | solution.py:327
  220.7 3.6 %collective-permute-done.35 = bf16[32,1152]{1,0:T(8,128)(2,1)S(1)} collective-permute-done((bf16[32,1152]{1,0:T(8,128)(2,1)S(1)}, bf16[32,1152]{1,0:T(8,128)(2,1)S(1)}, u32[]{:S(2)}, u32[]{:S(2)}) %collective-permute-start.35) | collective-permute-done | bytes 73760 | tf_op jit(solution)/shard_map/text_loss/ppermute | solution.py:20
  225.0 3.8 %collective-permute-done.31 = bf16[8,32,224]{2,1,0:T(8,128)(2,1)S(1)} collective-permute-done((bf16[8,32,224]{2,1,0:T(8,128)(2,1)S(1)}, bf16[8,32,224]{2,1,0:T(8,128)(2,1)S(1)}, u32[]{:S(2)}, u32[]{:S(2)}) %collective-permute-start.31) | collective-permute-done | bytes 114720 | tf_op jit(solution)/shard_map/image_backward/ppermute | solution.py:20
  228.8 7.2 %all-gather.1 = bf16[32,32,224]{2,1,0:T(8,128)(2,1)S(1)} all-gather(bf16[8,32,224]{2,1,0:T(8,128)(2,1)S(1)} %collective-permute-done.31), channel_id=3, replica_groups=mesh['img'=8,'grp'=4] {'grp'}, dimensions={0}, use_global_device_ids=true | all-gather | bytes 573440 | tf_op jit(solution)/shard_map/image_backward/all_gather | solution.py:328
  242.4 4.4 %back.1 = (f32[8,256,224]{2,1,0:T(8,128)S(1)}, f32[256,1]{1,0:T(8,128)S(1)}, f32[256,1]{1,0:T(8,128)S(1)}) custom-call(s32[2]{0:T(128)S(1)} %pad_add_fusion.1.ids, bf16[4,8,32,224]{3,2,1,0:T(8,128)(2,1)S(1)} %bitcast.216, bf16[4,8,32,224]{3,2,1,0:T(8,128)(2,1)S(1)} %bitcast.218, f32[256,960]{1,0:T(8,128)S(1)} %copy-done.23, ...), custom_call_target="tpu_custom_call" | custom-call | flops 1761607680 | bytes 6291456 | tf_op jit(solution)/shard_map/image_backward/back/pallas_call | solution.py:127
  253.6 2.5 copy.113
  263.9 2.8 fusion
  266.8 3.7 %all-to-all-start = ((bf16[8,32,1152]{2,1,0:T(8,128)(2,1)}), bf16[8,32,1152]{2,1,0:T(8,128)(2,1)S(1)}, u32[]{:S(2)}, u32[]{:S(2)}) async-start(bf16[8,32,1152]{2,1,0:T(8,128)(2,1)} %bitcast.244), calls=%async_computation | async-start | bytes 1179648 | tf_op jit(solution)/shard_map/text_loss/all_to_all | solution.py:381
  275.5 16.3 %collective-permute-done.34 = bf16[2,128,228]{1,2,0:T(8,128)(2,1)} collective-permute-done((bf16[2,128,228]{1,2,0:T(8,128)(2,1)S(1)}, bf16[2,128,228]{1,2,0:T(8,128)(2,1)}, u32[]{:S(2)}, u32[]{:S(2)}) %collective-permute-start.34) | collective-permute-done | bytes 116768 | tf_op jit(solution)/shard_map/image_backward/ppermute | solution.py:20
  304.3 3.0 collective-permute-done.40
  (340 shorter events, 130.1 us)
Async XLA Ops:
  3.0 83.6 %collective-permute-start.3 = (bf16[224,960]{1,0:T(8,128)(2,1)S(1)}, bf16[224,960]{1,0:T(8,128)(2,1)}, u32[]{:S(2)}, u32[]{:S(2)}) collective-permute-start(bf16[224,960]{1,0:T(8,128)(2,1)S(1)} %get-tuple-element.34.refs_0_.refs_8_), channel_id=1, source_target_pairs={{0,4},{4,0},{8,12},{12,8},{16,20},{20,16},{24,28},{28,24},{1,5},{5... | collective-permute-start | bytes 1290248 | tf_op jit(solution)/shard_map/weights/ppermute | solution.py:20
  6.0 81.1 %collective-permute-start.4 = (bf16[224,960]{1,0:T(8,128)(2,1)S(1)}, bf16[224,960]{1,0:T(8,128)(2,1)}, u32[]{:S(2)}, u32[]{:S(2)}) collective-permute-start(bf16[224,960]{1,0:T(8,128)(2,1)S(1)} %get-tuple-element.34.refs_0_.refs_8_), channel_id=1, source_target_pairs={{0,8},{4,12},{8,0},{12,4},{16,24},{20,28},{24,16},{28,20},{1,9},{5... | collective-permute-start | bytes 1290248 | tf_op jit(solution)/shard_map/weights/ppermute | solution.py:20
  7.5 19.3 %collective-permute-start = (bf16[2,128,224]{1,2,0:T(8,128)(2,1)}, bf16[2,128,224]{1,2,0:T(8,128)(2,1)}, u32[]{:S(2)}, u32[]{:S(2)}) collective-permute-start(bf16[2,128,224]{1,2,0:T(8,128)(2,1)} %bitcast.249), channel_id=1, source_target_pairs={{0,16},{4,20},{8,24},{12,28},{16,0},{20,4},{24,8},{28,12},{1,17},{... | collective-permute-start | bytes 344072 | tf_op jit(solution)/shard_map/image_rows/ppermute | solution.py:20
  10.1 72.9 %collective-permute-start.6 = (bf16[224,960]{1,0:T(8,128)(2,1)}, bf16[224,960]{1,0:T(8,128)(2,1)}, u32[]{:S(2)}, u32[]{:S(2)}) collective-permute-start(bf16[224,960]{1,0:T(8,128)(2,1)} %get-tuple-element.33), channel_id=1, source_target_pairs={{0,16},{4,20},{8,24},{12,28},{16,0},{20,4},{24,8},{28,12},{1,17},{... | collective-permute-start | bytes 1290248 | tf_op jit(solution)/shard_map/weights/ppermute | solution.py:20
  10.5 13.9 %collective-permute-start.22 = (bf16[128,288]{0,1:T(8,128)(2,1)}, bf16[128,288]{0,1:T(8,128)(2,1)}, u32[]{:S(2)}, u32[]{:S(2)}) collective-permute-start(bf16[128,288]{0,1:T(8,128)(2,1)} %param.12), channel_id=1, source_target_pairs={{0,2},{1,3},{2,0},{3,1},{4,6},{5,7},{6,4},{7,5},{8,10},{9,11},{10,... | collective-permute-start | bytes 221192 | tf_op jit(solution)/shard_map/text_forward/ppermute | solution.py:20
  29.4 13.9 %collective-permute-start.1 = (bf16[2,2,128,224]{2,3,0,1:T(8,128)(2,1)}, bf16[2,2,128,224]{2,3,0,1:T(8,128)(2,1)}, u32[]{:S(2)}, u32[]{:S(2)}) collective-permute-start(bf16[2,2,128,224]{2,3,0,1:T(8,128)(2,1)} %get-tuple-element.37), channel_id=1, source_target_pairs={{0,2},{1,3},{2,0},{3,1},{4,6},{5,7},{6,4},{7,5},{8,10},{9,11},{10,... | collective-permute-start | bytes 688136 | tf_op jit(solution)/shard_map/image_rows/ppermute | solution.py:20
  40.0 5.5 %collective-permute-start.24 = (bf16[2,32,1152]{2,1,0:T(8,128)(2,1)}, bf16[2,32,1152]{2,1,0:T(8,128)(2,1)}, u32[]{:S(2)}, u32[]{:S(2)}) collective-permute-start(bf16[2,32,1152]{2,1,0:T(8,128)(2,1)} %fusion.57), channel_id=1, source_target_pairs={{0,1},{1,0},{2,3},{3,2},{4,5},{5,4},{6,7},{7,6},{8,9},{9,8},{10,11... | collective-permute-start | bytes 442376 | tf_op jit(solution)/shard_map/text_forward/ppermute | solution.py:20
  43.3 65.5 %collective-permute-start.11 = (bf16[224,960]{1,0:T(8,128)(2,1)S(1)}, bf16[224,960]{1,0:T(8,128)(2,1)}, u32[]{:S(2)}, u32[]{:S(2)}) collective-permute-start(bf16[224,960]{1,0:T(8,128)(2,1)S(1)} %get-tuple-element.32.refs_0_), channel_id=1, source_target_pairs={{0,8},{4,12},{8,0},{12,4},{16,24},{20,28},{24,16},{28,20},{1,9},{5... | collective-permute-start | bytes 1290248 | tf_op jit(solution)/shard_map/weights/ppermute | solution.py:20
  58.7 5.2 %collective-permute-start.27 = (bf16[2,32,1152]{2,1,0:T(8,128)(2,1)S(1)}, bf16[2,32,1152]{2,1,0:T(8,128)(2,1)S(1)}, u32[]{:S(2)}, u32[]{:S(2)}) collective-permute-start(bf16[2,32,1152]{2,1,0:T(8,128)(2,1)S(1)} %pad_maximum_fusion.11), channel_id=1, source_target_pairs={{0,8},{4,12},{8,0},{12,4},{16,24},{20,28},{24,16},{28,20},{1,9},{5... | collective-permute-start | bytes 442376 | tf_op jit(solution)/shard_map/text_units/ppermute | solution.py:20
  66.0 17.5 %collective-permute-start.28 = (bf16[4,32,1152]{2,1,0:T(8,128)(2,1)}, bf16[4,32,1152]{2,1,0:T(8,128)(2,1)}, u32[]{:S(2)}, u32[]{:S(2)}) collective-permute-start(bf16[4,32,1152]{2,1,0:T(8,128)(2,1)} %pad_maximum_fusion.5), channel_id=1, source_target_pairs={{0,16},{4,20},{8,24},{12,28},{16,0},{20,4},{24,8},{28,12},{1,17},{... | collective-permute-start | bytes 884744 | tf_op jit(solution)/shard_map/text_units/ppermute | solution.py:20
  83.1 23.7 %collective-permute-start.13 = (bf16[224,960]{1,0:T(8,128)(2,1)}, bf16[224,960]{1,0:T(8,128)(2,1)S(1)}, u32[]{:S(2)}, u32[]{:S(2)}) collective-permute-start(bf16[224,960]{1,0:T(8,128)(2,1)} %get-tuple-element.31), channel_id=1, source_target_pairs={{0,16},{4,20},{8,24},{12,28},{16,0},{20,4},{24,8},{28,12},{1,17},{... | collective-permute-start | bytes 1290248 | tf_op jit(solution)/shard_map/weights/ppermute | solution.py:20
  83.5 23.3 %collective-permute-start.8 = (bf16[224,960]{1,0:T(8,128)(2,1)}, bf16[224,960]{1,0:T(8,128)(2,1)S(1)}, u32[]{:S(2)}, u32[]{:S(2)}) collective-permute-start(bf16[224,960]{1,0:T(8,128)(2,1)} %collective-permute-done.6.refs_4_.refs_12_), channel_id=1, source_target_pairs={{0,8},{4,12},{8,0},{12,4},{16,24},{20,28},{24,16},{28,20},{1,9},{5... | collective-permute-start | bytes 1290248 | tf_op jit(solution)/shard_map/weights/ppermute | solution.py:20
  86.6 25.2 %collective-permute-start.7 = (bf16[224,960]{1,0:T(8,128)(2,1)}, bf16[224,960]{1,0:T(8,128)(2,1)S(1)}, u32[]{:S(2)}, u32[]{:S(2)}) collective-permute-start(bf16[224,960]{1,0:T(8,128)(2,1)} %collective-permute-done.6.refs_4_.refs_12_), channel_id=1, source_target_pairs={{0,4},{4,0},{8,12},{12,8},{16,20},{20,16},{24,28},{28,24},{1,5},{5... | collective-permute-start | bytes 1290248 | tf_op jit(solution)/shard_map/weights/ppermute | solution.py:20
  87.1 23.2 %collective-permute-start.5 = (bf16[224,960]{1,0:T(8,128)(2,1)}, bf16[224,960]{1,0:T(8,128)(2,1)S(1)}, u32[]{:S(2)}, u32[]{:S(2)}) collective-permute-start(bf16[224,960]{1,0:T(8,128)(2,1)} %collective-permute-done.4.refs_2_.refs_10_), channel_id=1, source_target_pairs={{0,4},{4,0},{8,12},{12,8},{16,20},{20,16},{24,28},{28,24},{1,5},{5... | collective-permute-start | bytes 1290248 | tf_op jit(solution)/shard_map/weights/ppermute | solution.py:20
  106.8 11.8 %collective-permute-start.15 = (bf16[224,960]{1,0:T(8,128)(2,1)S(1)}, bf16[224,960]{1,0:T(8,128)(2,1)S(1)}, u32[]{:S(2)}, u32[]{:S(2)}) collective-permute-start(bf16[224,960]{1,0:T(8,128)(2,1)S(1)} %collective-permute-done.13.refs_4_), channel_id=1, source_target_pairs={{0,8},{4,12},{8,0},{12,4},{16,24},{20,28},{24,16},{28,20},{1,9},{5... | collective-permute-start | bytes 1290248 | tf_op jit(solution)/shard_map/weights/ppermute | solution.py:20
  106.8 13.5 %collective-permute-start.9 = (bf16[224,960]{1,0:T(8,128)(2,1)S(1)}, bf16[224,960]{1,0:T(8,128)(2,1)S(1)}, u32[]{:S(2)}, u32[]{:S(2)}) collective-permute-start(bf16[224,960]{1,0:T(8,128)(2,1)S(1)} %collective-permute-done.8.refs_6_.refs_14_), channel_id=1, source_target_pairs={{0,4},{4,0},{8,12},{12,8},{16,20},{20,16},{24,28},{28,24},{1,5},{5... | collective-permute-start | bytes 1290248 | tf_op jit(solution)/shard_map/weights/ppermute | solution.py:20
  108.9 54.8 %collective-permute-start.20 = (bf16[448,1152]{1,0:T(8,128)(2,1)}, bf16[448,1152]{1,0:T(8,128)(2,1)S(1)}, u32[]{:S(2)}, u32[]{:S(2)}) collective-permute-start(bf16[448,1152]{1,0:T(8,128)(2,1)} %param.19), channel_id=1, source_target_pairs={{0,2},{1,3},{2,0},{3,1},{4,6},{5,7},{6,4},{7,5},{8,10},{9,11},{10,... | collective-permute-start | bytes 3096584 | tf_op jit(solution)/shard_map/head/ppermute | solution.py:20
  110.3 19.8 %collective-permute-start.10 = (bf16[224,960]{1,0:T(8,128)(2,1)S(1)}, bf16[224,960]{1,0:T(8,128)(2,1)S(1)}, u32[]{:S(2)}, u32[]{:S(2)}) collective-permute-start(bf16[224,960]{1,0:T(8,128)(2,1)S(1)} %get-tuple-element.32.refs_0_), channel_id=1, source_target_pairs={{0,4},{4,0},{8,12},{12,8},{16,20},{20,16},{24,28},{28,24},{1,5},{5... | collective-permute-start | bytes 1290248 | tf_op jit(solution)/shard_map/weights/ppermute | solution.py:20
  111.8 38.0 %collective-permute-start.14 = (bf16[224,960]{1,0:T(8,128)(2,1)S(1)}, bf16[224,960]{1,0:T(8,128)(2,1)S(1)}, u32[]{:S(2)}, u32[]{:S(2)}) collective-permute-start(bf16[224,960]{1,0:T(8,128)(2,1)S(1)} %collective-permute-done.13.refs_4_), channel_id=1, source_target_pairs={{0,4},{4,0},{8,12},{12,8},{16,20},{20,16},{24,28},{28,24},{1,5},{5... | collective-permute-start | bytes 1290248 | tf_op jit(solution)/shard_map/weights/ppermute | solution.py:20
  118.6 31.2 %collective-permute-start.12 = (bf16[224,960]{1,0:T(8,128)(2,1)}, bf16[224,960]{1,0:T(8,128)(2,1)S(1)}, u32[]{:S(2)}, u32[]{:S(2)}) collective-permute-start(bf16[224,960]{1,0:T(8,128)(2,1)} %collective-permute-done.11.refs_2_), channel_id=1, source_target_pairs={{0,4},{4,0},{8,12},{12,8},{16,20},{20,16},{24,28},{28,24},{1,5},{5... | collective-permute-start | bytes 1290248 | tf_op jit(solution)/shard_map/weights/ppermute | solution.py:20
  120.3 37.7 %collective-permute-start.16 = (bf16[224,960]{1,0:T(8,128)(2,1)S(1)}, bf16[224,960]{1,0:T(8,128)(2,1)S(1)}, u32[]{:S(2)}, u32[]{:S(2)}) collective-permute-start(bf16[224,960]{1,0:T(8,128)(2,1)S(1)} %collective-permute-done.15.refs_6_), channel_id=1, source_target_pairs={{0,4},{4,0},{8,12},{12,8},{16,20},{20,16},{24,28},{28,24},{1,5},{5... | collective-permute-start | bytes 1290248 | tf_op jit(solution)/shard_map/weights/ppermute | solution.py:20
  162.2 16.3 %collective-permute-start.29 = (bf16[256,1152]{1,0:T(8,128)(2,1)}, bf16[256,1152]{1,0:T(8,128)(2,1)S(1)}, u32[]{:S(2)}, u32[]{:S(2)}) collective-permute-start(bf16[256,1152]{1,0:T(8,128)(2,1)} %bitcast.35), channel_id=1, source_target_pairs={{0,2},{1,3},{2,0},{3,1},{4,6},{5,7},{6,4},{7,5},{8,10},{9,11},{10,... | collective-permute-start | bytes 1769480 | tf_op jit(solution)/shard_map/text_units/ppermute | solution.py:20
  165.1 32.1 %collective-permute-start.21 = (bf16[2,448,1152]{2,1,0:T(8,128)(2,1)}, bf16[2,448,1152]{2,1,0:T(8,128)(2,1)}, u32[]{:S(2)}, u32[]{:S(2)}) collective-permute-start(bf16[2,448,1152]{2,1,0:T(8,128)(2,1)} %pad_maximum_fusion.1), channel_id=1, source_target_pairs={{0,1},{1,0},{2,3},{3,2},{4,5},{5,4},{6,7},{7,6},{8,9},{9,8},{10,11... | collective-permute-start | bytes 6193160 | tf_op jit(solution)/shard_map/head/ppermute | solution.py:20
  165.6 18.2 %collective-permute-start.18 = (bf16[8,2,32,224]{3,2,0,1:T(8,128)(2,1)S(1)}, bf16[8,2,32,224]{3,2,0,1:T(8,128)(2,1)S(1)}, u32[]{:S(2)}, u32[]{:S(2)}) collective-permute-start(bf16[8,2,32,224]{3,2,0,1:T(8,128)(2,1)S(1)} %fusion.41), channel_id=1, source_target_pairs={{0,2},{1,3},{2,0},{3,1},{4,6},{5,7},{6,4},{7,5},{8,10},{9,11},{10,... | collective-permute-start | bytes 688136 | tf_op jit(solution)/shard_map/image_forward/ppermute | solution.py:20
  181.0 13.0 %collective-permute-start.30 = (bf16[2,256,1152]{2,1,0:T(8,128)(2,1)}, bf16[2,256,1152]{2,1,0:T(8,128)(2,1)}, u32[]{:S(2)}, u32[]{:S(2)}) collective-permute-start(bf16[2,256,1152]{2,1,0:T(8,128)(2,1)} %pad_maximum_fusion.2), channel_id=1, source_target_pairs={{0,1},{1,0},{2,3},{3,2},{4,5},{5,4},{6,7},{7,6},{8,9},{9,8},{10,11... | collective-permute-start | bytes 3538952 | tf_op jit(solution)/shard_map/text_units/ppermute | solution.py:20
  183.9 8.9 %collective-permute-start.19 = (bf16[8,32,224]{2,1,0:T(8,128)(2,1)S(1)}, bf16[8,32,224]{2,1,0:T(8,128)(2,1)S(1)}, u32[]{:S(2)}, u32[]{:S(2)}) collective-permute-start(bf16[8,32,224]{2,1,0:T(8,128)(2,1)S(1)} %fusion.70), channel_id=1, source_target_pairs={{0,16},{4,20},{8,24},{12,28},{16,0},{20,4},{24,8},{28,12},{1,17},{... | collective-permute-start | bytes 344072 | tf_op jit(solution)/shard_map/image_forward/ppermute | solution.py:20
  219.6 9.2 %collective-permute-start.31 = (bf16[8,32,224]{2,1,0:T(8,128)(2,1)S(1)}, bf16[8,32,224]{2,1,0:T(8,128)(2,1)S(1)}, u32[]{:S(2)}, u32[]{:S(2)}) collective-permute-start(bf16[8,32,224]{2,1,0:T(8,128)(2,1)S(1)} %bitcast.246), channel_id=1, source_target_pairs={{0,16},{4,20},{8,24},{12,28},{16,0},{20,4},{24,8},{28,12},{1,17},{... | collective-permute-start | bytes 344072 | tf_op jit(solution)/shard_map/image_backward/ppermute | solution.py:20
  225.0 31.1 %collective-permute-start.36 = (bf16[2,32,1152]{2,1,0:T(8,128)(2,1)}, bf16[2,32,1152]{2,1,0:T(8,128)(2,1)}, u32[]{:S(2)}, u32[]{:S(2)}) collective-permute-start(bf16[2,32,1152]{2,1,0:T(8,128)(2,1)} %pad_maximum_fusion.12), channel_id=1, source_target_pairs={{0,1},{1,0},{2,3},{3,2},{4,5},{5,4},{6,7},{7,6},{8,9},{9,8},{10,11... | collective-permute-start | bytes 442376 | tf_op jit(solution)/shard_map/text_loss/ppermute | solution.py:20
  250.8 6.3 %collective-permute-start.32 = (bf16[2,2,256,228]{3,2,1,0:T(8,128)(2,1)}, bf16[2,2,256,228]{3,2,1,0:T(8,128)(2,1)}, u32[]{:S(2)}, u32[]{:S(2)}) collective-permute-start(bf16[2,2,256,228]{3,2,1,0:T(8,128)(2,1)} %pad_maximum_fusion.3), channel_id=1, source_target_pairs={{0,1},{1,0},{2,3},{3,2},{4,5},{5,4},{6,7},{7,6},{8,9},{9,8},{10,11... | collective-permute-start | bytes 1400840 | tf_op jit(solution)/shard_map/image_backward/ppermute | solution.py:20
  263.1 8.1 %collective-permute-start.33 = (bf16[2,256,228]{1,2,0:T(8,128)(2,1)}, bf16[2,256,228]{1,2,0:T(8,128)(2,1)S(1)}, u32[]{:S(2)}, u32[]{:S(2)}) collective-permute-start(bf16[2,256,228]{1,2,0:T(8,128)(2,1)} %pad_maximum_fusion.7), channel_id=1, source_target_pairs={{0,2},{1,3},{2,0},{3,1},{4,6},{5,7},{6,4},{7,5},{8,10},{9,11},{10,... | collective-permute-start | bytes 700424 | tf_op jit(solution)/shard_map/image_backward/ppermute | solution.py:20
  266.8 26.6 %all-to-all-start = ((bf16[8,32,1152]{2,1,0:T(8,128)(2,1)}), bf16[8,32,1152]{2,1,0:T(8,128)(2,1)S(1)}, u32[]{:S(2)}, u32[]{:S(2)}) async-start(bf16[8,32,1152]{2,1,0:T(8,128)(2,1)} %bitcast.244), calls=%async_computation | async-start | bytes 1179648 | tf_op jit(solution)/shard_map/text_loss/all_to_all | solution.py:381
  272.4 19.3 %collective-permute-start.34 = (bf16[2,128,228]{1,2,0:T(8,128)(2,1)S(1)}, bf16[2,128,228]{1,2,0:T(8,128)(2,1)}, u32[]{:S(2)}, u32[]{:S(2)}) collective-permute-start(bf16[2,128,228]{1,2,0:T(8,128)(2,1)S(1)} %pad_maximum_fusion.14), channel_id=1, source_target_pairs={{0,16},{4,20},{8,24},{12,28},{16,0},{20,4},{24,8},{28,12},{1,17},{... | collective-permute-start | bytes 350216 | tf_op jit(solution)/shard_map/image_backward/ppermute | solution.py:20
  (74 other events, 719.0 us)

commit v3 on v2

v3 whole, which is shorter than its diff:
```python
import functools

import jax
import jax.numpy as jnp
from jax import lax
from jax.experimental import pallas as pl
from jax.experimental.pallas import tpu as pltpu
from jax.sharding import PartitionSpec as P

EPS = 1e-06
BF16 = jnp.bfloat16
F32 = jnp.float32
FLIPS = (0, 2, 1, 3)
GELU_C = 0.7978845608028654
GELU_A = 0.044715
VMEM = pl.BlockSpec(memory_space=pltpu.VMEM)
SMEM = pl.BlockSpec(memory_space=pltpu.SMEM)
ANY = pl.BlockSpec(memory_space=pl.ANY)
TAIL = 32
PARAMS = pltpu.CompilerParams(vmem_limit_bytes=60 * 1024 * 1024)


def swap(value, axis, flip):
    return lax.ppermute(value, axis, [(i, i ^ flip) for i in range(lax.axis_size(axis))])


def place(parts, index, flips):
    whole = jnp.zeros((len(flips),) + parts[0].shape, parts[0].dtype)
    for part, flip in zip(parts, flips):
        whole = lax.dynamic_update_index_in_dim(whole, part, index ^ flip, 0)
    return whole


def tie(value, *events):
    return lax.optimization_barrier((value,) + events)[0]


def dot(left, right, left_dim, right_dim):
    dims = (((left_dim,), (right_dim,)), ((), ()))
    return lax.dot_general(left, right, dims, preferred_element_type=F32)


def take(array, index, axis=0):
    return lax.dynamic_index_in_dim(array, index, axis, False)


def halves(shard, img):
    half = shard.shape[-1] // 2
    low, high = shard[..., :half], shard[..., half:]
    upper = img >= lax.axis_size("img") // 2
    return jnp.where(upper, high, low), jnp.where(upper, low, high)


def widen(block, img):
    members = lax.axis_size("img")
    held, flips, bit = block[None], [0], 4
    while bit < members // 2:
        held = jnp.concatenate([held, swap(held, "img", bit)])
        flips = flips + [flip ^ (bit // 4) for flip in flips]
        bit *= 2
    if len(flips) == 1:
        return block
    middle = img // 4 % (members // 8)
    held = place([held[at] for at in range(len(flips))], middle, flips)
    return held.transpose(1, 0, 2, 3).reshape(2, -1, block.shape[2])


def blocked(natural):
    members, rows, width = natural.shape
    if members == 8:
        return natural
    split = natural.reshape(2, members // 8, 4, rows, width)
    return split.transpose(0, 2, 3, 1, 4).reshape(8, rows, members // 8 * width)


def in_order(blocks, members):
    if members == 8:
        return blocks
    rows, width = blocks.shape[1], blocks.shape[2] * 8 // members
    split = blocks.reshape(2, 4, rows, members // 8, width)
    return split.transpose(0, 3, 1, 2, 4).reshape(members, rows, width)


def norm_kernel(ids, parts, gain, scaled, own, mean, inverse):
    _, share_count, rows, _ = parts.shape
    quarter = own.shape[1]
    features = float(4 * share_count * parts.shape[3])
    picks = [(at, sub) for at in range(4) for sub in range(share_count)]

    def sum_rows(term):
        return sum(jnp.sum(term(parts[pick].astype(F32)), axis=1, keepdims=True) for pick in picks)

    center = sum_rows(lambda value: value) / features
    variance = sum_rows(lambda value: (value - center) * (value - center)) / features
    factor = lax.rsqrt(variance + EPS)
    mean[...] = center
    inverse[...] = factor
    start = pl.multiple_of(ids[2] * quarter, quarter)
    for at, sub in picks:
        block = (ids[2] ^ FLIPS[at]) * share_count + sub
        value = parts[at, sub].astype(F32)
        scaled[block, :rows] = ((value - center) * factor * gain[block]).astype(BF16)
        own[block] = parts[at, sub, pl.ds(start, quarter)]
        rest = jnp.broadcast_to(gain[block], (16, gain.shape[2]))
        line = lax.broadcasted_iota(jnp.int32, rest.shape, 0)
        split = jnp.zeros_like(rest)
        for index in range(3):
            part = rest.astype(BF16).astype(F32)
            split = jnp.where(line == index, part, split)
            rest = rest - part
        scaled[block, rows:] = split.astype(BF16)


def fetch(which, blocks, buffer, sems):
    copies = []
    for at, block in enumerate(blocks):
        source, slot = block.at[which] if at < 7 else block, which * 8 + at
        copies.append(pltpu.make_async_copy(source, buffer.at[slot], sems.at[slot]))
    for copy in copies:
        copy.start()
    return copies


def forward_kernel(ids, scaled, *refs):
    before, gains, keep, send, buffer, sems = refs[9:]
    ups = fetch(0, refs[:8], buffer, sems)
    downs = fetch(1, refs[:7] + refs[8:9], buffer, sems)
    rows = before.shape[0]
    total = jnp.zeros((scaled.shape[1], before.shape[1]), F32)
    for at in range(8):
        ups[at].wait()
        total = total + dot(scaled[ids[0] ^ at], buffer[at], 1, 0)
    value = total[:rows]
    before[...] = value
    bend = jnp.tanh(GELU_C * (value + GELU_A * value * value * value))
    hidden = (0.5 * value * (1.0 + bend)).astype(BF16)
    gains[...] = jnp.sum(total[rows:], axis=0, keepdims=True)
    _, pairs, quarter, width = keep.shape
    for at in range(8):
        downs[at].wait()
        block = ids[0] ^ at
        value = dot(hidden, buffer[8 + at], 1, 1).reshape(pairs, 2, quarter, width)
        odd = ids[1] == 1
        keep[block] = jnp.where(odd, value[:, 1], value[:, 0])
        send[block] = jnp.where(odd, value[:, 0], value[:, 1]).astype(BF16)


def back_kernel(split, ids, near, far, before, gains, *refs):
    outs, others, buffer, sems = refs[9:]
    downs = fetch(1, refs[:7] + refs[8:9], buffer, sems)
    ups = fetch(0, refs[:8], buffer, sems)
    rows, hidden = before.shape
    half, width = rows // 2, buffer.shape[1]
    total = jnp.zeros((rows, hidden), F32)
    for at in range(8):
        downs[at].wait()
        block = ids[0] ^ at
        upstream = jnp.concatenate(
            [near[:, block].reshape(half, width), far[:, block].reshape(half, width)]
        )
        total = total + dot(upstream, buffer[8 + at], 1, 0)
    value = before[...]
    square = value * value
    bend = jnp.tanh(GELU_C * value * (1.0 + GELU_A * square))
    slope = 0.5 * (1.0 + bend) + 0.5 * GELU_C * value * (1.0 - bend * bend) * (
        1.0 + 3.0 * GELU_A * square
    )
    grad16 = (total * slope).astype(BF16)
    grad = grad16.astype(F32)
    first = jnp.sum(grad * gains[...], axis=1, keepdims=True)
    second = jnp.sum(grad * value, axis=1, keepdims=True)
    lane = lax.broadcasted_iota(jnp.int32, (rows, TAIL), 1)
    tail = jnp.where(lane == 0, first, jnp.where(lane == 1, second, 0.0))
    for copy in ups:
        copy.wait()
    if not split:
        others[...] = tail
        for at in range(8):
            outs[ids[0] ^ at] = dot(grad16, buffer[at], 1, 1)
        return
    for ref, core in ((others, 1 - ids[1]), (outs, ids[1])):
        for at in range(4):
            block = at // 2 * 4 + core * 2 + at % 2
            value = dot(grad16, buffer[ids[0] ^ block], 1, 1)
            ref[at // 2, at % 2, :, :width] = value.astype(ref.dtype)
            ref[at // 2, at % 2, :, width:] = tail.astype(ref.dtype)


def call(kernel, name, shapes, operands, weights=()):
    scratch = []
    if weights:
        scratch.append(pltpu.VMEM((16,) + weights[0].shape[1:], BF16))
        scratch.append(pltpu.SemaphoreType.DMA((16,)))
    flops = 2 * 256 * 224 * 960 * 16 if weights else 0
    return pl.pallas_call(
        kernel,
        out_shape=shapes,
        in_specs=[SMEM] + [VMEM] * (len(operands) - 1) + [ANY] * len(weights),
        out_specs=tuple(VMEM for _ in shapes),
        scratch_shapes=scratch,
        compiler_params=PARAMS,
        cost_estimate=pl.CostEstimate(flops=flops, bytes_accessed=6 << 20, transcendentals=0),
        name=name,
    )(*operands, *weights)


def norm_stats(rows, axes):
    mean = jnp.mean(rows, axis=axes, keepdims=True)
    centered = rows - mean
    return mean, lax.rsqrt(jnp.mean(centered * centered, axis=axes, keepdims=True) + EPS)


def packed(data, sums):
    high = lax.reduce_precision(sums, 8, 7)
    tail = jnp.concatenate([high, sums - high], -1).astype(BF16)
    return jnp.concatenate([data.astype(BF16), jnp.broadcast_to(tail, data.shape[:-1] + (4,))], -1)


def unpacked(payload, cols):
    payload = payload.astype(F32)
    sums = payload[0, :, cols : cols + 2] + payload[0, :, cols + 2 : cols + 4]
    return payload[..., :cols], sums


def norm_back(grad, sums, rows, mean, inverse, gain, features):
    normed = (rows - mean) * inverse
    first, second = sums[:, 0:1] / features, sums[:, 1:2] / features
    return inverse * (grad * gain - first - normed * second)


def unit_rows(embed):
    inv = lax.rsqrt(jnp.sum(embed * embed, axis=1, keepdims=True) + EPS)
    return inv, (embed * inv).astype(BF16)


def unit_back(embed, inv, grad):
    along = jnp.sum(embed * grad, axis=1, keepdims=True)
    return inv * (grad - embed * (inv * inv) * along)


def gelu16(before):
    return jax.nn.gelu(before, approximate=True).astype(BF16)


def gelu_back16(before, grad):
    _, back = jax.vjp(lambda value: jax.nn.gelu(value, approximate=True), before)
    return back(grad)[0].astype(BF16)


def shards(
    image_in,
    text_in,
    image_gain,
    text_gain,
    image_up,
    image_down,
    text_up,
    text_down,
    image_head,
    log_scale,
    bias,
):
    img, grp = lax.axis_index("img"), lax.axis_index("grp")
    x, core = grp // 2, grp % 2
    members = lax.axis_size("img")
    top = members // 2
    rows, image_cols = image_in.shape
    quarter = rows // 4
    text_cols = text_in.shape[1]
    image_features, text_features = image_cols * 4, text_cols * 4
    width = image_features // members
    share_count = members // 4
    hidden_half = image_up.shape[1] // 2
    embed_width = image_head.shape[1]
    scale = jnp.exp(log_scale[0])
    shift = bias[0]
    ids = jnp.stack([img // top * 4 + img % 4, core, grp]).astype(jnp.int32)

    gate = lax.optimization_barrier

    with jax.named_scope("first"):
        near, send = halves(jnp.stack([image_up, image_down.T]), img)
        near, far = widen(near, img), widen(swap(send, "img", top), img)
        near_y, near_z = swap(near, "img", 1), swap(near, "img", 2)
        near_zy = swap(near_z, "img", 1)
        text_x = swap(text_in, "grp", 2)
        text_parts = [text_in, text_x, swap(text_in, "grp", 1), swap(text_x, "grp", 1)]
        text_parts = place(text_parts, grp, FLIPS)
        text_whole = text_parts.transpose(1, 0, 2).reshape(rows, text_features).astype(F32)
        text_mean, text_inverse = norm_stats(text_whole, 1)
        text_normed = (text_whole - text_mean) * text_inverse
        text_before = dot((text_normed * text_gain).astype(BF16), text_up, 1, 0)
        text_branch = dot(gelu16(text_before), text_down, 1, 0)
        text_branch = text_branch.reshape(2, 2, quarter, text_features)
        send = take(text_branch, 1 - core, 1).astype(BF16)
        total = take(text_branch, core, 1) + swap(send, "grp", 1).astype(F32)
        send = take(total, 1 - x).astype(BF16)
        total = take(total, x) + swap(send, "grp", 2).astype(F32)
        own_in = image_in.reshape(rows, share_count, width).transpose(1, 0, 2)
        far_in = swap(own_in, "img", top)
        head_x = swap(tie(image_head, text_parts), "grp", 2)
        far, near_y, near_zy, total, far_in, head_x = gate(
            (far, near_y, near_zy, total, far_in, head_x)
        )

    with jax.named_scope("second"):
        far_y, far_z = swap(far, "img", 1), swap(far, "img", 2)
        both = jnp.concatenate([own_in, far_in], 1)
        both = jnp.stack([both, swap(both, "grp", 2)])
        text_embed = lax.dynamic_slice_in_dim(text_whole, grp * quarter, quarter, 0) + total
        text_inv, text_unit = unit_rows(text_embed)
        copies = jnp.broadcast_to(text_unit, (members,) + text_unit.shape)
        share = lax.all_to_all(copies, "img", split_axis=0, concat_axis=0, tiled=True)
        far_y, far_z, both, share = gate((far_y, far_z, both, share))

    with jax.named_scope("third"):
        up_last, down_last = swap(far_z[0], "img", 1), swap(far_y[1], "img", 2)
        weights = [near, near_y, near_z, near_zy, far, far_y, far_z, up_last, down_last]
        both = jnp.concatenate([both, swap(both, "grp", 1)])
        text_gains = jnp.sum(text_up.astype(F32) * text_gain[:, None], axis=0)
        share = share.reshape(members * quarter, embed_width)
        at = jnp.arange(members * quarter, dtype=jnp.int32)
        share_ids = at // quarter * rows + at % quarter
        text_ids = jnp.concatenate([share_ids + (grp ^ flip) * quarter for flip in FLIPS])

    with jax.named_scope("norm"):
        share_x = swap(share, "grp", 2)
        every = [share, share_x, swap(share, "grp", 1), swap(share_x, "grp", 1)]
        every_text = jnp.concatenate(every)
        heads = [image_head, head_x, swap(image_head, "grp", 1), swap(head_x, "grp", 1)]
        head = place(heads, grp, FLIPS).reshape(members, width, embed_width)
        gain = image_gain.reshape(members, 1, width)
        scaled, own_rows, mean, inverse = call(
            norm_kernel,
            "norm",
            (
                jax.ShapeDtypeStruct((members, 2 * rows + 16, width), BF16),
                jax.ShapeDtypeStruct((members, quarter, width), BF16),
                jax.ShapeDtypeStruct((2 * rows, 1), F32),
                jax.ShapeDtypeStruct((2 * rows, 1), F32),
            ),
            (ids, both, gain),
        )
        scaled = blocked(tie(scaled, share_x, head))

    with jax.named_scope("image_forward"):
        shape = (8, 4, quarter, image_features // 8)
        before, gains, keep, send = call(
            forward_kernel,
            "forward",
            (
                jax.ShapeDtypeStruct((2 * rows, hidden_half), F32),
                jax.ShapeDtypeStruct((1, hidden_half), F32),
                jax.ShapeDtypeStruct(shape, F32),
                jax.ShapeDtypeStruct(shape, BF16),
            ),
            (ids, scaled),
            weights,
        )
        total = (keep + swap(send, "grp", 1).astype(F32)).reshape(8, 2, 2, quarter, -1)
        send = take(total, 1 - x, 2).astype(BF16)
        got = swap(send, "grp", 2)
        total = take(total, x, 2) + got.astype(F32)
        branch = total[:, 0] + swap(total[:, 1].astype(BF16), "img", top).astype(F32)
        image_mid16 = (own_rows.astype(F32) + in_order(branch, members)).astype(BF16)
        image_mid16 = image_mid16.transpose(1, 0, 2).reshape(quarter, image_features)
        image_embed = dot(image_mid16, head.reshape(image_features, embed_width), 1, 0)
        image_inv, image_unit = unit_rows(image_embed)

    with jax.named_scope("text_loss"):
        pair = jnp.stack([image_unit, swap(image_unit, "grp", 2)])
        image_units = jnp.concatenate([pair, swap(pair, "grp", 1)]).reshape(rows, embed_width)
        logits = scale * dot(image_units, share, 1, 1) + shift
        at = jnp.arange(quarter, dtype=jnp.int32)
        group_ids = jnp.concatenate([img * rows + (grp ^ flip) * quarter + at for flip in FLIPS])
        same = (group_ids[:, None] == (share_ids + grp * quarter)[None, :]).astype(F32)
        pull = (jax.nn.sigmoid(logits) - same).astype(BF16)
        text_partial = (scale * dot(pull, image_units, 0, 0)).astype(BF16)
        text_partial = text_partial.reshape(members, quarter, embed_width)
        text_parts = lax.all_to_all(
            text_partial, "img", split_axis=0, concat_axis=0, tiled=True
        )

    with jax.named_scope("image_loss"):
        image_ids = img * rows + grp * quarter + jnp.arange(quarter, dtype=jnp.int32)
        logits = scale * dot(image_unit, every_text, 1, 1) + shift
        same = (image_ids[:, None] == text_ids[None, :]).astype(F32)
        pull = (jax.nn.sigmoid(logits) - same).astype(BF16)
        grad_image_unit = scale * dot(pull, every_text, 1, 0)
        grad_embed16 = unit_back(image_embed, image_inv, grad_image_unit).astype(BF16)
        grad_mid16 = dot(grad_embed16, head.reshape(image_features, embed_width), 1, 1)
        grad_mid16 = grad_mid16.astype(BF16).reshape(quarter, members, width)
        grad_mid16 = blocked(grad_mid16.transpose(1, 0, 2))

    with jax.named_scope("image_backward"):
        far_grad = swap(grad_mid16, "img", top)
        near_whole = lax.all_gather(grad_mid16, "grp")
        far_whole = lax.all_gather(tie(far_grad, text_partial), "grp")
        split = members == 8
        if split:
            shape = (2, share_count, 2 * rows, width + TAIL)
            shapes = (jax.ShapeDtypeStruct(shape, F32), jax.ShapeDtypeStruct(shape, BF16))
        else:
            shapes = (
                jax.ShapeDtypeStruct((8, 2 * rows, image_features // 8), F32),
                jax.ShapeDtypeStruct((2 * rows, TAIL), F32),
            )
        keep, send = call(
            functools.partial(back_kernel, split),
            "back",
            shapes,
            (ids, near_whole, far_whole, before, gains),
            weights,
        )
        if not split:
            tail = jnp.broadcast_to(send, (members,) + send.shape)
            total = jnp.concatenate([in_order(keep, members), tail], -1)
            total = total.reshape(2, 2, share_count, 2 * rows, width + TAIL)
            keep, send = take(total, core, 1), take(total, 1 - core, 1).astype(BF16)
        total = keep + tie(swap(send, "grp", 1), text_parts).astype(F32)
        send = take(total, 1 - x).astype(BF16)
        total = take(total, x) + swap(send, "grp", 2).astype(F32)
        got = swap(total[:, rows:].astype(BF16), "img", top).astype(F32)
        total = total[:, :rows] + got
        total, sums = total[..., :width], total[0, :, width : width + 2]
        back = norm_back(
            total,
            sums,
            own_in.astype(F32),
            mean[:rows],
            inverse[:rows],
            take(gain.reshape(4, share_count, 1, width), grp),
            image_features,
        )
        own_grad = in_order(near_whole.transpose(1, 0, 2, 3).reshape(8, rows, -1), members)
        own_grad = take(own_grad.reshape(4, share_count, rows, width), grp)
        image_grad = (own_grad.astype(F32) + back).astype(BF16)
        image_grad = image_grad.transpose(1, 0, 2).reshape(rows, image_cols)

    with jax.named_scope("text_sum"):
        grad_text_unit = jnp.sum(text_parts.astype(F32), axis=0)
        grad_text16 = unit_back(text_embed, text_inv, grad_text_unit).astype(BF16)

    with jax.named_scope("text_backward"):
        pair = jnp.stack([grad_text16, swap(grad_text16, "grp", 2)])
        parts = jnp.concatenate([pair, swap(pair, "grp", 1)])
        upstream = place([parts[at] for at in range(4)], grp, FLIPS).reshape(rows, text_features)
        grad_before = gelu_back16(text_before, dot(upstream, text_down, 1, 1))
        grad32 = grad_before.astype(F32)
        sums = jnp.stack([jnp.sum(grad32 * text_gains, 1), jnp.sum(grad32 * text_before, 1)], 1)
        blocks = text_up.reshape(4, text_cols, -1)
        partial = {flip: dot(grad_before, take(blocks, grp ^ flip), 1, 1) for flip in FLIPS}
        send = jnp.stack([packed(partial[flip], sums) for flip in (1, 3)])
        data, more = unpacked(swap(send, "grp", 1), text_cols)
        sums = sums + more
        send = packed(partial[2] + data[1], sums)[None]
        more_data, more = unpacked(swap(send, "grp", 2), text_cols)
        total, sums = partial[0] + data[0] + more_data[0], sums + more
        own_gain = lax.dynamic_slice_in_dim(text_gain, grp * text_cols, text_cols, 0)
        back = norm_back(
            total, sums, text_in.astype(F32), text_mean, text_inverse, own_gain, text_features
        )
        own_grad = lax.dynamic_slice_in_dim(upstream, grp * text_cols, text_cols, 1)
        text_grad = (own_grad.astype(F32) + back).astype(BF16)
    return (image_grad, text_grad)


def solution(mesh):
    in_specs = (
        P("img", "grp"),
        P("img", "grp"),
        P(),
        P(),
        P("img", "grp"),
        P("grp", "img"),
        P(None, "grp"),
        P("grp", None),
        P("grp", None),
        P(),
        P(),
    )
    out_specs = (P("img", "grp"), P("img", "grp"))
    return jax.shard_map(shards, mesh=mesh, in_specs=in_specs, out_specs=out_specs, check_vma=False)
```

time: 310 us -> 235 us (0.76)
  waiting for transfers between devices: 118 us -> 79.4 us
  local copies, waits for them, and re-layouts: 66.1 us -> 31.3 us
  other arithmetic: 40.1 us -> 26.9 us
  Pallas kernels: 9.76 us -> 20 us
    ppermute x41 -> x35, waiting for transfers between devices: 118 us -> 79.4 us  [swap(): lax.ppermute(value, axis, [(i, i ^ flip) for i in range(lax.axis_size(axi...]
    dynamic_update_slice x22 -> x11, local copies, waits for them, and re-layouts: 21.6 us -> 10.6 us  [place(): whole = lax.dynamic_update_index_in_dim(whole, part, index ^ flip, 0)]
    unnamed x131 -> x54, local copies, waits for them, and re-layouts: 14 us -> 3.61 us
    pallas_call x3, Pallas kernels: 9.76 us -> 20 us  [call(): pl.pallas_call(kernel, out_shape=shapes, in_specs=[SMEM] + [VMEM] * (len(...]
    another operation x12 -> x4, other arithmetic: 8.16 us -> 0.7 us  [the longest x1 0.67 us: shards(): ids = jnp.stack([img // top * 4 + img % 4, core, grp]).astype(jnp.int32)]
    ppermute x41 -> x35, starting transfers between devices: 37.3 us -> 31.7 us  [swap(): lax.ppermute(value, axis, [(i, i ^ flip) for i in range(lax.axis_size(axi...]
    all_to_all x1 -> x2, starting transfers between devices: 3.67 us -> 8.92 us  [the longest x1 4.54 us: shards(): lax.all_to_all(text_partial, 'img', split_axis=0, concat_axis=0, tiled=True)]
    concatenate x2 -> x0, local copies, waits for them, and re-layouts: 4.95 us -> none  [the longest x1 4.8 us: shards(): scaled = blocked(jnp.concatenate([scaled] + parts, 1))]
  transfers between devices with their start and end apart: 42 -> 37, of which waited for: 20 -> 14; matrix products, arithmetic and copies ran while one was open for 28% -> 29% of each run, Pallas kernels for 3% -> 9%
where the time goes in v3:
time: 235 us; the launch traced here: 234 us
  waiting for transfers between devices  79.4 us (34%)
  starting transfers between devices  40.6 us (17%)
  local copies, waits for them, and re-layouts  31.3 us (13%)
  other arithmetic  26.9 us (11%)
  Pallas kernels  20 us (9%)
  matrix products  17.5 us (7%)
  blocking collectives  15.5 us (7%)
  between operations  2.65 us (1%)
    ppermute x35, waiting for transfers between devices, swap(): lax.ppermute(value, axis, [(i, i ^ flip) for i in range(lax.axis_size(axi...  79.4 us
    ppermute x35, starting transfers between devices, swap(): lax.ppermute(value, axis, [(i, i ^ flip) for i in range(lax.axis_size(axi...  31.7 us
    pallas_call x3, Pallas kernels, call(): pl.pallas_call(kernel, out_shape=shapes, in_specs=[SMEM] + [VMEM] * (len(...  20 us
    dot_general x11, matrix products, dot(): return lax.dot_general(left, right, dims, preferred_element_type=F32)  17.5 us
    dynamic_update_slice x11, local copies, waits for them, and re-layouts, place(): whole = lax.dynamic_update_index_in_dim(whole, part, index ^ flip, 0)  10.6 us
    all_gather x1, blocking collectives, shards(): far_whole = lax.all_gather(tie(far_grad, text_partial), 'grp')  7.95 us
    all_gather x1, blocking collectives, shards(): near_whole = lax.all_gather(grad_mid16, 'grp')  7.56 us
  transfers between devices with their start and end apart: 37, of which 14 were waited for; matrix products, arithmetic and copies ran while one was open for 29% of the time, Pallas kernels for 9%

profile of v3, /device:TPU:0, one launch (start us, length us, event | category | flops | bytes accessed | tf_op | source)
XLA Modules:
  0.0 234.0 jit_solution(12814546756316990587)
XLA Ops:
  0.7 3.0 %collective-permute-start.4 = (bf16[128,288]{0,1:T(8,128)(2,1)}, bf16[128,288]{0,1:T(8,128)(2,1)S(1)}, u32[]{:S(2)}, u32[]{:S(2)}) collective-permute-start(bf16[128,288]{0,1:T(8,128)(2,1)} %param.12), channel_id=1, source_target_pairs={{0,2},{1,3},{2,0},{3,1},{4,6},{5,7},{6,4},{7,5},{8,10},{9,11},{10,... | collective-permute-start | bytes 221192 | tf_op jit(solution)/shard_map/first/ppermute | solution.py:24
  3.7 3.9 %broadcast_select_fusion = (bf16[2,224,960]{2,1,0:T(8,128)(2,1)}, bf16[2,224,960]{2,1,0:T(8,128)(2,1)}) fusion(pred[]{:T(512)S(6)} %ge.3, bf16[1,224,1920]{2,1,0:T(8,128)(2,1)} %bitcast.202, bf16[1,224,1920]{2,1,0:T(8,128)(2,1)} %bitcast.203), kind=kLoop, calls=%fused_computation.36 | loop fusion | flops 6021120 | bytes 3440641 | tf_op jit(solution)/shard_map/first/jit(_where)/select_n | solution.py:51
  20.5 2.6 %collective-permute-start = (bf16[2,224,960]{2,1,0:T(8,128)(2,1)}, bf16[2,224,960]{2,1,0:T(8,128)(2,1)}, u32[]{:S(2)}, u32[]{:S(2)}) collective-permute-start(bf16[2,224,960]{2,1,0:T(8,128)(2,1)} %get-tuple-element.62), channel_id=1, source_target_pairs={{0,16},{4,20},{8,24},{12,28},{16,0},{20,4},{24,8},{28,12},{1,17},{... | collective-permute-start | bytes 2580488 | tf_op jit(solution)/shard_map/first/ppermute | solution.py:24
  26.4 12.8 %collective-permute-done.2.refs_2_ = bf16[2,224,960]{2,1,0:T(8,128)(2,1)} collective-permute-done((bf16[2,224,960]{2,1,0:T(8,128)(2,1)}, bf16[2,224,960]{2,1,0:T(8,128)(2,1)}, u32[]{:S(2)}, u32[]{:S(2)}) %collective-permute-start.2) | collective-permute-done | bytes 860192 | tf_op jit(solution)/shard_map/first/ppermute | solution.py:24
  39.1 2.5 %collective-permute-start.3 = (bf16[2,224,960]{2,1,0:T(8,128)(2,1)}, bf16[2,224,960]{2,1,0:T(8,128)(2,1)}, u32[]{:S(2)}, u32[]{:S(2)}) collective-permute-start(bf16[2,224,960]{2,1,0:T(8,128)(2,1)} %collective-permute-done.2.refs_2_), channel_id=1, source_target_pairs={{0,4},{4,0},{8,12},{12,8},{16,20},{20,16},{24,28},{28,24},{1,5},{5... | collective-permute-start | bytes 2580488 | tf_op jit(solution)/shard_map/first/ppermute | solution.py:24
  45.2 5.8 %collective-permute-done.8 = bf16[32,1152]{1,0:T(8,128)(2,1)} collective-permute-done((bf16[32,1152]{1,0:T(8,128)(2,1)}, bf16[32,1152]{1,0:T(8,128)(2,1)}, u32[]{:S(2)}, u32[]{:S(2)}) %collective-permute-start.8) | collective-permute-done | bytes 73760 | tf_op jit(solution)/shard_map/first/ppermute | solution.py:24
  52.3 16.8 %collective-permute-done.9 = bf16[2,128,224]{2,1,0:T(8,128)(2,1)S(1)} collective-permute-done((bf16[2,128,224]{2,1,0:T(8,128)(2,1)}, bf16[2,128,224]{2,1,0:T(8,128)(2,1)S(1)}, u32[]{:S(2)}, u32[]{:S(2)}) %collective-permute-start.9) | collective-permute-done | bytes 114720 | tf_op jit(solution)/shard_map/first/ppermute | solution.py:24
  70.9 4.4 %all-to-all-start = ((bf16[8,32,1152]{2,1,0:T(8,128)(2,1)}), bf16[8,32,1152]{2,1,0:T(8,128)(2,1)}, u32[]{:S(2)}, u32[]{:S(2)}) async-start(bf16[8,32,1152]{2,1,0:T(8,128)(2,1)} %broadcast_in_dim.74), calls=%async_computation | async-start | bytes 1179648 | tf_op jit(solution)/shard_map/second/all_to_all | solution.py:313
  75.3 2.3 broadcast_in_dim.75
  85.9 4.7 %collective-permute-done.13 = bf16[2,256,224]{2,1,0:T(8,128)(2,1)} collective-permute-done((bf16[2,256,224]{2,1,0:T(8,128)(2,1)S(1)}, bf16[2,256,224]{2,1,0:T(8,128)(2,1)}, u32[]{:S(2)}, u32[]{:S(2)}) %collective-permute-start.13) | collective-permute-done | bytes 229408 | tf_op jit(solution)/shard_map/second/ppermute | solution.py:24
  91.7 13.5 %collective-permute-done.11.refs_5_ = bf16[2,224,960]{2,1,0:T(8,128)(2,1)} collective-permute-done((bf16[2,224,960]{2,1,0:T(8,128)(2,1)}, bf16[2,224,960]{2,1,0:T(8,128)(2,1)}, u32[]{:S(2)}, u32[]{:S(2)}) %collective-permute-start.11) | collective-permute-done | bytes 860192 | tf_op jit(solution)/shard_map/second/ppermute | solution.py:24
  105.2 2.8 %collective-permute-done.12.refs_6_ = bf16[2,224,960]{2,1,0:T(8,128)(2,1)} collective-permute-done((bf16[2,224,960]{2,1,0:T(8,128)(2,1)}, bf16[2,224,960]{2,1,0:T(8,128)(2,1)}, u32[]{:S(2)}, u32[]{:S(2)}) %collective-permute-start.12) | collective-permute-done | bytes 860192 | tf_op jit(solution)/shard_map/second/ppermute | solution.py:24
  115.2 3.5 %norm.1 = (bf16[8,272,224]{2,1,0:T(8,128)(2,1)}, bf16[8,32,224]{2,1,0:T(8,128)(2,1)}, f32[256,1]{1,0:T(8,128)}, f32[256,1]{1,0:T(8,128)}) custom-call(s32[3]{0:T(128)} %pad_add_fusion.1.ids, bf16[4,2,256,224]{3,2,1,0:T(8,128)(2,1)} %pad_maximum_fusion.3.parts, f32[8,1,224]{2,1,0:T(1,128)} %reshape.143.gain), custom_call_target="tpu_custom_call" | custom-call | bytes 6291456 | tf_op jit(solution)/shard_map/norm/norm/pallas_call | solution.py:195
  118.7 5.4 %collective-permute-done.15 = bf16[256,1152]{1,0:T(8,128)(2,1)} collective-permute-done((bf16[256,1152]{1,0:T(8,128)(2,1)}, bf16[256,1152]{1,0:T(8,128)(2,1)}, u32[]{:S(2)}, u32[]{:S(2)}) %collective-permute-start.15) | collective-permute-done | bytes 589856 | tf_op jit(solution)/shard_map/norm/ppermute | solution.py:24
  124.0 1.9 collective-permute-done.17.refs_8_
  126.0 9.0 %forward.1 = (f32[256,960]{1,0:T(8,128)}, f32[1,960]{1,0:T(1,128)}, f32[8,4,32,224]{3,2,1,0:T(8,128)}, bf16[8,4,32,224]{3,2,1,0:T(8,128)(2,1)}) custom-call(s32[3]{0:T(128)} %pad_add_fusion.1.ids, bf16[8,272,224]{2,1,0:T(8,128)(2,1)} %get-tuple-element.34.scaled, bf16[2,224,960]{2,1,0:T(8,128)(2,1)} %get-tuple-element.61.refs_0_, ...), custom_call_target="tpu_custom_call" | custom-call | flops 1761607680 | bytes 6291456 | tf_op jit(solution)/shard_map/image_forward/forward/pallas_call | solution.py:195
  135.1 2.3 %bitcast_dynamic-update-slice_fusion.2 = bf16[4,448,1152]{2,1,0:T(8,128)(2,1)} fusion(bf16[4,448,1152]{2,1,0:T(8,128)(2,1)} %bitcast_dynamic-update-slice_fusion.3, s32[]{:T(128)S(6)} %select_n.127, bf16[448,1152]{1,0:T(8,128)(2,1)} %collective-permute-done.10), kind=kLoop, calls=%fused_computation.32 | loop fusion | bytes 2064388 | tf_op jit(solution)/shard_map/norm/jit(dynamic_update_index_in_dim)/dynamic_update_slice | solution.py:30
  139.3 2.3 bitcast_dynamic-update-slice_fusion.1
  141.7 4.7 %collective-permute-done.19 = bf16[8,2,32,224]{3,2,0,1:T(8,128)(2,1)S(1)} collective-permute-done((bf16[8,2,32,224]{3,2,0,1:T(8,128)(2,1)S(1)}, bf16[8,2,32,224]{3,2,0,1:T(8,128)(2,1)S(1)}, u32[]{:S(2)}, u32[]{:S(2)}) %collective-permute-start.19) | collective-permute-done | bytes 229408 | tf_op jit(solution)/shard_map/image_forward/ppermute | solution.py:24
  146.5 2.5 %collective-permute-start.20 = (bf16[8,32,224]{2,1,0:T(8,128)(2,1)S(1)}, bf16[8,32,224]{2,1,0:T(8,128)(2,1)S(1)}, u32[]{:S(2)}, u32[]{:S(2)}) collective-permute-start(bf16[8,32,224]{2,1,0:T(8,128)(2,1)S(1)} %fusion.66), channel_id=1, source_target_pairs={{0,16},{4,20},{8,24},{12,28},{16,0},{20,4},{24,8},{28,12},{1,17},{... | collective-permute-start | bytes 344072 | tf_op jit(solution)/shard_map/image_forward/ppermute | solution.py:24
  149.0 2.3 bitcast_dynamic-update-slice_fusion
  151.3 4.0 %collective-permute-done.20 = bf16[8,32,224]{2,1,0:T(8,128)(2,1)S(1)} collective-permute-done((bf16[8,32,224]{2,1,0:T(8,128)(2,1)S(1)}, bf16[8,32,224]{2,1,0:T(8,128)(2,1)S(1)}, u32[]{:S(2)}, u32[]{:S(2)}) %collective-permute-start.20) | collective-permute-done | bytes 114720 | tf_op jit(solution)/shard_map/image_forward/ppermute | solution.py:24
  155.7 3.1 %multiply_reduce_fusion.4 = (f32[32]{0:T(128)S(1)}, f32[32,1152]{1,0:T(8,128)S(1)}) fusion(bf16[32,1792]{1,0:T(8,128)(2,1)S(1)} %reshape.146, bf16[1792,1152]{1,0:T(8,128)(2,1)} %bitcast.35), kind=kOutput, calls=%fused_computation.123 | convolution fusion | flops 132194272 | bytes 4391040 | tf_op jit(solution)/shard_map/image_forward/dot_general | solution.py:40
  160.3 4.4 %multiply_reduce_fusion.3 = (f32[32]{0:T(128)S(1)}, f32[32,1152]{1,0:T(8,128)}) fusion(f32[32,1152]{1,0:T(8,128)S(1)} %get-tuple-element.76, bf16[256,1152]{1,0:T(8,128)(2,1)} %collective-permute-done.24, bf16[256,1152]{1,0:T(8,128)(2,1)} %collective-permute-done.23, bf16[256,1152]{1,0:T(8,128)(2,1)} %collective-permute-done.15, ...), kind=kOutput, calls=%fused_computation.121 | convolution fusion | flops 170348512 | bytes 2658696 | tf_op jit(solution)/shard_map/image_loss/dot_general | solution.py:40
  165.5 3.5 %convolution_convert_fusion = bf16[32,1792]{1,0:T(8,128)(2,1)S(1)} fusion(bf16[1792,1152]{1,0:T(8,128)(2,1)} %bitcast.35, f32[32,1152]{1,0:T(8,128)} %get-tuple-element.78, f32[32,1152]{1,0:T(8,128)S(1)} %get-tuple-element.76, f32[32]{0:T(128)S(1)} %get-tuple-element.77, f32[32]{0:T(128)S(1)} %get-tuple-element.73, f32[32]{0:T(128)S(1)} %get-tuple-element.74), kind=kOutput, calls=%fused_computation.5 | convolution fusion | flops 132362240 | bytes 4538752 | tf_op jit(solution)/shard_map/image_loss/dot_general | solution.py:40
  171.0 3.0 %fusion = bf16[256,1152]{1,0:T(8,128)(2,1)} fusion(bf16[128,1152]{1,0:T(8,128)(2,1)} %bitcast.211, bf16[256,1152]{1,0:T(8,128)(2,1)} %bitcast.22, f32[]{:T(128)} %bitcast.36, s32[256]{0:T(256)S(1)} %broadcast_add_fusion.3, f32[]{:T(128)} %bitcast.186, s32[128]{0:T(128)S(1)} %pad_add_fusion.2), kind=kOutput, calls=%fused_computation.2 | convolution fusion | flops 151879680 | bytes 1476104 | tf_op jit(solution)/shard_map/text_loss/dot_general | solution.py:40
  174.0 4.5 %all-to-all-start.1 = ((bf16[8,32,1152]{2,1,0:T(8,128)(2,1)}), bf16[8,32,1152]{2,1,0:T(8,128)(2,1)}, u32[]{:S(2)}, u32[]{:S(2)}) async-start(bf16[8,32,1152]{2,1,0:T(8,128)(2,1)} %bitcast.46), calls=%async_computation.1 | async-start | bytes 1179648 | tf_op jit(solution)/shard_map/text_loss/all_to_all | solution.py:380
  178.6 7.6 %all-gather = bf16[32,32,224]{2,1,0:T(8,128)(2,1)} all-gather(bf16[8,32,224]{2,1,0:T(8,128)(2,1)S(1)} %bitcast.206), channel_id=2, replica_groups=mesh['img'=8,'grp'=4] {'grp'}, dimensions={0}, use_global_device_ids=true | all-gather | bytes 573440 | tf_op jit(solution)/shard_map/image_backward/all_gather | solution.py:397
  186.1 7.9 %all-gather.1 = bf16[32,32,224]{2,1,0:T(8,128)(2,1)} all-gather(bf16[8,32,224]{2,1,0:T(8,128)(2,1)S(1)} %collective-permute-done.25), channel_id=3, replica_groups=mesh['img'=8,'grp'=4] {'grp'}, dimensions={0}, use_global_device_ids=true | all-gather | bytes 573440 | tf_op jit(solution)/shard_map/image_backward/all_gather | solution.py:398
  194.1 7.5 %back.1 = (f32[2,2,256,256]{3,2,1,0:T(8,128)}, bf16[2,2,256,256]{3,2,1,0:T(8,128)(2,1)}) custom-call(s32[3]{0:T(128)} %pad_add_fusion.1.ids, bf16[4,8,32,224]{3,2,1,0:T(8,128)(2,1)} %bitcast.193, bf16[4,8,32,224]{3,2,1,0:T(8,128)(2,1)} %bitcast.197, f32[256,960]{1,0:T(8,128)} %get-tuple-element.44.before, f32[1,960]{1,0:T(1,128)} %get-tuple-element.45.gains, ...), custom_call_target="tpu_custom_call" | custom-call | flops 1761607680 | bytes 6291456 | tf_op jit(solution)/shard_map/image_backward/back/pallas_call | solution.py:195
  220.6 2.9 %collective-permute-start.30 = (bf16[2,128,256]{2,1,0:T(8,128)(2,1)S(1)}, bf16[2,128,256]{2,1,0:T(8,128)(2,1)S(1)}, u32[]{:S(2)}, u32[]{:S(2)}) collective-permute-start(bf16[2,128,256]{2,1,0:T(8,128)(2,1)S(1)} %slice.217), channel_id=1, source_target_pairs={{0,16},{4,20},{8,24},{12,28},{16,0},{20,4},{24,8},{28,12},{1,17},{... | collective-permute-start | bytes 393224 | tf_op jit(solution)/shard_map/image_backward/ppermute | solution.py:24
  225.9 3.4 %collective-permute-done.30 = bf16[2,128,256]{2,1,0:T(8,128)(2,1)S(1)} collective-permute-done((bf16[2,128,256]{2,1,0:T(8,128)(2,1)S(1)}, bf16[2,128,256]{2,1,0:T(8,128)(2,1)S(1)}, u32[]{:S(2)}, u32[]{:S(2)}) %collective-permute-start.30) | collective-permute-done | bytes 131104 | tf_op jit(solution)/shard_map/image_backward/ppermute | solution.py:24
  (202 shorter events, 70.4 us)
Async XLA Ops:
  0.7 9.9 %collective-permute-start.4 = (bf16[128,288]{0,1:T(8,128)(2,1)}, bf16[128,288]{0,1:T(8,128)(2,1)S(1)}, u32[]{:S(2)}, u32[]{:S(2)}) collective-permute-start(bf16[128,288]{0,1:T(8,128)(2,1)} %param.12), channel_id=1, source_target_pairs={{0,2},{1,3},{2,0},{3,1},{4,6},{5,7},{6,4},{7,5},{8,10},{9,11},{10,... | collective-permute-start | bytes 221192 | tf_op jit(solution)/shard_map/first/ppermute | solution.py:24
  3.7 7.8 %collective-permute-start.5 = (bf16[128,288]{0,1:T(8,128)(2,1)}, bf16[128,288]{0,1:T(8,128)(2,1)S(1)}, u32[]{:S(2)}, u32[]{:S(2)}) collective-permute-start(bf16[128,288]{0,1:T(8,128)(2,1)} %param.12), channel_id=1, source_target_pairs={{0,1},{1,0},{2,3},{3,2},{4,5},{5,4},{6,7},{7,6},{8,9},{9,8},{10,11... | collective-permute-start | bytes 221192 | tf_op jit(solution)/shard_map/first/ppermute | solution.py:24
  7.6 31.6 %collective-permute-start.2 = (bf16[2,224,960]{2,1,0:T(8,128)(2,1)}, bf16[2,224,960]{2,1,0:T(8,128)(2,1)}, u32[]{:S(2)}, u32[]{:S(2)}) collective-permute-start(bf16[2,224,960]{2,1,0:T(8,128)(2,1)} %get-tuple-element.61.refs_0_), channel_id=1, source_target_pairs={{0,8},{4,12},{8,0},{12,4},{16,24},{20,28},{24,16},{28,20},{1,9},{5... | collective-permute-start | bytes 2580488 | tf_op jit(solution)/shard_map/first/ppermute | solution.py:24
  18.7 6.6 %collective-permute-start.7 = (bf16[2,32,1152]{2,1,0:T(8,128)(2,1)}, bf16[2,32,1152]{2,1,0:T(8,128)(2,1)}, u32[]{:S(2)}, u32[]{:S(2)}) collective-permute-start(bf16[2,32,1152]{2,1,0:T(8,128)(2,1)} %fusion.54), channel_id=1, source_target_pairs={{0,1},{1,0},{2,3},{3,2},{4,5},{5,4},{6,7},{7,6},{8,9},{9,8},{10,11... | collective-permute-start | bytes 442376 | tf_op jit(solution)/shard_map/first/ppermute | solution.py:24
  19.0 50.2 %collective-permute-start.1 = (bf16[2,224,960]{2,1,0:T(8,128)(2,1)}, bf16[2,224,960]{2,1,0:T(8,128)(2,1)}, u32[]{:S(2)}, u32[]{:S(2)}) collective-permute-start(bf16[2,224,960]{2,1,0:T(8,128)(2,1)} %get-tuple-element.61.refs_0_), channel_id=1, source_target_pairs={{0,4},{4,0},{8,12},{12,8},{16,20},{20,16},{24,28},{28,24},{1,5},{5... | collective-permute-start | bytes 2580488 | tf_op jit(solution)/shard_map/first/ppermute | solution.py:24
  20.5 48.7 %collective-permute-start = (bf16[2,224,960]{2,1,0:T(8,128)(2,1)}, bf16[2,224,960]{2,1,0:T(8,128)(2,1)}, u32[]{:S(2)}, u32[]{:S(2)}) collective-permute-start(bf16[2,224,960]{2,1,0:T(8,128)(2,1)} %get-tuple-element.62), channel_id=1, source_target_pairs={{0,16},{4,20},{8,24},{12,28},{16,0},{20,4},{24,8},{28,12},{1,17},{... | collective-permute-start | bytes 2580488 | tf_op jit(solution)/shard_map/first/ppermute | solution.py:24
  24.7 44.4 %collective-permute-start.10 = (bf16[448,1152]{1,0:T(8,128)(2,1)}, bf16[448,1152]{1,0:T(8,128)(2,1)}, u32[]{:S(2)}, u32[]{:S(2)}) collective-permute-start(bf16[448,1152]{1,0:T(8,128)(2,1)} %param.19), channel_id=1, source_target_pairs={{0,2},{1,3},{2,0},{3,1},{4,6},{5,7},{6,4},{7,5},{8,10},{9,11},{10,... | collective-permute-start | bytes 3096584 | tf_op jit(solution)/shard_map/first/ppermute | solution.py:24
  39.1 30.0 %collective-permute-start.3 = (bf16[2,224,960]{2,1,0:T(8,128)(2,1)}, bf16[2,224,960]{2,1,0:T(8,128)(2,1)}, u32[]{:S(2)}, u32[]{:S(2)}) collective-permute-start(bf16[2,224,960]{2,1,0:T(8,128)(2,1)} %collective-permute-done.2.refs_2_), channel_id=1, source_target_pairs={{0,4},{4,0},{8,12},{12,8},{16,20},{20,16},{24,28},{28,24},{1,5},{5... | collective-permute-start | bytes 2580488 | tf_op jit(solution)/shard_map/first/ppermute | solution.py:24
  42.3 8.7 %collective-permute-start.8 = (bf16[32,1152]{1,0:T(8,128)(2,1)}, bf16[32,1152]{1,0:T(8,128)(2,1)}, u32[]{:S(2)}, u32[]{:S(2)}) collective-permute-start(bf16[32,1152]{1,0:T(8,128)(2,1)} %fusion.74), channel_id=1, source_target_pairs={{0,2},{1,3},{2,0},{3,1},{4,6},{5,7},{6,4},{7,5},{8,10},{9,11},{10,... | collective-permute-start | bytes 221192 | tf_op jit(solution)/shard_map/first/ppermute | solution.py:24
  51.0 18.1 %collective-permute-start.9 = (bf16[2,128,224]{2,1,0:T(8,128)(2,1)}, bf16[2,128,224]{2,1,0:T(8,128)(2,1)S(1)}, u32[]{:S(2)}, u32[]{:S(2)}) collective-permute-start(bf16[2,128,224]{2,1,0:T(8,128)(2,1)} %bitcast.200), channel_id=1, source_target_pairs={{0,16},{4,20},{8,24},{12,28},{16,0},{20,4},{24,8},{28,12},{1,17},{... | collective-permute-start | bytes 344072 | tf_op jit(solution)/shard_map/first/ppermute | solution.py:24
  69.2 70.2 %collective-permute-start.21 = (bf16[448,1152]{1,0:T(8,128)(2,1)}, bf16[448,1152]{1,0:T(8,128)(2,1)}, u32[]{:S(2)}, u32[]{:S(2)}) collective-permute-start(bf16[448,1152]{1,0:T(8,128)(2,1)} %param.19), channel_id=1, source_target_pairs={{0,1},{1,0},{2,3},{3,2},{4,5},{5,4},{6,7},{7,6},{8,9},{9,8},{10,11... | collective-permute-start | bytes 3096584 | tf_op jit(solution)/shard_map/norm/ppermute | solution.py:24
  70.9 37.0 %all-to-all-start = ((bf16[8,32,1152]{2,1,0:T(8,128)(2,1)}), bf16[8,32,1152]{2,1,0:T(8,128)(2,1)}, u32[]{:S(2)}, u32[]{:S(2)}) async-start(bf16[8,32,1152]{2,1,0:T(8,128)(2,1)} %broadcast_in_dim.74), calls=%async_computation | async-start | bytes 1179648 | tf_op jit(solution)/shard_map/second/all_to_all | solution.py:313
  78.7 26.5 %collective-permute-start.11 = (bf16[2,224,960]{2,1,0:T(8,128)(2,1)}, bf16[2,224,960]{2,1,0:T(8,128)(2,1)}, u32[]{:S(2)}, u32[]{:S(2)}) collective-permute-start(bf16[2,224,960]{2,1,0:T(8,128)(2,1)} %collective-permute-done.refs_4_), channel_id=1, source_target_pairs={{0,4},{4,0},{8,12},{12,8},{16,20},{20,16},{24,28},{28,24},{1,5},{5... | collective-permute-start | bytes 2580488 | tf_op jit(solution)/shard_map/second/ppermute | solution.py:24
  80.4 27.6 %collective-permute-start.12 = (bf16[2,224,960]{2,1,0:T(8,128)(2,1)}, bf16[2,224,960]{2,1,0:T(8,128)(2,1)}, u32[]{:S(2)}, u32[]{:S(2)}) collective-permute-start(bf16[2,224,960]{2,1,0:T(8,128)(2,1)} %collective-permute-done.refs_4_), channel_id=1, source_target_pairs={{0,8},{4,12},{8,0},{12,4},{16,24},{20,28},{24,16},{28,20},{1,9},{5... | collective-permute-start | bytes 2580488 | tf_op jit(solution)/shard_map/second/ppermute | solution.py:24
  82.6 7.9 %collective-permute-start.13 = (bf16[2,256,224]{2,1,0:T(8,128)(2,1)S(1)}, bf16[2,256,224]{2,1,0:T(8,128)(2,1)}, u32[]{:S(2)}, u32[]{:S(2)}) collective-permute-start(bf16[2,256,224]{2,1,0:T(8,128)(2,1)S(1)} %get-tuple-element.64), channel_id=1, source_target_pairs={{0,2},{1,3},{2,0},{3,1},{4,6},{5,7},{6,4},{7,5},{8,10},{9,11},{10,... | collective-permute-start | bytes 688136 | tf_op jit(solution)/shard_map/second/ppermute | solution.py:24
  108.0 6.0 %collective-permute-start.14 = (bf16[2,2,256,224]{3,2,1,0:T(8,128)(2,1)S(1)}, bf16[2,2,256,224]{3,2,1,0:T(8,128)(2,1)S(1)}, u32[]{:S(2)}, u32[]{:S(2)}) collective-permute-start(bf16[2,2,256,224]{3,2,1,0:T(8,128)(2,1)S(1)} %pad_maximum_fusion.5), channel_id=1, source_target_pairs={{0,1},{1,0},{2,3},{3,2},{4,5},{5,4},{6,7},{7,6},{8,9},{9,8},{10,11... | collective-permute-start | bytes 1376264 | tf_op jit(solution)/shard_map/third/ppermute | solution.py:24
  108.0 16.1 %collective-permute-start.15 = (bf16[256,1152]{1,0:T(8,128)(2,1)}, bf16[256,1152]{1,0:T(8,128)(2,1)}, u32[]{:S(2)}, u32[]{:S(2)}) collective-permute-start(bf16[256,1152]{1,0:T(8,128)(2,1)} %bitcast.22), channel_id=1, source_target_pairs={{0,2},{1,3},{2,0},{3,1},{4,6},{5,7},{6,4},{7,5},{8,10},{9,11},{10,... | collective-permute-start | bytes 1769480 | tf_op jit(solution)/shard_map/norm/ppermute | solution.py:24
  110.3 13.7 %collective-permute-start.16 = (bf16[224,960]{1,0:T(8,128)(2,1)}, bf16[224,960]{1,0:T(8,128)(2,1)S(1)}, u32[]{:S(2)}, u32[]{:S(2)}) collective-permute-start(bf16[224,960]{1,0:T(8,128)(2,1)} %slice_bitcast_fusion.1), channel_id=1, source_target_pairs={{0,4},{4,0},{8,12},{12,8},{16,20},{20,16},{24,28},{28,24},{1,5},{5... | collective-permute-start | bytes 1290248 | tf_op jit(solution)/shard_map/third/ppermute | solution.py:24
  113.3 12.7 %collective-permute-start.17 = (bf16[224,960]{1,0:T(8,128)(2,1)}, bf16[224,960]{1,0:T(8,128)(2,1)}, u32[]{:S(2)}, u32[]{:S(2)}) collective-permute-start(bf16[224,960]{1,0:T(8,128)(2,1)} %slice_bitcast_fusion), channel_id=1, source_target_pairs={{0,8},{4,12},{8,0},{12,4},{16,24},{20,28},{24,16},{28,20},{1,9},{5... | collective-permute-start | bytes 1290248 | tf_op jit(solution)/shard_map/third/ppermute | solution.py:24
  113.9 35.1 %collective-permute-start.22 = (bf16[448,1152]{1,0:T(8,128)(2,1)}, bf16[448,1152]{1,0:T(8,128)(2,1)}, u32[]{:S(2)}, u32[]{:S(2)}) collective-permute-start(bf16[448,1152]{1,0:T(8,128)(2,1)} %collective-permute-done.10), channel_id=1, source_target_pairs={{0,1},{1,0},{2,3},{3,2},{4,5},{5,4},{6,7},{7,6},{8,9},{9,8},{10,11... | collective-permute-start | bytes 3096584 | tf_op jit(solution)/shard_map/norm/ppermute | solution.py:24
  137.7 8.7 %collective-permute-start.19 = (bf16[8,2,32,224]{3,2,0,1:T(8,128)(2,1)S(1)}, bf16[8,2,32,224]{3,2,0,1:T(8,128)(2,1)S(1)}, u32[]{:S(2)}, u32[]{:S(2)}) collective-permute-start(bf16[8,2,32,224]{3,2,0,1:T(8,128)(2,1)S(1)} %fusion.40), channel_id=1, source_target_pairs={{0,2},{1,3},{2,0},{3,1},{4,6},{5,7},{6,4},{7,5},{8,10},{9,11},{10,... | collective-permute-start | bytes 688136 | tf_op jit(solution)/shard_map/image_forward/ppermute | solution.py:24
  141.6 18.7 %collective-permute-start.23 = (bf16[256,1152]{1,0:T(8,128)(2,1)}, bf16[256,1152]{1,0:T(8,128)(2,1)}, u32[]{:S(2)}, u32[]{:S(2)}) collective-permute-start(bf16[256,1152]{1,0:T(8,128)(2,1)} %bitcast.22), channel_id=1, source_target_pairs={{0,1},{1,0},{2,3},{3,2},{4,5},{5,4},{6,7},{7,6},{8,9},{9,8},{10,11... | collective-permute-start | bytes 1769480 | tf_op jit(solution)/shard_map/norm/ppermute | solution.py:24
  146.5 8.8 %collective-permute-start.20 = (bf16[8,32,224]{2,1,0:T(8,128)(2,1)S(1)}, bf16[8,32,224]{2,1,0:T(8,128)(2,1)S(1)}, u32[]{:S(2)}, u32[]{:S(2)}) collective-permute-start(bf16[8,32,224]{2,1,0:T(8,128)(2,1)S(1)} %fusion.66), channel_id=1, source_target_pairs={{0,16},{4,20},{8,24},{12,28},{16,0},{20,4},{24,8},{28,12},{1,17},{... | collective-permute-start | bytes 344072 | tf_op jit(solution)/shard_map/image_forward/ppermute | solution.py:24
  151.3 9.0 %collective-permute-start.24 = (bf16[256,1152]{1,0:T(8,128)(2,1)}, bf16[256,1152]{1,0:T(8,128)(2,1)}, u32[]{:S(2)}, u32[]{:S(2)}) collective-permute-start(bf16[256,1152]{1,0:T(8,128)(2,1)} %collective-permute-done.15), channel_id=1, source_target_pairs={{0,1},{1,0},{2,3},{3,2},{4,5},{5,4},{6,7},{7,6},{8,9},{9,8},{10,11... | collective-permute-start | bytes 1769480 | tf_op jit(solution)/shard_map/norm/ppermute | solution.py:24
  158.9 5.9 %collective-permute-start.26 = (bf16[32,1152]{1,0:T(8,128)(2,1)S(1)}, bf16[32,1152]{1,0:T(8,128)(2,1)S(1)}, u32[]{:S(2)}, u32[]{:S(2)}) collective-permute-start(bf16[32,1152]{1,0:T(8,128)(2,1)S(1)} %multiply_convert_fusion.6), channel_id=1, source_target_pairs={{0,2},{1,3},{2,0},{3,1},{4,6},{5,7},{6,4},{7,5},{8,10},{9,11},{10,... | collective-permute-start | bytes 221192 | tf_op jit(solution)/shard_map/text_loss/ppermute | solution.py:24
  169.3 16.8 %collective-permute-start.25 = (bf16[8,32,224]{2,1,0:T(8,128)(2,1)S(1)}, bf16[8,32,224]{2,1,0:T(8,128)(2,1)S(1)}, u32[]{:S(2)}, u32[]{:S(2)}) collective-permute-start(bf16[8,32,224]{2,1,0:T(8,128)(2,1)S(1)} %bitcast.205), channel_id=1, source_target_pairs={{0,16},{4,20},{8,24},{12,28},{16,0},{20,4},{24,8},{28,12},{1,17},{... | collective-permute-start | bytes 344072 | tf_op jit(solution)/shard_map/image_backward/ppermute | solution.py:24
  174.0 30.9 %all-to-all-start.1 = ((bf16[8,32,1152]{2,1,0:T(8,128)(2,1)}), bf16[8,32,1152]{2,1,0:T(8,128)(2,1)}, u32[]{:S(2)}, u32[]{:S(2)}) async-start(bf16[8,32,1152]{2,1,0:T(8,128)(2,1)} %bitcast.46), calls=%async_computation.1 | async-start | bytes 1179648 | tf_op jit(solution)/shard_map/text_loss/all_to_all | solution.py:380
  208.3 4.4 %collective-permute-start.31 = (bf16[32,1152]{1,0:T(8,128)(2,1)S(1)}, bf16[32,1152]{1,0:T(8,128)(2,1)S(1)}, u32[]{:S(2)}, u32[]{:S(2)}) collective-permute-start(bf16[32,1152]{1,0:T(8,128)(2,1)S(1)} %get-tuple-element.58), channel_id=1, source_target_pairs={{0,2},{1,3},{2,0},{3,1},{4,6},{5,7},{6,4},{7,5},{8,10},{9,11},{10,... | collective-permute-start | bytes 221192 | tf_op jit(solution)/shard_map/text_backward/ppermute | solution.py:24
  211.0 8.4 %collective-permute-start.29 = (bf16[2,256,256]{2,1,0:T(8,128)(2,1)}, bf16[2,256,256]{2,1,0:T(8,128)(2,1)}, u32[]{:S(2)}, u32[]{:S(2)}) collective-permute-start(bf16[2,256,256]{2,1,0:T(8,128)(2,1)} %fusion.39), channel_id=1, source_target_pairs={{0,2},{1,3},{2,0},{3,1},{4,6},{5,7},{6,4},{7,5},{8,10},{9,11},{10,... | collective-permute-start | bytes 786440 | tf_op jit(solution)/shard_map/image_backward/ppermute | solution.py:24
  215.7 7.8 %collective-permute-start.33 = (bf16[2,128,292]{1,2,0:T(8,128)(2,1)S(1)}, bf16[2,128,292]{1,2,0:T(8,128)(2,1)}, u32[]{:S(2)}, u32[]{:S(2)}) collective-permute-start(bf16[2,128,292]{1,2,0:T(8,128)(2,1)S(1)} %pad_maximum_fusion.8), channel_id=1, source_target_pairs={{0,1},{1,0},{2,3},{3,2},{4,5},{5,4},{6,7},{7,6},{8,9},{9,8},{10,11... | collective-permute-start | bytes 448520 | tf_op jit(solution)/shard_map/text_backward/ppermute | solution.py:24
  220.6 8.7 %collective-permute-start.30 = (bf16[2,128,256]{2,1,0:T(8,128)(2,1)S(1)}, bf16[2,128,256]{2,1,0:T(8,128)(2,1)S(1)}, u32[]{:S(2)}, u32[]{:S(2)}) collective-permute-start(bf16[2,128,256]{2,1,0:T(8,128)(2,1)S(1)} %slice.217), channel_id=1, source_target_pairs={{0,16},{4,20},{8,24},{12,28},{16,0},{20,4},{24,8},{28,12},{1,17},{... | collective-permute-start | bytes 393224 | tf_op jit(solution)/shard_map/image_backward/ppermute | solution.py:24
  224.8 6.7 %collective-permute-start.34 = (bf16[1,128,292]{1,2,0:T(8,128)(2,1)S(1)}, bf16[1,128,292]{1,2,0:T(8,128)(2,1)S(1)}, u32[]{:S(2)}, u32[]{:S(2)}) collective-permute-start(bf16[1,128,292]{1,2,0:T(8,128)(2,1)S(1)} %maximum_bitcast_fusion), channel_id=1, source_target_pairs={{0,2},{1,3},{2,0},{3,1},{4,6},{5,7},{6,4},{7,5},{8,10},{9,11},{10,... | collective-permute-start | bytes 224264 | tf_op jit(solution)/shard_map/text_backward/ppermute | solution.py:24
  (31 other events, 184.0 us)

commit v4 on v3

--- a/solution.py
+++ b/solution.py
@@ -17,6 +17,8 @@
 SMEM = pl.BlockSpec(memory_space=pltpu.SMEM)
 ANY = pl.BlockSpec(memory_space=pl.ANY)
 TAIL = 32
+SLOTS = (0, 1, 2, 4, 3, 5, 6, 7)
+PAIRED = 5
 PARAMS = pltpu.CompilerParams(vmem_limit_bytes=60 * 1024 * 1024)
 
 
@@ -44,11 +46,13 @@
     return lax.dynamic_index_in_dim(array, index, axis, False)
 
 
-def halves(shard, img):
-    half = shard.shape[-1] // 2
-    low, high = shard[..., :half], shard[..., half:]
-    upper = img >= lax.axis_size("img") // 2
-    return jnp.where(upper, high, low), jnp.where(upper, low, high)
+def exchange(halves, img):
+    top = lax.axis_size("img") // 2
+    pairs = [[at, at + top] for at in range(top)]
+    got = lax.all_to_all(
+        halves, "img", split_axis=0, concat_axis=0, tiled=True, axis_index_groups=pairs
+    )
+    return take(got, 1 - img // top)
 
 
 def widen(block, img):
@@ -113,23 +117,34 @@
 
 def fetch(which, blocks, buffer, sems):
     copies = []
-    for at, block in enumerate(blocks):
-        source, slot = block.at[which] if at < 7 else block, which * 8 + at
-        copies.append(pltpu.make_async_copy(source, buffer.at[slot], sems.at[slot]))
-    for copy in copies:
-        copy.start()
-    return copies
-
-
-def forward_kernel(ids, scaled, *refs):
-    before, gains, keep, send, buffer, sems = refs[9:]
-    ups = fetch(0, refs[:8], buffer, sems)
-    downs = fetch(1, refs[:7] + refs[8:9], buffer, sems)
-    rows = before.shape[0]
-    total = jnp.zeros((scaled.shape[1], before.shape[1]), F32)
-    for at in range(8):
+    for at, block in zip(SLOTS, blocks[:5] + blocks[5 + 3 * which : 8 + 3 * which]):
+        source, slot = block.at[which] if at in SLOTS[:PAIRED] else block, which * 8 + at
+        copies.append((at, pltpu.make_async_copy(source, buffer.at[slot], sems.at[slot])))
+    return dict(copies)
+
+
+def up_kernel(ids, scaled, *refs):
+    partial, buffer, sems = refs[11:]
+    ups = fetch(0, refs[:11], buffer, sems)
+    for at in range(7):
+        ups[at].start()
+    total = jnp.zeros(partial.shape, F32)
+    for at in range(7):
         ups[at].wait()
         total = total + dot(scaled[ids[0] ^ at], buffer[at], 1, 0)
+    partial[...] = total
+
+
+def forward_kernel(ids, scaled, partial, *refs):
+    before, gains, keep, send, buffer, sems = refs[11:]
+    ups = fetch(0, refs[:11], buffer, sems)
+    downs = fetch(1, refs[:11], buffer, sems)
+    ups[7].start()
+    for copy in downs.values():
+        copy.start()
+    rows = before.shape[0]
+    ups[7].wait()
+    total = partial[...] + dot(scaled[ids[0] ^ 7], buffer[7], 1, 0)
     value = total[:rows]
     before[...] = value
     bend = jnp.tanh(GELU_C * (value + GELU_A * value * value * value))
@@ -145,19 +160,24 @@
         send[block] = jnp.where(odd, value[:, 0], value[:, 1]).astype(BF16)
 
 
-def back_kernel(split, ids, near, far, before, gains, *refs):
-    outs, others, buffer, sems = refs[9:]
-    downs = fetch(1, refs[:7] + refs[8:9], buffer, sems)
-    ups = fetch(0, refs[:8], buffer, sems)
+def back_kernel(split, ids, *refs):
+    parts, (before, gains), refs = refs[:8], refs[8:10], refs[10:]
+    outs, others, buffer, sems, upstreams = refs[11:]
+    downs = fetch(1, refs[:11], buffer, sems)
+    ups = fetch(0, refs[:11], buffer, sems)
+    for copy in downs.values():
+        copy.start()
     rows, hidden = before.shape
-    half, width = rows // 2, buffer.shape[1]
+    width = buffer.shape[1]
+    for side in range(2):
+        for at, flip in enumerate(FLIPS):
+            upstreams[:, side * 4 + (ids[2] ^ flip)] = parts[side * 4 + at][...]
     total = jnp.zeros((rows, hidden), F32)
     for at in range(8):
         downs[at].wait()
+        ups[at].start()
         block = ids[0] ^ at
-        upstream = jnp.concatenate(
-            [near[:, block].reshape(half, width), far[:, block].reshape(half, width)]
-        )
+        upstream = upstreams[block].reshape(rows, width)
         total = total + dot(upstream, buffer[8 + at], 1, 0)
     value = before[...]
     square = value * value
@@ -171,7 +191,7 @@
     second = jnp.sum(grad * value, axis=1, keepdims=True)
     lane = lax.broadcasted_iota(jnp.int32, (rows, TAIL), 1)
     tail = jnp.where(lane == 0, first, jnp.where(lane == 1, second, 0.0))
-    for copy in ups:
+    for copy in ups.values():
         copy.wait()
     if not split:
         others[...] = tail
@@ -186,11 +206,12 @@
             ref[at // 2, at % 2, :, width:] = tail.astype(ref.dtype)
 
 
-def call(kernel, name, shapes, operands, weights=()):
+def call(kernel, name, shapes, operands, weights=(), more=()):
     scratch = []
     if weights:
         scratch.append(pltpu.VMEM((16,) + weights[0].shape[1:], BF16))
         scratch.append(pltpu.SemaphoreType.DMA((16,)))
+    scratch.extend(more)
     flops = 2 * 256 * 224 * 960 * 16 if weights else 0
     return pl.pallas_call(
         kernel,
@@ -279,10 +300,12 @@
     gate = lax.optimization_barrier
 
     with jax.named_scope("first"):
-        near, send = halves(jnp.stack([image_up, image_down.T]), img)
-        near, far = widen(near, img), widen(swap(send, "img", top), img)
+        shard = jnp.stack([image_up, image_down.T])
+        low, high = shard[..., :hidden_half], shard[..., hidden_half:]
+        both_halves = gate(jnp.stack([low, high]))
+        far = widen(exchange(both_halves, img), img)
+        near = widen(take(both_halves, img // top), img)
         near_y, near_z = swap(near, "img", 1), swap(near, "img", 2)
-        near_zy = swap(near_z, "img", 1)
         text_x = swap(text_in, "grp", 2)
         text_parts = [text_in, text_x, swap(text_in, "grp", 1), swap(text_x, "grp", 1)]
         text_parts = place(text_parts, grp, FLIPS)
@@ -298,25 +321,29 @@
         total = take(total, x) + swap(send, "grp", 2).astype(F32)
         own_in = image_in.reshape(rows, share_count, width).transpose(1, 0, 2)
         far_in = swap(own_in, "img", top)
-        head_x = swap(tie(image_head, text_parts), "grp", 2)
-        far, near_y, near_zy, total, far_in, head_x = gate(
-            (far, near_y, near_zy, total, far_in, head_x)
+        head_x = swap(image_head, "grp", 2)
+        near_last = swap(near_z, "img", 1)
+        far, near_y, near_z, near_last, total, far_in, head_x = gate(
+            (far, near_y, near_z, near_last, total, far_in, head_x)
         )
 
     with jax.named_scope("second"):
-        far_y, far_z = swap(far, "img", 1), swap(far, "img", 2)
+        far_y = [swap(far[at], "img", 1) for at in (0, 1)]
+        far_z = [swap(far[at], "img", 2) for at in (0, 1)]
         both = jnp.concatenate([own_in, far_in], 1)
         both = jnp.stack([both, swap(both, "grp", 2)])
+        far_y, far_z, both = gate((far_y, far_z, both))
+
+    with jax.named_scope("third"):
+        far_last = [swap(far_z[0], "img", 1), swap(far_y[1], "img", 2)]
+        weights = [near, near_y, near_z, far, near_last]
+        for at in (0, 1):
+            weights += [far_y[at], far_z[at], far_last[at]]
+        both = jnp.concatenate([both, swap(both, "grp", 1)])
         text_embed = lax.dynamic_slice_in_dim(text_whole, grp * quarter, quarter, 0) + total
         text_inv, text_unit = unit_rows(text_embed)
         copies = jnp.broadcast_to(text_unit, (members,) + text_unit.shape)
         share = lax.all_to_all(copies, "img", split_axis=0, concat_axis=0, tiled=True)
-        far_y, far_z, both, share = gate((far_y, far_z, both, share))
-
-    with jax.named_scope("third"):
-        up_last, down_last = swap(far_z[0], "img", 1), swap(far_y[1], "img", 2)
-        weights = [near, near_y, near_z, near_zy, far, far_y, far_z, up_last, down_last]
-        both = jnp.concatenate([both, swap(both, "grp", 1)])
         text_gains = jnp.sum(text_up.astype(F32) * text_gain[:, None], axis=0)
         share = share.reshape(members * quarter, embed_width)
         at = jnp.arange(members * quarter, dtype=jnp.int32)
@@ -341,10 +368,17 @@
             ),
             (ids, both, gain),
         )
-        scaled = blocked(tie(scaled, share_x, head))
+        scaled = blocked(scaled)
 
     with jax.named_scope("image_forward"):
         shape = (8, 4, quarter, image_features // 8)
+        (partial,) = call(
+            up_kernel,
+            "up",
+            (jax.ShapeDtypeStruct((2 * rows + 16, hidden_half), F32),),
+            (ids, scaled),
+            weights[:7] + [weights[6]] * 4,
+        )
         before, gains, keep, send = call(
             forward_kernel,
             "forward",
@@ -354,10 +388,10 @@
                 jax.ShapeDtypeStruct(shape, F32),
                 jax.ShapeDtypeStruct(shape, BF16),
             ),
-            (ids, scaled),
+            (ids, scaled, tie(partial, share, head)),
             weights,
         )
-        total = (keep + swap(send, "grp", 1).astype(F32)).reshape(8, 2, 2, quarter, -1)
+        total = (keep + tie(swap(send, "grp", 1), share_x).astype(F32)).reshape(8, 2, 2, quarter, -1)
         send = take(total, 1 - x, 2).astype(BF16)
         got = swap(send, "grp", 2)
         total = take(total, x, 2) + got.astype(F32)
@@ -366,20 +400,6 @@
         image_mid16 = image_mid16.transpose(1, 0, 2).reshape(quarter, image_features)
         image_embed = dot(image_mid16, head.reshape(image_features, embed_width), 1, 0)
         image_inv, image_unit = unit_rows(image_embed)
-
-    with jax.named_scope("text_loss"):
-        pair = jnp.stack([image_unit, swap(image_unit, "grp", 2)])
-        image_units = jnp.concatenate([pair, swap(pair, "grp", 1)]).reshape(rows, embed_width)
-        logits = scale * dot(image_units, share, 1, 1) + shift
-        at = jnp.arange(quarter, dtype=jnp.int32)
-        group_ids = jnp.concatenate([img * rows + (grp ^ flip) * quarter + at for flip in FLIPS])
-        same = (group_ids[:, None] == (share_ids + grp * quarter)[None, :]).astype(F32)
-        pull = (jax.nn.sigmoid(logits) - same).astype(BF16)
-        text_partial = (scale * dot(pull, image_units, 0, 0)).astype(BF16)
-        text_partial = text_partial.reshape(members, quarter, embed_width)
-        text_parts = lax.all_to_all(
-            text_partial, "img", split_axis=0, concat_axis=0, tiled=True
-        )
 
     with jax.named_scope("image_loss"):
         image_ids = img * rows + grp * quarter + jnp.arange(quarter, dtype=jnp.int32)
@@ -392,10 +412,28 @@
         grad_mid16 = grad_mid16.astype(BF16).reshape(quarter, members, width)
         grad_mid16 = blocked(grad_mid16.transpose(1, 0, 2))
 
+    with jax.named_scope("text_loss"):
+        unit_x = tie(swap(image_unit, "grp", 2), grad_embed16)
+        pair = jnp.stack([image_unit, unit_x])
+        image_units = jnp.concatenate([pair, swap(pair, "grp", 1)]).reshape(rows, embed_width)
+        image_units = tie(image_units, grad_mid16)
+        logits = scale * dot(image_units, share, 1, 1) + shift
+        at = jnp.arange(quarter, dtype=jnp.int32)
+        group_ids = jnp.concatenate([img * rows + (grp ^ flip) * quarter + at for flip in FLIPS])
+        same = (group_ids[:, None] == (share_ids + grp * quarter)[None, :]).astype(F32)
+        pull = (jax.nn.sigmoid(logits) - same).astype(BF16)
+        text_partial = (scale * dot(pull, image_units, 0, 0)).astype(BF16)
+        text_partial = text_partial.reshape(members, quarter, embed_width)
+        text_parts = lax.all_to_all(
+            text_partial, "img", split_axis=0, concat_axis=0, tiled=True
+        )
+
     with jax.named_scope("image_backward"):
-        far_grad = swap(grad_mid16, "img", top)
-        near_whole = lax.all_gather(grad_mid16, "grp")
-        far_whole = lax.all_gather(tie(far_grad, text_partial), "grp")
+        far_grad = tie(swap(grad_mid16, "img", top), text_partial)
+        sides = []
+        for part in (grad_mid16, far_grad):
+            part_x = swap(part, "grp", 2)
+            sides += [part, part_x, swap(part, "grp", 1), swap(part_x, "grp", 1)]
         split = members == 8
         if split:
             shape = (2, share_count, 2 * rows, width + TAIL)
@@ -409,8 +447,9 @@
             functools.partial(back_kernel, split),
             "back",
             shapes,
-            (ids, near_whole, far_whole, before, gains),
+            (ids, *sides, before, gains),
             weights,
+            [pltpu.VMEM((8, 8, quarter, image_features // 8), BF16)],
         )
         if not split:
             tail = jnp.broadcast_to(send, (members,) + send.shape)
@@ -419,6 +458,7 @@
             keep, send = take(total, core, 1), take(total, 1 - core, 1).astype(BF16)
         total = keep + tie(swap(send, "grp", 1), text_parts).astype(F32)
         send = take(total, 1 - x).astype(BF16)
+        text_parts, send, own_parts = gate((text_parts, send, sides[:4]))
         total = take(total, x) + swap(send, "grp", 2).astype(F32)
         got = swap(total[:, rows:].astype(BF16), "img", top).astype(F32)
         total = total[:, :rows] + got
@@ -432,8 +472,12 @@
             take(gain.reshape(4, share_count, 1, width), grp),
             image_features,
         )
-        own_grad = in_order(near_whole.transpose(1, 0, 2, 3).reshape(8, rows, -1), members)
-        own_grad = take(own_grad.reshape(4, share_count, rows, width), grp)
+        own_grad = [
+            take(in_order(part, members).reshape(4, share_count, quarter, width), grp)
+            for part in own_parts
+        ]
+        own_grad = place(own_grad, grp, FLIPS).transpose(1, 0, 2, 3)
+        own_grad = own_grad.reshape(share_count, rows, width)
         image_grad = (own_grad.astype(F32) + back).astype(BF16)
         image_grad = image_grad.transpose(1, 0, 2).reshape(rows, image_cols)
 

time: 235 us -> 220 us (0.936)
  blocking collectives: 15.5 us -> 0 us
  starting transfers between devices: 40.6 us -> 56 us
  waiting for transfers between devices: 79.4 us -> 65.8 us
  other arithmetic: 26.9 us -> 22.3 us
  Pallas kernels: 20 us -> 24.4 us
    ppermute x35 -> x42, waiting for transfers between devices: 79.4 us -> 55.9 us  [swap(): lax.ppermute(value, axis, [(i, i ^ flip) for i in range(lax.axis_size(axi...]
    all_gather x2 -> x0, blocking collectives: 15.5 us -> none  [the longest x1 7.95 us: shards(): far_whole = lax.all_gather(tie(far_grad, text_partial), 'grp')]
    all_to_all x0 -> x1, waiting for transfers between devices: none -> 9.88 us  [exchange(): lax.all_to_all(halves, 'img', split_axis=0, concat_axis=0, tiled=True, ax...]
    ppermute x35 -> x42, starting transfers between devices: 31.7 us -> 39.7 us  [swap(): lax.ppermute(value, axis, [(i, i ^ flip) for i in range(lax.axis_size(axi...]
    all_to_all x0 -> x1, starting transfers between devices: none -> 4.73 us  [exchange(): lax.all_to_all(halves, 'img', split_axis=0, concat_axis=0, tiled=True, ax...]
    pallas_call x3 -> x4, Pallas kernels: 20 us -> 24.4 us  [call(): pl.pallas_call(kernel, out_shape=shapes, in_specs=[SMEM] + [VMEM] * (len(...]
    select_n x1 -> x0, other arithmetic: 3.92 us -> none  [halves(): return (jnp.where(upper, high, low), jnp.where(upper, low, high))]
    all_to_all x1, starting transfers between devices: 4.38 us -> 7.34 us  [shards(): lax.all_to_all(copies, 'img', split_axis=0, concat_axis=0, tiled=True)]
  transfers between devices with their start and end apart: 37 -> 45, of which waited for: 14 -> 20; matrix products, arithmetic and copies ran while one was open for 29% -> 28% of each run, Pallas kernels for 9% -> 11%
where the time goes in v4:
time: 220 us; the launch traced here: 218 us
  waiting for transfers between devices  65.8 us (30%)
  starting transfers between devices  56 us (25%)
  local copies, waits for them, and re-layouts  31.3 us (14%)
  Pallas kernels  24.4 us (11%)
  other arithmetic  22.3 us (10%)
  matrix products  15.9 us (7%)
  between operations  2.94 us (1%)
    ppermute x42, waiting for transfers between devices, swap(): lax.ppermute(value, axis, [(i, i ^ flip) for i in range(lax.axis_size(axi...  55.9 us
    ppermute x42, starting transfers between devices, swap(): lax.ppermute(value, axis, [(i, i ^ flip) for i in range(lax.axis_size(axi...  39.7 us
    pallas_call x4, Pallas kernels, call(): pl.pallas_call(kernel, out_shape=shapes, in_specs=[SMEM] + [VMEM] * (len(...  24.4 us
    dot_general x11, matrix products, dot(): return lax.dot_general(left, right, dims, preferred_element_type=F32)  15.9 us
    dynamic_update_slice x15, local copies, waits for them, and re-layouts, place(): whole = lax.dynamic_update_index_in_dim(whole, part, index ^ flip, 0)  12.4 us
    all_to_all x1, waiting for transfers between devices, exchange(): lax.all_to_all(halves, 'img', split_axis=0, concat_axis=0, tiled=True, ax...  9.88 us
    all_to_all x1, starting transfers between devices, shards(): lax.all_to_all(copies, 'img', split_axis=0, concat_axis=0, tiled=True)  7.34 us
    unnamed x86, local copies, waits for them, and re-layouts  5.05 us
  transfers between devices with their start and end apart: 45, of which 20 were waited for; matrix products, arithmetic and copies ran while one was open for 28% of the time, Pallas kernels for 11%

profile of v4, /device:TPU:0, one launch (start us, length us, event | category | flops | bytes accessed | tf_op | source)
XLA Modules:
  0.0 218.5 jit_solution(703018973591429726)
XLA Ops:
  0.6 3.0 %collective-permute-start.3 = (bf16[128,288]{0,1:T(8,128)(2,1)}, bf16[128,288]{0,1:T(8,128)(2,1)S(1)}, u32[]{:S(2)}, u32[]{:S(2)}) collective-permute-start(bf16[128,288]{0,1:T(8,128)(2,1)} %param.12), channel_id=1, source_target_pairs={{0,2},{1,3},{2,0},{3,1},{4,6},{5,7},{6,4},{7,5},{8,10},{9,11},{10,... | collective-permute-start | bytes 221192 | tf_op jit(solution)/shard_map/first/ppermute | solution.py:26
  11.4 4.7 %all-to-all-start = ((bf16[2,2,224,960]{3,2,1,0:T(8,128)(2,1)}), bf16[2,2,224,960]{3,2,1,0:T(8,128)(2,1)}, u32[]{:S(2)}, u32[]{:S(2)}) async-start(bf16[2,2,224,960]{3,2,1,0:T(8,128)(2,1)} %pad_maximum_fusion.1), calls=%async_computation | async-start | bytes 3670016 | tf_op jit(solution)/shard_map/first/all_to_all | solution.py:52
  16.7 2.3 %broadcast_in_dim.84 = bf16[4,448,1152]{2,1,0:T(8,128)(2,1)} broadcast(bf16[]{:T(256)} %constant.203.clone.1), dimensions={} | broadcast | bytes 4128770 | tf_op jit(solution)/shard_map/norm/broadcast_in_dim | solution.py:30
  19.0 2.3 %bitcast_dynamic-update-slice_fusion.3 = bf16[4,448,1152]{2,1,0:T(8,128)(2,1)} fusion(bf16[4,448,1152]{2,1,0:T(8,128)(2,1)} %broadcast_in_dim.84, s32[]{:T(128)S(6)} %select_n.130, bf16[448,1152]{1,0:T(8,128)(2,1)} %param.19), kind=kLoop, calls=%fused_computation.34 | loop fusion | bytes 2064388 | tf_op jit(solution)/shard_map/norm/jit(dynamic_update_index_in_dim)/dynamic_update_slice | solution.py:32
  21.6 2.9 %collective-permute-start.8 = (bf16[2,128,224]{2,1,0:T(8,128)(2,1)S(1)}, bf16[2,128,224]{2,1,0:T(8,128)(2,1)}, u32[]{:S(2)}, u32[]{:S(2)}) collective-permute-start(bf16[2,128,224]{2,1,0:T(8,128)(2,1)S(1)} %bitcast.211), channel_id=1, source_target_pairs={{0,16},{4,20},{8,24},{12,28},{16,0},{20,4},{24,8},{28,12},{1,17},{... | collective-permute-start | bytes 344072 | tf_op jit(solution)/shard_map/first/ppermute | solution.py:26
  31.0 13.5 %collective-permute-done.1.refs_2_.refs_12_ = bf16[2,224,960]{2,1,0:T(8,128)(2,1)} collective-permute-done((bf16[2,224,960]{2,1,0:T(8,128)(2,1)S(1)}, bf16[2,224,960]{2,1,0:T(8,128)(2,1)}, u32[]{:S(2)}, u32[]{:S(2)}) %collective-permute-start.1) | collective-permute-done | bytes 860192 | tf_op jit(solution)/shard_map/first/ppermute | solution.py:26
  44.5 2.5 %collective-permute-start.2 = (bf16[2,224,960]{2,1,0:T(8,128)(2,1)}, bf16[2,224,960]{2,1,0:T(8,128)(2,1)}, u32[]{:S(2)}, u32[]{:S(2)}) collective-permute-start(bf16[2,224,960]{2,1,0:T(8,128)(2,1)} %collective-permute-done.1.refs_2_.refs_12_), channel_id=1, source_target_pairs={{0,4},{4,0},{8,12},{12,8},{16,20},{20,16},{24,28},{28,24},{1,5},{5... | collective-permute-start | bytes 2580488 | tf_op jit(solution)/shard_map/first/ppermute | solution.py:26
  53.1 9.9 %all-to-all-done = bf16[2,2,224,960]{3,2,1,0:T(8,128)(2,1)} async-done(((bf16[2,2,224,960]{3,2,1,0:T(8,128)(2,1)}), bf16[2,2,224,960]{3,2,1,0:T(8,128)(2,1)}, u32[]{:S(2)}, u32[]{:S(2)}) %all-to-all-start) | async-done | bytes 1720352 | tf_op jit(solution)/shard_map/first/all_to_all | solution.py:52
  64.9 2.7 %collective-permute-done.2.refs_4_.refs_14_ = bf16[2,224,960]{2,1,0:T(8,128)(2,1)} collective-permute-done((bf16[2,224,960]{2,1,0:T(8,128)(2,1)}, bf16[2,224,960]{2,1,0:T(8,128)(2,1)}, u32[]{:S(2)}, u32[]{:S(2)}) %collective-permute-start.2) | collective-permute-done | bytes 860192 | tf_op jit(solution)/shard_map/first/ppermute | solution.py:26
  70.6 2.0 collective-permute-start.13
  76.6 7.3 %all-to-all-start.1 = ((bf16[8,32,1152]{2,1,0:T(8,128)(2,1)}), bf16[8,32,1152]{2,1,0:T(8,128)(2,1)}, u32[]{:S(2)}, u32[]{:S(2)}) async-start(bf16[8,32,1152]{2,1,0:T(8,128)(2,1)} %broadcast_in_dim.83), calls=%async_computation.1 | async-start | bytes 1179648 | tf_op jit(solution)/shard_map/third/all_to_all | solution.py:346
  85.2 7.5 %collective-permute-done.11.refs_8_.refs_18_ = bf16[224,960]{1,0:T(8,128)(2,1)} collective-permute-done((bf16[224,960]{1,0:T(8,128)(2,1)}, bf16[224,960]{1,0:T(8,128)(2,1)}, u32[]{:S(2)}, u32[]{:S(2)}) %collective-permute-start.11) | collective-permute-done | bytes 430112 | tf_op jit(solution)/shard_map/second/ppermute | solution.py:26
  92.7 4.3 %collective-permute-done.13.refs_9_.refs_19_ = bf16[224,960]{1,0:T(8,128)(2,1)} collective-permute-done((bf16[224,960]{1,0:T(8,128)(2,1)}, bf16[224,960]{1,0:T(8,128)(2,1)}, u32[]{:S(2)}, u32[]{:S(2)}) %collective-permute-start.13) | collective-permute-done | bytes 430112 | tf_op jit(solution)/shard_map/second/ppermute | solution.py:26
  100.5 2.2 %pad_maximum_fusion.4.parts = bf16[4,2,256,224]{3,2,1,0:T(8,128)(2,1)} fusion(bf16[2,2,256,224]{3,2,1,0:T(8,128)(2,1)} %collective-permute-done.15, bf16[2,2,256,224]{3,2,1,0:T(8,128)(2,1)S(1)} %pad_maximum_fusion.6), kind=kLoop, calls=%fused_computation.28 | loop fusion | flops 458752 | bytes 1835008 | tf_op jit(solution)/shard_map/third/concatenate | solution.py:342
  102.7 3.5 %norm.1 = (bf16[8,272,224]{2,1,0:T(8,128)(2,1)}, bf16[8,32,224]{2,1,0:T(8,128)(2,1)}, f32[256,1]{1,0:T(8,128)}, f32[256,1]{1,0:T(8,128)}) custom-call(s32[3]{0:T(128)} %pad_add_fusion.1.ids, bf16[4,2,256,224]{3,2,1,0:T(8,128)(2,1)} %pad_maximum_fusion.4.parts, f32[8,1,224]{2,1,0:T(1,128)} %reshape.153.gain), custom_call_target="tpu_custom_call" | custom-call | bytes 6291456 | tf_op jit(solution)/shard_map/norm/norm/pallas_call | solution.py:216
  106.2 5.0 %up.1.partial = f32[272,960]{1,0:T(8,128)} custom-call(s32[3]{0:T(128)} %pad_add_fusion.1.ids, bf16[8,272,224]{2,1,0:T(8,128)(2,1)} %get-tuple-element.40.scaled, bf16[2,224,960]{2,1,0:T(8,128)(2,1)} %copy-done.3, bf16[2,224,960]{2,1,0:T(8,128)(2,1)} %collective-permute-done.refs_1_.refs_11_, bf16[2,224,960]{2,1,0:T(8,128)(2,1)} %collective-permute-done.1.refs_2_.refs_12_, ...), custom_call_target="tpu_custom_call" | custom-call | flops 1761607680 | bytes 6291456 | tf_op jit(solution)/shard_map/image_forward/up/pallas_call | solution.py:216
  112.6 8.0 %forward.1 = (f32[256,960]{1,0:T(8,128)}, f32[1,960]{1,0:T(1,128)}, f32[8,4,32,224]{3,2,1,0:T(8,128)}, bf16[8,4,32,224]{3,2,1,0:T(8,128)(2,1)}) custom-call(s32[3]{0:T(128)} %pad_add_fusion.1.ids, bf16[8,272,224]{2,1,0:T(8,128)(2,1)} %get-tuple-element.40.scaled, f32[272,960]{1,0:T(8,128)} %up.1.partial, bf16[2,224,960]{2,1,0:T(8,128)(2,1)} %copy-done.3, ...), custom_call_target="tpu_custom_call" | custom-call | flops 1761607680 | bytes 6291456 | tf_op jit(solution)/shard_map/image_forward/forward/pallas_call | solution.py:216
  120.7 2.4 %bitcast_dynamic-update-slice_fusion.2 = bf16[4,448,1152]{2,1,0:T(8,128)(2,1)} fusion(bf16[4,448,1152]{2,1,0:T(8,128)(2,1)} %bitcast_dynamic-update-slice_fusion.3, s32[]{:T(128)S(6)} %select_n.131, bf16[448,1152]{1,0:T(8,128)(2,1)} %collective-permute-done.9), kind=kLoop, calls=%fused_computation.33 | loop fusion | bytes 2064388 | tf_op jit(solution)/shard_map/norm/jit(dynamic_update_index_in_dim)/dynamic_update_slice | solution.py:32
  123.1 3.7 %collective-permute-done.19 = bf16[256,1152]{1,0:T(8,128)(2,1)S(1)} collective-permute-done((bf16[256,1152]{1,0:T(8,128)(2,1)}, bf16[256,1152]{1,0:T(8,128)(2,1)S(1)}, u32[]{:S(2)}, u32[]{:S(2)}) %collective-permute-start.19) | collective-permute-done | bytes 589856 | tf_op jit(solution)/shard_map/norm/ppermute | solution.py:26
  127.6 2.3 %bitcast_dynamic-update-slice_fusion.1 = bf16[4,448,1152]{2,1,0:T(8,128)(2,1)} fusion(bf16[4,448,1152]{2,1,0:T(8,128)(2,1)} %bitcast_dynamic-update-slice_fusion.2, s32[]{:T(128)S(6)} %select_n.132, bf16[448,1152]{1,0:T(8,128)(2,1)} %collective-permute-done.22), kind=kLoop, calls=%fused_computation.32 | loop fusion | bytes 2064388 | tf_op jit(solution)/shard_map/norm/jit(dynamic_update_index_in_dim)/dynamic_update_slice | solution.py:32
  129.9 4.7 %collective-permute-done.20 = bf16[8,2,32,224]{3,2,0,1:T(8,128)(2,1)S(1)} collective-permute-done((bf16[8,2,32,224]{3,2,0,1:T(8,128)(2,1)S(1)}, bf16[8,2,32,224]{3,2,0,1:T(8,128)(2,1)S(1)}, u32[]{:S(2)}, u32[]{:S(2)}) %collective-permute-start.20) | collective-permute-done | bytes 229408 | tf_op jit(solution)/shard_map/image_forward/ppermute | solution.py:26
  134.7 8.6 %collective-permute-start.21 = (bf16[8,32,224]{2,1,0:T(8,128)(2,1)S(1)}, bf16[8,32,224]{2,1,0:T(8,128)(2,1)S(1)}, u32[]{:S(2)}, u32[]{:S(2)}) collective-permute-start(bf16[8,32,224]{2,1,0:T(8,128)(2,1)S(1)} %fusion.68), channel_id=1, source_target_pairs={{0,16},{4,20},{8,24},{12,28},{16,0},{20,4},{24,8},{28,12},{1,17},{... | collective-permute-start | bytes 344072 | tf_op jit(solution)/shard_map/image_forward/ppermute | solution.py:26
  143.3 2.3 %bitcast_dynamic-update-slice_fusion = bf16[4,448,1152]{2,1,0:T(8,128)(2,1)} fusion(bf16[4,448,1152]{2,1,0:T(8,128)(2,1)} %bitcast_dynamic-update-slice_fusion.1, s32[]{:T(128)S(6)} %select_n.133, bf16[448,1152]{1,0:T(8,128)(2,1)} %collective-permute-done.23), kind=kLoop, calls=%fused_computation.31 | loop fusion | bytes 2064388 | tf_op jit(solution)/shard_map/norm/jit(dynamic_update_index_in_dim)/dynamic_update_slice | solution.py:32
  147.9 3.1 %multiply_reduce_fusion.4 = (f32[32]{0:T(128)S(1)}, f32[32,1152]{1,0:T(8,128)S(1)}) fusion(bf16[32,1792]{1,0:T(8,128)(2,1)S(1)} %reshape.156, bf16[1792,1152]{1,0:T(8,128)(2,1)} %bitcast.40), kind=kOutput, calls=%fused_computation.126 | convolution fusion | flops 132194272 | bytes 4391040 | tf_op jit(solution)/shard_map/image_forward/dot_general | solution.py:42
  151.9 3.0 %multiply_reduce_fusion.3 = (f32[32]{0:T(128)S(1)}, f32[32,1152]{1,0:T(8,128)S(1)}) fusion(f32[32,1152]{1,0:T(8,128)S(1)} %get-tuple-element.98, bf16[256,1152]{1,0:T(8,128)(2,1)} %collective-permute-done.26, bf16[256,1152]{1,0:T(8,128)(2,1)S(1)} %collective-permute-done.25, bf16[256,1152]{1,0:T(8,128)(2,1)S(1)} %collective-permute-done.19, ...), kind=kOutput, calls=%fused_computation.124 | convolution fusion | flops 170348512 | bytes 2658696 | tf_op jit(solution)/shard_map/image_loss/dot_general | solution.py:42
  155.6 3.4 %convolution_convert_fusion = bf16[32,1792]{1,0:T(8,128)(2,1)S(1)} fusion(bf16[32,1152]{1,0:T(8,128)(2,1)S(1)} %multiply_convert_fusion.5, bf16[1792,1152]{1,0:T(8,128)(2,1)} %bitcast.40), kind=kOutput, calls=%fused_computation.5 | convolution fusion | flops 132177920 | bytes 4317184 | tf_op jit(solution)/shard_map/image_loss/dot_general | solution.py:42
  161.1 2.9 %fusion = bf16[256,1152]{1,0:T(8,128)(2,1)} fusion(bf16[128,1152]{1,0:T(8,128)(2,1)S(1)} %bitcast.225, bf16[256,1152]{1,0:T(8,128)(2,1)} %bitcast.29, f32[]{:T(128)} %bitcast, s32[256]{0:T(256)S(1)} %get-tuple-element.104, f32[]{:T(128)} %bitcast.200, s32[128]{0:T(128)S(1)} %pad_add_fusion.2), kind=kOutput, calls=%fused_computation.2 | convolution fusion | flops 151879680 | bytes 1476104 | tf_op jit(solution)/shard_map/text_loss/dot_general | solution.py:42
  164.0 4.2 %all-to-all-start.2 = ((bf16[8,32,1152]{2,1,0:T(8,128)(2,1)}), bf16[8,32,1152]{2,1,0:T(8,128)(2,1)S(1)}, u32[]{:S(2)}, u32[]{:S(2)}) async-start(bf16[8,32,1152]{2,1,0:T(8,128)(2,1)} %bitcast.46), calls=%async_computation.2 | async-start | bytes 1179648 | tf_op jit(solution)/shard_map/text_loss/all_to_all | solution.py:427
  170.2 4.3 %collective-permute-done.28.refs_1_ = bf16[8,32,224]{2,1,0:T(8,128)(2,1)S(1)} collective-permute-done((bf16[8,32,224]{2,1,0:T(8,128)(2,1)S(1)}, bf16[8,32,224]{2,1,0:T(8,128)(2,1)S(1)}, u32[]{:S(2)}, u32[]{:S(2)}) %collective-permute-start.28) | collective-permute-done | bytes 114720 | tf_op jit(solution)/shard_map/image_backward/ppermute | solution.py:26
  178.4 7.9 %back.1 = (f32[2,2,256,256]{3,2,1,0:T(8,128)}, bf16[2,2,256,256]{3,2,1,0:T(8,128)(2,1)}) custom-call(s32[3]{0:T(128)} %pad_add_fusion.1.ids, bf16[8,32,224]{2,1,0:T(8,128)(2,1)} %bitcast.218, bf16[8,32,224]{2,1,0:T(8,128)(2,1)} %copy-done.22, bf16[8,32,224]{2,1,0:T(8,128)(2,1)} %copy-done.23, bf16[8,32,224]{2,1,0:T(8,128)(2,1)} %copy-done.24, ...), custom_call_target="tpu_custom_call" | custom-call | flops 1761607680 | bytes 6291456 | tf_op jit(solution)/shard_map/image_backward/back/pallas_call | solution.py:216
  205.2 2.7 %collective-permute-start.37 = (bf16[2,128,256]{2,1,0:T(8,128)(2,1)S(1)}, bf16[2,128,256]{2,1,0:T(8,128)(2,1)S(1)}, u32[]{:S(2)}, u32[]{:S(2)}) collective-permute-start(bf16[2,128,256]{2,1,0:T(8,128)(2,1)S(1)} %slice.211), channel_id=1, source_target_pairs={{0,16},{4,20},{8,24},{12,28},{16,0},{20,4},{24,8},{28,12},{1,17},{... | collective-permute-start | bytes 393224 | tf_op jit(solution)/shard_map/image_backward/ppermute | solution.py:26
  210.2 4.3 %collective-permute-done.37 = bf16[2,128,256]{2,1,0:T(8,128)(2,1)S(1)} collective-permute-done((bf16[2,128,256]{2,1,0:T(8,128)(2,1)S(1)}, bf16[2,128,256]{2,1,0:T(8,128)(2,1)S(1)}, u32[]{:S(2)}, u32[]{:S(2)}) %collective-permute-start.37) | collective-permute-done | bytes 131104 | tf_op jit(solution)/shard_map/image_backward/ppermute | solution.py:26
  (255 shorter events, 72.0 us)
Async XLA Ops:
  0.6 21.0 %collective-permute-start.3 = (bf16[128,288]{0,1:T(8,128)(2,1)}, bf16[128,288]{0,1:T(8,128)(2,1)S(1)}, u32[]{:S(2)}, u32[]{:S(2)}) collective-permute-start(bf16[128,288]{0,1:T(8,128)(2,1)} %param.12), channel_id=1, source_target_pairs={{0,2},{1,3},{2,0},{3,1},{4,6},{5,7},{6,4},{7,5},{8,10},{9,11},{10,... | collective-permute-start | bytes 221192 | tf_op jit(solution)/shard_map/first/ppermute | solution.py:26
  3.6 20.9 %collective-permute-start.4 = (bf16[128,288]{0,1:T(8,128)(2,1)}, bf16[128,288]{0,1:T(8,128)(2,1)S(1)}, u32[]{:S(2)}, u32[]{:S(2)}) collective-permute-start(bf16[128,288]{0,1:T(8,128)(2,1)} %param.12), channel_id=1, source_target_pairs={{0,1},{1,0},{2,3},{3,2},{4,5},{5,4},{6,7},{7,6},{8,9},{9,8},{10,11... | collective-permute-start | bytes 221192 | tf_op jit(solution)/shard_map/first/ppermute | solution.py:26
  8.2 36.3 %collective-permute-start.1 = (bf16[2,224,960]{2,1,0:T(8,128)(2,1)S(1)}, bf16[2,224,960]{2,1,0:T(8,128)(2,1)}, u32[]{:S(2)}, u32[]{:S(2)}) collective-permute-start(bf16[2,224,960]{2,1,0:T(8,128)(2,1)S(1)} %dynamic-slice_bitcast_fusion.refs_0_.refs_10_), channel_id=1, source_target_pairs={{0,8},{4,12},{8,0},{12,4},{16,24},{20,28},{24,16},{28,20},{1,9},{5... | collective-permute-start | bytes 2580488 | tf_op jit(solution)/shard_map/first/ppermute | solution.py:26
  9.9 55.0 %collective-permute-start = (bf16[2,224,960]{2,1,0:T(8,128)(2,1)S(1)}, bf16[2,224,960]{2,1,0:T(8,128)(2,1)}, u32[]{:S(2)}, u32[]{:S(2)}) collective-permute-start(bf16[2,224,960]{2,1,0:T(8,128)(2,1)S(1)} %dynamic-slice_bitcast_fusion.refs_0_.refs_10_), channel_id=1, source_target_pairs={{0,4},{4,0},{8,12},{12,8},{16,20},{20,16},{24,28},{28,24},{1,5},{5... | collective-permute-start | bytes 2580488 | tf_op jit(solution)/shard_map/first/ppermute | solution.py:26
  11.4 51.6 %all-to-all-start = ((bf16[2,2,224,960]{3,2,1,0:T(8,128)(2,1)}), bf16[2,2,224,960]{3,2,1,0:T(8,128)(2,1)}, u32[]{:S(2)}, u32[]{:S(2)}) async-start(bf16[2,2,224,960]{3,2,1,0:T(8,128)(2,1)} %pad_maximum_fusion.1), calls=%async_computation | async-start | bytes 3670016 | tf_op jit(solution)/shard_map/first/all_to_all | solution.py:52
  16.1 48.8 %collective-permute-start.9 = (bf16[448,1152]{1,0:T(8,128)(2,1)}, bf16[448,1152]{1,0:T(8,128)(2,1)}, u32[]{:S(2)}, u32[]{:S(2)}) collective-permute-start(bf16[448,1152]{1,0:T(8,128)(2,1)} %param.19), channel_id=1, source_target_pairs={{0,2},{1,3},{2,0},{3,1},{4,6},{5,7},{6,4},{7,5},{8,10},{9,11},{10,... | collective-permute-start | bytes 3096584 | tf_op jit(solution)/shard_map/first/ppermute | solution.py:26
  21.6 43.2 %collective-permute-start.8 = (bf16[2,128,224]{2,1,0:T(8,128)(2,1)S(1)}, bf16[2,128,224]{2,1,0:T(8,128)(2,1)}, u32[]{:S(2)}, u32[]{:S(2)}) collective-permute-start(bf16[2,128,224]{2,1,0:T(8,128)(2,1)S(1)} %bitcast.211), channel_id=1, source_target_pairs={{0,16},{4,20},{8,24},{12,28},{16,0},{20,4},{24,8},{28,12},{1,17},{... | collective-permute-start | bytes 344072 | tf_op jit(solution)/shard_map/first/ppermute | solution.py:26
  44.5 23.1 %collective-permute-start.2 = (bf16[2,224,960]{2,1,0:T(8,128)(2,1)}, bf16[2,224,960]{2,1,0:T(8,128)(2,1)}, u32[]{:S(2)}, u32[]{:S(2)}) collective-permute-start(bf16[2,224,960]{2,1,0:T(8,128)(2,1)} %collective-permute-done.1.refs_2_.refs_12_), channel_id=1, source_target_pairs={{0,4},{4,0},{8,12},{12,8},{16,20},{20,16},{24,28},{28,24},{1,5},{5... | collective-permute-start | bytes 2580488 | tf_op jit(solution)/shard_map/first/ppermute | solution.py:26
  68.6 16.6 %collective-permute-start.10 = (bf16[224,960]{1,0:T(8,128)(2,1)}, bf16[224,960]{1,0:T(8,128)(2,1)S(1)}, u32[]{:S(2)}, u32[]{:S(2)}) collective-permute-start(bf16[224,960]{1,0:T(8,128)(2,1)} %get-tuple-element.84), channel_id=1, source_target_pairs={{0,4},{4,0},{8,12},{12,8},{16,20},{20,16},{24,28},{28,24},{1,5},{5... | collective-permute-start | bytes 1290248 | tf_op jit(solution)/shard_map/second/ppermute | solution.py:26
  70.3 22.4 %collective-permute-start.12 = (bf16[224,960]{1,0:T(8,128)(2,1)}, bf16[224,960]{1,0:T(8,128)(2,1)S(1)}, u32[]{:S(2)}, u32[]{:S(2)}) collective-permute-start(bf16[224,960]{1,0:T(8,128)(2,1)} %get-tuple-element.84), channel_id=1, source_target_pairs={{0,8},{4,12},{8,0},{12,4},{16,24},{20,28},{24,16},{28,20},{1,9},{5... | collective-permute-start | bytes 1290248 | tf_op jit(solution)/shard_map/second/ppermute | solution.py:26
  70.3 22.4 %collective-permute-start.11 = (bf16[224,960]{1,0:T(8,128)(2,1)}, bf16[224,960]{1,0:T(8,128)(2,1)}, u32[]{:S(2)}, u32[]{:S(2)}) collective-permute-start(bf16[224,960]{1,0:T(8,128)(2,1)} %get-tuple-element.83), channel_id=1, source_target_pairs={{0,4},{4,0},{8,12},{12,8},{16,20},{20,16},{24,28},{28,24},{1,5},{5... | collective-permute-start | bytes 1290248 | tf_op jit(solution)/shard_map/second/ppermute | solution.py:26
  70.6 26.4 %collective-permute-start.13 = (bf16[224,960]{1,0:T(8,128)(2,1)}, bf16[224,960]{1,0:T(8,128)(2,1)}, u32[]{:S(2)}, u32[]{:S(2)}) collective-permute-start(bf16[224,960]{1,0:T(8,128)(2,1)} %get-tuple-element.83), channel_id=1, source_target_pairs={{0,8},{4,12},{8,0},{12,4},{16,24},{20,28},{24,16},{28,20},{1,9},{5... | collective-permute-start | bytes 1290248 | tf_op jit(solution)/shard_map/second/ppermute | solution.py:26
  75.1 8.9 %collective-permute-start.14 = (bf16[2,256,224]{2,1,0:T(8,128)(2,1)}, bf16[2,256,224]{2,1,0:T(8,128)(2,1)}, u32[]{:S(2)}, u32[]{:S(2)}) collective-permute-start(bf16[2,256,224]{2,1,0:T(8,128)(2,1)} %get-tuple-element.86), channel_id=1, source_target_pairs={{0,2},{1,3},{2,0},{3,1},{4,6},{5,7},{6,4},{7,5},{8,10},{9,11},{10,... | collective-permute-start | bytes 688136 | tf_op jit(solution)/shard_map/second/ppermute | solution.py:26
  76.6 34.6 %all-to-all-start.1 = ((bf16[8,32,1152]{2,1,0:T(8,128)(2,1)}), bf16[8,32,1152]{2,1,0:T(8,128)(2,1)}, u32[]{:S(2)}, u32[]{:S(2)}) async-start(bf16[8,32,1152]{2,1,0:T(8,128)(2,1)} %broadcast_in_dim.83), calls=%async_computation.1 | async-start | bytes 1179648 | tf_op jit(solution)/shard_map/third/all_to_all | solution.py:346
  83.9 43.6 %collective-permute-start.22 = (bf16[448,1152]{1,0:T(8,128)(2,1)}, bf16[448,1152]{1,0:T(8,128)(2,1)}, u32[]{:S(2)}, u32[]{:S(2)}) collective-permute-start(bf16[448,1152]{1,0:T(8,128)(2,1)} %param.19), channel_id=1, source_target_pairs={{0,1},{1,0},{2,3},{3,2},{4,5},{5,4},{6,7},{7,6},{8,9},{9,8},{10,11... | collective-permute-start | bytes 3096584 | tf_op jit(solution)/shard_map/norm/ppermute | solution.py:26
  97.7 14.1 %collective-permute-start.16 = (bf16[224,960]{1,0:T(8,128)(2,1)S(1)}, bf16[224,960]{1,0:T(8,128)(2,1)S(1)}, u32[]{:S(2)}, u32[]{:S(2)}) collective-permute-start(bf16[224,960]{1,0:T(8,128)(2,1)S(1)} %collective-permute-done.12.refs_6_.refs_7_.refs_8_.refs_9_.refs_10_.refs_16_), channel_id=1, source_target_pairs={{0,4},{4,0},{8,12},{12,8},{16,20},{20,16},{24,28},{28,24},{1,5},{5... | collective-permute-start | bytes 1290248 | tf_op jit(solution)/shard_map/third/ppermute | solution.py:26
  97.9 14.0 %collective-permute-start.17 = (bf16[224,960]{1,0:T(8,128)(2,1)}, bf16[224,960]{1,0:T(8,128)(2,1)}, u32[]{:S(2)}, u32[]{:S(2)}) collective-permute-start(bf16[224,960]{1,0:T(8,128)(2,1)} %collective-permute-done.11.refs_8_.refs_18_), channel_id=1, source_target_pairs={{0,8},{4,12},{8,0},{12,4},{16,24},{20,28},{24,16},{28,20},{1,9},{5... | collective-permute-start | bytes 1290248 | tf_op jit(solution)/shard_map/third/ppermute | solution.py:26
  100.0 43.3 %collective-permute-start.23 = (bf16[448,1152]{1,0:T(8,128)(2,1)}, bf16[448,1152]{1,0:T(8,128)(2,1)}, u32[]{:S(2)}, u32[]{:S(2)}) collective-permute-start(bf16[448,1152]{1,0:T(8,128)(2,1)} %collective-permute-done.9), channel_id=1, source_target_pairs={{0,1},{1,0},{2,3},{3,2},{4,5},{5,4},{6,7},{7,6},{8,9},{9,8},{10,11... | collective-permute-start | bytes 3096584 | tf_op jit(solution)/shard_map/norm/ppermute | solution.py:26
  111.2 15.6 %collective-permute-start.19 = (bf16[256,1152]{1,0:T(8,128)(2,1)}, bf16[256,1152]{1,0:T(8,128)(2,1)S(1)}, u32[]{:S(2)}, u32[]{:S(2)}) collective-permute-start(bf16[256,1152]{1,0:T(8,128)(2,1)} %bitcast.29), channel_id=1, source_target_pairs={{0,2},{1,3},{2,0},{3,1},{4,6},{5,7},{6,4},{7,5},{8,10},{9,11},{10,... | collective-permute-start | bytes 1769480 | tf_op jit(solution)/shard_map/norm/ppermute | solution.py:26
  127.1 7.5 %collective-permute-start.20 = (bf16[8,2,32,224]{3,2,0,1:T(8,128)(2,1)S(1)}, bf16[8,2,32,224]{3,2,0,1:T(8,128)(2,1)S(1)}, u32[]{:S(2)}, u32[]{:S(2)}) collective-permute-start(bf16[8,2,32,224]{3,2,0,1:T(8,128)(2,1)S(1)} %fusion.42), channel_id=1, source_target_pairs={{0,2},{1,3},{2,0},{3,1},{4,6},{5,7},{6,4},{7,5},{8,10},{9,11},{10,... | collective-permute-start | bytes 688136 | tf_op jit(solution)/shard_map/image_forward/ppermute | solution.py:26
  129.9 22.0 %collective-permute-start.25 = (bf16[256,1152]{1,0:T(8,128)(2,1)}, bf16[256,1152]{1,0:T(8,128)(2,1)S(1)}, u32[]{:S(2)}, u32[]{:S(2)}) collective-permute-start(bf16[256,1152]{1,0:T(8,128)(2,1)} %bitcast.29), channel_id=1, source_target_pairs={{0,1},{1,0},{2,3},{3,2},{4,5},{5,4},{6,7},{7,6},{8,9},{9,8},{10,11... | collective-permute-start | bytes 1769480 | tf_op jit(solution)/shard_map/norm/ppermute | solution.py:26
  134.7 12.9 %collective-permute-start.21 = (bf16[8,32,224]{2,1,0:T(8,128)(2,1)S(1)}, bf16[8,32,224]{2,1,0:T(8,128)(2,1)S(1)}, u32[]{:S(2)}, u32[]{:S(2)}) collective-permute-start(bf16[8,32,224]{2,1,0:T(8,128)(2,1)S(1)} %fusion.68), channel_id=1, source_target_pairs={{0,16},{4,20},{8,24},{12,28},{16,0},{20,4},{24,8},{28,12},{1,17},{... | collective-permute-start | bytes 344072 | tf_op jit(solution)/shard_map/image_forward/ppermute | solution.py:26
  145.6 6.3 %collective-permute-start.26 = (bf16[256,1152]{1,0:T(8,128)(2,1)S(1)}, bf16[256,1152]{1,0:T(8,128)(2,1)}, u32[]{:S(2)}, u32[]{:S(2)}) collective-permute-start(bf16[256,1152]{1,0:T(8,128)(2,1)S(1)} %collective-permute-done.19), channel_id=1, source_target_pairs={{0,1},{1,0},{2,3},{3,2},{4,5},{5,4},{6,7},{7,6},{8,9},{9,8},{10,11... | collective-permute-start | bytes 1769480 | tf_op jit(solution)/shard_map/norm/ppermute | solution.py:26
  159.3 9.8 %collective-permute-start.31 = (bf16[8,32,224]{2,1,0:T(8,128)(2,1)S(1)}, bf16[8,32,224]{2,1,0:T(8,128)(2,1)S(1)}, u32[]{:S(2)}, u32[]{:S(2)}) collective-permute-start(bf16[8,32,224]{2,1,0:T(8,128)(2,1)S(1)} %bitcast.215), channel_id=1, source_target_pairs={{0,16},{4,20},{8,24},{12,28},{16,0},{20,4},{24,8},{28,12},{1,17},{... | collective-permute-start | bytes 344072 | tf_op jit(solution)/shard_map/image_backward/ppermute | solution.py:26
  164.0 26.4 %all-to-all-start.2 = ((bf16[8,32,1152]{2,1,0:T(8,128)(2,1)}), bf16[8,32,1152]{2,1,0:T(8,128)(2,1)S(1)}, u32[]{:S(2)}, u32[]{:S(2)}) async-start(bf16[8,32,1152]{2,1,0:T(8,128)(2,1)} %bitcast.46), calls=%async_computation.2 | async-start | bytes 1179648 | tf_op jit(solution)/shard_map/text_loss/all_to_all | solution.py:427
  168.2 6.4 %collective-permute-start.28 = (bf16[8,32,224]{2,1,0:T(8,128)(2,1)S(1)}, bf16[8,32,224]{2,1,0:T(8,128)(2,1)S(1)}, u32[]{:S(2)}, u32[]{:S(2)}) collective-permute-start(bf16[8,32,224]{2,1,0:T(8,128)(2,1)S(1)} %bitcast.216), channel_id=1, source_target_pairs={{0,2},{1,3},{2,0},{3,1},{4,6},{5,7},{6,4},{7,5},{8,10},{9,11},{10,... | collective-permute-start | bytes 344072 | tf_op jit(solution)/shard_map/image_backward/ppermute | solution.py:26
  169.1 7.2 %collective-permute-start.32 = (bf16[8,32,224]{2,1,0:T(8,128)(2,1)S(1)}, bf16[8,32,224]{2,1,0:T(8,128)(2,1)S(1)}, u32[]{:S(2)}, u32[]{:S(2)}) collective-permute-start(bf16[8,32,224]{2,1,0:T(8,128)(2,1)S(1)} %collective-permute-done.31.refs_4_), channel_id=1, source_target_pairs={{0,2},{1,3},{2,0},{3,1},{4,6},{5,7},{6,4},{7,5},{8,10},{9,11},{10,... | collective-permute-start | bytes 344072 | tf_op jit(solution)/shard_map/image_backward/ppermute | solution.py:26
  170.2 6.2 %collective-permute-start.29 = (bf16[8,32,224]{2,1,0:T(8,128)(2,1)S(1)}, bf16[8,32,224]{2,1,0:T(8,128)(2,1)S(1)}, u32[]{:S(2)}, u32[]{:S(2)}) collective-permute-start(bf16[8,32,224]{2,1,0:T(8,128)(2,1)S(1)} %bitcast.217), channel_id=1, source_target_pairs={{0,1},{1,0},{2,3},{3,2},{4,5},{5,4},{6,7},{7,6},{8,9},{9,8},{10,11... | collective-permute-start | bytes 344072 | tf_op jit(solution)/shard_map/image_backward/ppermute | solution.py:26
  194.7 9.3 %collective-permute-start.36 = (bf16[2,256,256]{2,1,0:T(8,128)(2,1)}, bf16[2,256,256]{2,1,0:T(8,128)(2,1)}, u32[]{:S(2)}, u32[]{:S(2)}) collective-permute-start(bf16[2,256,256]{2,1,0:T(8,128)(2,1)} %fusion.41), channel_id=1, source_target_pairs={{0,2},{1,3},{2,0},{3,1},{4,6},{5,7},{6,4},{7,5},{8,10},{9,11},{10,... | collective-permute-start | bytes 786440 | tf_op jit(solution)/shard_map/image_backward/ppermute | solution.py:26
  201.9 6.0 %collective-permute-start.40 = (bf16[2,128,292]{1,2,0:T(8,128)(2,1)S(1)}, bf16[2,128,292]{1,2,0:T(8,128)(2,1)}, u32[]{:S(2)}, u32[]{:S(2)}) collective-permute-start(bf16[2,128,292]{1,2,0:T(8,128)(2,1)S(1)} %pad_maximum_fusion.9), channel_id=1, source_target_pairs={{0,1},{1,0},{2,3},{3,2},{4,5},{5,4},{6,7},{7,6},{8,9},{9,8},{10,11... | collective-permute-start | bytes 448520 | tf_op jit(solution)/shard_map/text_backward/ppermute | solution.py:26
  205.2 9.3 %collective-permute-start.37 = (bf16[2,128,256]{2,1,0:T(8,128)(2,1)S(1)}, bf16[2,128,256]{2,1,0:T(8,128)(2,1)S(1)}, u32[]{:S(2)}, u32[]{:S(2)}) collective-permute-start(bf16[2,128,256]{2,1,0:T(8,128)(2,1)S(1)} %slice.211), channel_id=1, source_target_pairs={{0,16},{4,20},{8,24},{12,28},{16,0},{20,4},{24,8},{28,12},{1,17},{... | collective-permute-start | bytes 393224 | tf_op jit(solution)/shard_map/image_backward/ppermute | solution.py:26
  209.2 7.5 %collective-permute-start.41 = (bf16[1,128,292]{1,2,0:T(8,128)(2,1)S(1)}, bf16[1,128,292]{1,2,0:T(8,128)(2,1)S(1)}, u32[]{:S(2)}, u32[]{:S(2)}) collective-permute-start(bf16[1,128,292]{1,2,0:T(8,128)(2,1)S(1)} %maximum_bitcast_fusion), channel_id=1, source_target_pairs={{0,2},{1,3},{2,0},{3,1},{4,6},{5,7},{6,4},{7,5},{8,10},{9,11},{10,... | collective-permute-start | bytes 224264 | tf_op jit(solution)/shard_map/text_backward/ppermute | solution.py:26
  (55 other events, 419.4 us)

commit v5 on v4

--- a/solution.py
+++ b/solution.py
@@ -19,6 +19,7 @@
 TAIL = 32
 SLOTS = (0, 1, 2, 4, 3, 5, 6, 7)
 PAIRED = 5
+MEBIBYTES = {"norm": 12, "up": 18, "forward": 28, "back": 28}
 PARAMS = pltpu.CompilerParams(vmem_limit_bytes=60 * 1024 * 1024)
 
 
@@ -85,14 +86,17 @@
     return split.transpose(0, 3, 1, 2, 4).reshape(members, rows, width)
 
 
-def norm_kernel(ids, parts, gain, scaled, own, mean, inverse):
-    _, share_count, rows, _ = parts.shape
+def norm_kernel(ids, *refs):
+    parts, (gain, scaled, own, mean, inverse) = refs[:4], refs[4:]
+    share_count, rows, _ = parts[0].shape
     quarter = own.shape[1]
-    features = float(4 * share_count * parts.shape[3])
+    features = float(4 * share_count * parts[0].shape[2])
     picks = [(at, sub) for at in range(4) for sub in range(share_count)]
 
     def sum_rows(term):
-        return sum(jnp.sum(term(parts[pick].astype(F32)), axis=1, keepdims=True) for pick in picks)
+        return sum(
+            jnp.sum(term(parts[at][sub].astype(F32)), axis=1, keepdims=True) for at, sub in picks
+        )
 
     center = sum_rows(lambda value: value) / features
     variance = sum_rows(lambda value: (value - center) * (value - center)) / features
@@ -102,9 +106,9 @@
     start = pl.multiple_of(ids[2] * quarter, quarter)
     for at, sub in picks:
         block = (ids[2] ^ FLIPS[at]) * share_count + sub
-        value = parts[at, sub].astype(F32)
+        value = parts[at][sub].astype(F32)
         scaled[block, :rows] = ((value - center) * factor * gain[block]).astype(BF16)
-        own[block] = parts[at, sub, pl.ds(start, quarter)]
+        own[block] = parts[at][sub, pl.ds(start, quarter)]
         rest = jnp.broadcast_to(gain[block], (16, gain.shape[2]))
         line = lax.broadcasted_iota(jnp.int32, rest.shape, 0)
         split = jnp.zeros_like(rest)
@@ -220,7 +224,9 @@
         out_specs=tuple(VMEM for _ in shapes),
         scratch_shapes=scratch,
         compiler_params=PARAMS,
-        cost_estimate=pl.CostEstimate(flops=flops, bytes_accessed=6 << 20, transcendentals=0),
+        cost_estimate=pl.CostEstimate(
+            flops=flops, bytes_accessed=MEBIBYTES[name] << 20, transcendentals=0
+        ),
         name=name,
     )(*operands, *weights)
 
@@ -306,6 +312,8 @@
         far = widen(exchange(both_halves, img), img)
         near = widen(take(both_halves, img // top), img)
         near_y, near_z = swap(near, "img", 1), swap(near, "img", 2)
+        own_in = image_in.reshape(rows, share_count, width).transpose(1, 0, 2)
+        far_in = swap(own_in, "img", top)
         text_x = swap(text_in, "grp", 2)
         text_parts = [text_in, text_x, swap(text_in, "grp", 1), swap(text_x, "grp", 1)]
         text_parts = place(text_parts, grp, FLIPS)
@@ -319,44 +327,26 @@
         total = take(text_branch, core, 1) + swap(send, "grp", 1).astype(F32)
         send = take(total, 1 - x).astype(BF16)
         total = take(total, x) + swap(send, "grp", 2).astype(F32)
-        own_in = image_in.reshape(rows, share_count, width).transpose(1, 0, 2)
-        far_in = swap(own_in, "img", top)
         head_x = swap(image_head, "grp", 2)
         near_last = swap(near_z, "img", 1)
-        far, near_y, near_z, near_last, total, far_in, head_x = gate(
-            (far, near_y, near_z, near_last, total, far_in, head_x)
-        )
+        gain = image_gain.reshape(members, 1, width)
+        text_gains = jnp.sum(text_up.astype(F32) * text_gain[:, None], axis=0)
+        own_gain = lax.dynamic_slice_in_dim(text_gain, grp * text_cols, text_cols, 0)
+        ready = (ids, gain, text_gains, own_gain)
+        far, near_y, near_z, near_last, total, far_in, head_x, ready = gate(
+            (far, near_y, near_z, near_last, total, far_in, head_x, ready)
+        )
+        ids, gain, text_gains, own_gain = ready
 
     with jax.named_scope("second"):
-        far_y = [swap(far[at], "img", 1) for at in (0, 1)]
-        far_z = [swap(far[at], "img", 2) for at in (0, 1)]
+        far_parts, total = gate(([far[0], far[1]], total))
+        far_y = [swap(part, "img", 1) for part in far_parts]
+        far_z = [swap(part, "img", 2) for part in far_parts]
         both = jnp.concatenate([own_in, far_in], 1)
-        both = jnp.stack([both, swap(both, "grp", 2)])
-        far_y, far_z, both = gate((far_y, far_z, both))
-
-    with jax.named_scope("third"):
-        far_last = [swap(far_z[0], "img", 1), swap(far_y[1], "img", 2)]
-        weights = [near, near_y, near_z, far, near_last]
-        for at in (0, 1):
-            weights += [far_y[at], far_z[at], far_last[at]]
-        both = jnp.concatenate([both, swap(both, "grp", 1)])
-        text_embed = lax.dynamic_slice_in_dim(text_whole, grp * quarter, quarter, 0) + total
-        text_inv, text_unit = unit_rows(text_embed)
-        copies = jnp.broadcast_to(text_unit, (members,) + text_unit.shape)
-        share = lax.all_to_all(copies, "img", split_axis=0, concat_axis=0, tiled=True)
-        text_gains = jnp.sum(text_up.astype(F32) * text_gain[:, None], axis=0)
-        share = share.reshape(members * quarter, embed_width)
-        at = jnp.arange(members * quarter, dtype=jnp.int32)
-        share_ids = at // quarter * rows + at % quarter
-        text_ids = jnp.concatenate([share_ids + (grp ^ flip) * quarter for flip in FLIPS])
-
-    with jax.named_scope("norm"):
-        share_x = swap(share, "grp", 2)
-        every = [share, share_x, swap(share, "grp", 1), swap(share_x, "grp", 1)]
-        every_text = jnp.concatenate(every)
-        heads = [image_head, head_x, swap(image_head, "grp", 1), swap(head_x, "grp", 1)]
-        head = place(heads, grp, FLIPS).reshape(members, width, embed_width)
-        gain = image_gain.reshape(members, 1, width)
+        both_x = swap(both, "grp", 2)
+        total = tie(total, both_x)
+        far_y, far_z, both, both_x = gate((far_y, far_z, both, both_x))
+        parts = [both, both_x, swap(both, "grp", 1), swap(both_x, "grp", 1)]
         scaled, own_rows, mean, inverse = call(
             norm_kernel,
             "norm",
@@ -366,9 +356,36 @@
                 jax.ShapeDtypeStruct((2 * rows, 1), F32),
                 jax.ShapeDtypeStruct((2 * rows, 1), F32),
             ),
-            (ids, both, gain),
+            (ids, *parts, gain),
         )
         scaled = blocked(scaled)
+
+    with jax.named_scope("third"):
+        far_last = [swap(far_z[0], "img", 1), swap(far_y[1], "img", 2)]
+        weights = [near, near_y, near_z, far, near_last]
+        for at in (0, 1):
+            weights += [far_y[at], far_z[at], far_last[at]]
+        text_embed = lax.dynamic_slice_in_dim(text_whole, grp * quarter, quarter, 0) + total
+        text_inv, text_unit = unit_rows(text_embed)
+        copies = jnp.broadcast_to(text_unit, (top,) + text_unit.shape)
+        lines = [list(range(first, members, 2)) for first in (0, 1)]
+        line = lax.all_to_all(
+            copies, "img", split_axis=0, concat_axis=0, tiled=True, axis_index_groups=lines
+        )
+        other = swap(line, "img", 1)
+        odd = img % 2 == 1
+        share = jnp.stack([jnp.where(odd, other, line), jnp.where(odd, line, other)], 1)
+        share = share.reshape(members * quarter, embed_width)
+        at = jnp.arange(members * quarter, dtype=jnp.int32)
+        share_ids = at // quarter * rows + at % quarter
+        text_ids = jnp.concatenate([share_ids + (grp ^ flip) * quarter for flip in FLIPS])
+
+    with jax.named_scope("norm"):
+        share_x = swap(share, "grp", 2)
+        every = [share, share_x, swap(share, "grp", 1), swap(share_x, "grp", 1)]
+        every_text = jnp.concatenate(every)
+        heads = [image_head, head_x, swap(image_head, "grp", 1), swap(head_x, "grp", 1)]
+        head = place(heads, grp, FLIPS).reshape(members, width, embed_width)
 
     with jax.named_scope("image_forward"):
         shape = (8, 4, quarter, image_features // 8)
@@ -391,8 +408,8 @@
             (ids, scaled, tie(partial, share, head)),
             weights,
         )
-        total = (keep + tie(swap(send, "grp", 1), share_x).astype(F32)).reshape(8, 2, 2, quarter, -1)
-        send = take(total, 1 - x, 2).astype(BF16)
+        total = (keep + swap(send, "grp", 1).astype(F32)).reshape(8, 2, 2, quarter, -1)
+        send = tie(take(total, 1 - x, 2).astype(BF16), share_x)
         got = swap(send, "grp", 2)
         total = take(total, x, 2) + got.astype(F32)
         branch = total[:, 0] + swap(total[:, 1].astype(BF16), "img", top).astype(F32)
@@ -500,7 +517,6 @@
         send = packed(partial[2] + data[1], sums)[None]
         more_data, more = unpacked(swap(send, "grp", 2), text_cols)
         total, sums = partial[0] + data[0] + more_data[0], sums + more
-        own_gain = lax.dynamic_slice_in_dim(text_gain, grp * text_cols, text_cols, 0)
         back = norm_back(
             total, sums, text_in.astype(F32), text_mean, text_inverse, own_gain, text_features
         )

time: 220 us -> 216 us (0.982)
  starting transfers between devices: 56 us -> 52.9 us
    all_to_all x1, waiting for transfers between devices: 9.88 us -> 7.06 us  [exchange(): lax.all_to_all(halves, 'img', split_axis=0, concat_axis=0, tiled=True, ax...]
    ppermute x42 -> x44, starting transfers between devices: 39.7 us -> 36.9 us  [swap(): lax.ppermute(value, axis, [(i, i ^ flip) for i in range(lax.axis_size(axi...]
    all_to_all x1, waiting for transfers between devices: 0.01 us -> 2.63 us  [shards(): lax.all_to_all(copies, 'img', split_axis=0, concat_axis=0, tiled=True, ax...]
    ppermute x42 -> x44, waiting for transfers between devices: 55.9 us -> 58.2 us  [swap(): lax.ppermute(value, axis, [(i, i ^ flip) for i in range(lax.axis_size(axi...]
    unnamed x86 -> x83, local copies, waits for them, and re-layouts: 5.05 us -> 5.79 us
  transfers between devices with their start and end apart: 45 -> 47, of which waited for: 20 -> 21; matrix products, arithmetic and copies ran while one was open for 28% -> 28% of each run, Pallas kernels for 11% -> 11%
where the time goes in v5:
time: 216 us; the launch traced here: 214 us
  waiting for transfers between devices  67.9 us (31%)
  starting transfers between devices  52.9 us (24%)
  local copies, waits for them, and re-layouts  30.3 us (14%)
  Pallas kernels  24.2 us (11%)
  other arithmetic  20.3 us (9%)
  matrix products  15.9 us (7%)
  between operations  2.98 us (1%)
    ppermute x44, waiting for transfers between devices, swap(): lax.ppermute(value, axis, [(i, i ^ flip) for i in range(lax.axis_size(axi...  58.2 us
    ppermute x44, starting transfers between devices, swap(): lax.ppermute(value, axis, [(i, i ^ flip) for i in range(lax.axis_size(axi...  36.9 us
    pallas_call x4, Pallas kernels, call(): pl.pallas_call(kernel, out_shape=shapes, in_specs=[SMEM] + [VMEM] * (len(...  24.2 us
    dot_general x11, matrix products, dot(): return lax.dot_general(left, right, dims, preferred_element_type=F32)  15.9 us
    dynamic_update_slice x15, local copies, waits for them, and re-layouts, place(): whole = lax.dynamic_update_index_in_dim(whole, part, index ^ flip, 0)  12.4 us
    all_to_all x1, waiting for transfers between devices, exchange(): lax.all_to_all(halves, 'img', split_axis=0, concat_axis=0, tiled=True, ax...  7.06 us
    all_to_all x1, starting transfers between devices, shards(): lax.all_to_all(copies, 'img', split_axis=0, concat_axis=0, tiled=True, ax...  6.59 us
    unnamed x83, local copies, waits for them, and re-layouts  5.79 us
  transfers between devices with their start and end apart: 47, of which 21 were waited for; matrix products, arithmetic and copies ran while one was open for 28% of the time, Pallas kernels for 11%

profile of v5, /device:TPU:0, one launch (start us, length us, event | category | flops | bytes accessed | tf_op | source)
XLA Modules:
  0.0 214.5 jit_solution(12824088674374828533)
XLA Ops:
  0.6 3.0 %collective-permute-start.3 = (bf16[128,288]{0,1:T(8,128)(2,1)}, bf16[128,288]{0,1:T(8,128)(2,1)S(1)}, u32[]{:S(2)}, u32[]{:S(2)}) collective-permute-start(bf16[128,288]{0,1:T(8,128)(2,1)} %param.12), channel_id=1, source_target_pairs={{0,2},{1,3},{2,0},{3,1},{4,6},{5,7},{6,4},{7,5},{8,10},{9,11},{10,... | collective-permute-start | bytes 221192 | tf_op jit(solution)/shard_map/first/ppermute | solution.py:27
  11.4 4.7 %all-to-all-start = ((bf16[2,2,224,960]{3,2,1,0:T(8,128)(2,1)}), bf16[2,2,224,960]{3,2,1,0:T(8,128)(2,1)}, u32[]{:S(2)}, u32[]{:S(2)}) async-start(bf16[2,2,224,960]{3,2,1,0:T(8,128)(2,1)} %pad_maximum_fusion.1), calls=%async_computation | async-start | bytes 3670016 | tf_op jit(solution)/shard_map/first/all_to_all | solution.py:53
  26.7 17.9 %collective-permute-done.1.refs_2_.refs_12_ = bf16[2,224,960]{2,1,0:T(8,128)(2,1)} collective-permute-done((bf16[2,224,960]{2,1,0:T(8,128)(2,1)S(1)}, bf16[2,224,960]{2,1,0:T(8,128)(2,1)}, u32[]{:S(2)}, u32[]{:S(2)}) %collective-permute-start.1) | collective-permute-done | bytes 860192 | tf_op jit(solution)/shard_map/first/ppermute | solution.py:27
  44.6 2.5 %collective-permute-start.2 = (bf16[2,224,960]{2,1,0:T(8,128)(2,1)}, bf16[2,224,960]{2,1,0:T(8,128)(2,1)}, u32[]{:S(2)}, u32[]{:S(2)}) collective-permute-start(bf16[2,224,960]{2,1,0:T(8,128)(2,1)} %collective-permute-done.1.refs_2_.refs_12_), channel_id=1, source_target_pairs={{0,4},{4,0},{8,12},{12,8},{16,20},{20,16},{24,28},{28,24},{1,5},{5... | collective-permute-start | bytes 2580488 | tf_op jit(solution)/shard_map/first/ppermute | solution.py:27
  51.7 2.7 %collective-permute-start.8 = (bf16[2,128,224]{2,1,0:T(8,128)(2,1)S(1)}, bf16[2,128,224]{2,1,0:T(8,128)(2,1)}, u32[]{:S(2)}, u32[]{:S(2)}) collective-permute-start(bf16[2,128,224]{2,1,0:T(8,128)(2,1)S(1)} %bitcast.216), channel_id=1, source_target_pairs={{0,16},{4,20},{8,24},{12,28},{16,0},{20,4},{24,8},{28,12},{1,17},{... | collective-permute-start | bytes 344072 | tf_op jit(solution)/shard_map/first/ppermute | solution.py:27
  56.0 7.1 %all-to-all-done = bf16[2,2,224,960]{3,2,1,0:T(8,128)(2,1)} async-done(((bf16[2,2,224,960]{3,2,1,0:T(8,128)(2,1)}), bf16[2,2,224,960]{3,2,1,0:T(8,128)(2,1)}, u32[]{:S(2)}, u32[]{:S(2)}) %all-to-all-start) | async-done | bytes 1720352 | tf_op jit(solution)/shard_map/first/all_to_all | solution.py:53
  64.9 2.8 %collective-permute-done.2.refs_4_.refs_14_ = bf16[2,224,960]{2,1,0:T(8,128)(2,1)} collective-permute-done((bf16[2,224,960]{2,1,0:T(8,128)(2,1)}, bf16[2,224,960]{2,1,0:T(8,128)(2,1)}, u32[]{:S(2)}, u32[]{:S(2)}) %collective-permute-start.2) | collective-permute-done | bytes 860192 | tf_op jit(solution)/shard_map/first/ppermute | solution.py:27
  72.9 4.1 %collective-permute-done.14.refs_1_ = bf16[2,256,224]{2,1,0:T(8,128)(2,1)} collective-permute-done((bf16[2,256,224]{2,1,0:T(8,128)(2,1)}, bf16[2,256,224]{2,1,0:T(8,128)(2,1)}, u32[]{:S(2)}, u32[]{:S(2)}) %collective-permute-start.14) | collective-permute-done | bytes 229408 | tf_op jit(solution)/shard_map/second/ppermute | solution.py:27
  78.0 6.6 %all-to-all-start.1 = ((bf16[4,32,1152]{2,1,0:T(8,128)(2,1)}), bf16[4,32,1152]{2,1,0:T(8,128)(2,1)}, u32[]{:S(2)}, u32[]{:S(2)}) async-start(bf16[4,32,1152]{2,1,0:T(8,128)(2,1)} %broadcast_in_dim.83), calls=%async_computation.1 | async-start | bytes 589824 | tf_op jit(solution)/shard_map/third/all_to_all | solution.py:372
  84.6 2.3 %broadcast_in_dim.84 = bf16[4,448,1152]{2,1,0:T(8,128)(2,1)} broadcast(bf16[]{:T(256)} %constant.207.clone.1), dimensions={} | broadcast | bytes 4128770 | tf_op jit(solution)/shard_map/norm/broadcast_in_dim | solution.py:31
  86.8 2.3 %bitcast_dynamic-update-slice_fusion.3 = bf16[4,448,1152]{2,1,0:T(8,128)(2,1)} fusion(bf16[4,448,1152]{2,1,0:T(8,128)(2,1)} %broadcast_in_dim.84, s32[]{:T(128)S(6)} %select_n.144, bf16[448,1152]{1,0:T(8,128)(2,1)} %param.19), kind=kLoop, calls=%fused_computation.33 | loop fusion | bytes 2064388 | tf_op jit(solution)/shard_map/norm/jit(dynamic_update_index_in_dim)/dynamic_update_slice | solution.py:33
  89.2 3.1 %collective-permute-done.11.refs_8_.refs_18_ = bf16[224,960]{1,0:T(8,128)(2,1)} collective-permute-done((bf16[224,960]{1,0:T(8,128)(2,1)}, bf16[224,960]{1,0:T(8,128)(2,1)}, u32[]{:S(2)}, u32[]{:S(2)}) %collective-permute-start.11) | collective-permute-done | bytes 430112 | tf_op jit(solution)/shard_map/second/ppermute | solution.py:27
  92.3 4.3 %collective-permute-done.13.refs_9_.refs_19_ = bf16[224,960]{1,0:T(8,128)(2,1)} collective-permute-done((bf16[224,960]{1,0:T(8,128)(2,1)}, bf16[224,960]{1,0:T(8,128)(2,1)}, u32[]{:S(2)}, u32[]{:S(2)}) %collective-permute-start.13) | collective-permute-done | bytes 430112 | tf_op jit(solution)/shard_map/second/ppermute | solution.py:27
  97.1 2.6 %all-to-all-done.1 = bf16[4,32,1152]{2,1,0:T(8,128)(2,1)} async-done(((bf16[4,32,1152]{2,1,0:T(8,128)(2,1)}), bf16[4,32,1152]{2,1,0:T(8,128)(2,1)}, u32[]{:S(2)}, u32[]{:S(2)}) %all-to-all-start.1) | async-done | bytes 294944 | tf_op jit(solution)/shard_map/third/all_to_all | solution.py:372
  105.5 3.4 %norm.1 = (bf16[8,272,224]{2,1,0:T(8,128)(2,1)}, bf16[8,32,224]{2,1,0:T(8,128)(2,1)}, f32[256,1]{1,0:T(8,128)}, f32[256,1]{1,0:T(8,128)}) custom-call(s32[3]{0:T(128)} %pad_add_fusion.1.ids, bf16[2,256,224]{2,1,0:T(8,128)(2,1)} %pad_maximum_fusion.7.refs_0_, bf16[2,256,224]{2,1,0:T(8,128)(2,1)} %collective-permute-done.14.refs_1_, ...), custom_call_target="tpu_custom_call" | custom-call | bytes 12582912 | tf_op jit(solution)/shard_map/second/norm/pallas_call | solution.py:220
  109.0 5.0 %up.1.partial = f32[272,960]{1,0:T(8,128)} custom-call(s32[3]{0:T(128)} %pad_add_fusion.1.ids, bf16[8,272,224]{2,1,0:T(8,128)(2,1)} %get-tuple-element.55.scaled, bf16[2,224,960]{2,1,0:T(8,128)(2,1)} %copy-done.3, bf16[2,224,960]{2,1,0:T(8,128)(2,1)} %collective-permute-done.refs_1_.refs_11_, bf16[2,224,960]{2,1,0:T(8,128)(2,1)} %collective-permute-done.1.refs_2_.refs_12_, ...), custom_call_target="tpu_custom_call" | custom-call | flops 1761607680 | bytes 18874368 | tf_op jit(solution)/shard_map/image_forward/up/pallas_call | solution.py:220
  118.9 8.0 %forward.1 = (f32[256,960]{1,0:T(8,128)}, f32[1,960]{1,0:T(1,128)}, f32[8,4,32,224]{3,2,1,0:T(8,128)}, bf16[8,4,32,224]{3,2,1,0:T(8,128)(2,1)}) custom-call(s32[3]{0:T(128)} %pad_add_fusion.1.ids, bf16[8,272,224]{2,1,0:T(8,128)(2,1)} %get-tuple-element.55.scaled, f32[272,960]{1,0:T(8,128)} %up.1.partial, bf16[2,224,960]{2,1,0:T(8,128)(2,1)} %copy-done.3, ...), custom_call_target="tpu_custom_call" | custom-call | flops 1761607680 | bytes 29360128 | tf_op jit(solution)/shard_map/image_forward/forward/pallas_call | solution.py:220
  127.0 2.4 %bitcast_dynamic-update-slice_fusion.2 = bf16[4,448,1152]{2,1,0:T(8,128)(2,1)} fusion(bf16[4,448,1152]{2,1,0:T(8,128)(2,1)} %bitcast_dynamic-update-slice_fusion.3, s32[]{:T(128)S(6)} %select_n.145, bf16[448,1152]{1,0:T(8,128)(2,1)} %collective-permute-done.9), kind=kLoop, calls=%fused_computation.32 | loop fusion | bytes 2064388 | tf_op jit(solution)/shard_map/norm/jit(dynamic_update_index_in_dim)/dynamic_update_slice | solution.py:33
  132.8 2.3 %bitcast_dynamic-update-slice_fusion.1 = bf16[4,448,1152]{2,1,0:T(8,128)(2,1)} fusion(bf16[4,448,1152]{2,1,0:T(8,128)(2,1)} %bitcast_dynamic-update-slice_fusion.2, s32[]{:T(128)S(6)} %select_n.146, bf16[448,1152]{1,0:T(8,128)(2,1)} %collective-permute-done.24), kind=kLoop, calls=%fused_computation.31 | loop fusion | bytes 2064388 | tf_op jit(solution)/shard_map/norm/jit(dynamic_update_index_in_dim)/dynamic_update_slice | solution.py:33
  135.0 3.5 %collective-permute-done.22 = bf16[8,2,32,224]{3,2,0,1:T(8,128)(2,1)S(1)} collective-permute-done((bf16[8,2,32,224]{3,2,0,1:T(8,128)(2,1)S(1)}, bf16[8,2,32,224]{3,2,0,1:T(8,128)(2,1)S(1)}, u32[]{:S(2)}, u32[]{:S(2)}) %collective-permute-start.22) | collective-permute-done | bytes 229408 | tf_op jit(solution)/shard_map/image_forward/ppermute | solution.py:27
  138.7 2.3 %collective-permute-start.23 = (bf16[8,32,224]{2,1,0:T(8,128)(2,1)S(1)}, bf16[8,32,224]{2,1,0:T(8,128)(2,1)S(1)}, u32[]{:S(2)}, u32[]{:S(2)}) collective-permute-start(bf16[8,32,224]{2,1,0:T(8,128)(2,1)S(1)} %fusion.68), channel_id=1, source_target_pairs={{0,16},{4,20},{8,24},{12,28},{16,0},{20,4},{24,8},{28,12},{1,17},{... | collective-permute-start | bytes 344072 | tf_op jit(solution)/shard_map/image_forward/ppermute | solution.py:27
  141.0 2.3 %bitcast_dynamic-update-slice_fusion = bf16[4,448,1152]{2,1,0:T(8,128)(2,1)} fusion(bf16[4,448,1152]{2,1,0:T(8,128)(2,1)} %bitcast_dynamic-update-slice_fusion.1, s32[]{:T(128)S(6)} %select_n.147, bf16[448,1152]{1,0:T(8,128)(2,1)} %collective-permute-done.25), kind=kLoop, calls=%fused_computation.30 | loop fusion | bytes 2064388 | tf_op jit(solution)/shard_map/norm/jit(dynamic_update_index_in_dim)/dynamic_update_slice | solution.py:33
  143.3 4.1 %collective-permute-done.23 = bf16[8,32,224]{2,1,0:T(8,128)(2,1)S(1)} collective-permute-done((bf16[8,32,224]{2,1,0:T(8,128)(2,1)S(1)}, bf16[8,32,224]{2,1,0:T(8,128)(2,1)S(1)}, u32[]{:S(2)}, u32[]{:S(2)}) %collective-permute-start.23) | collective-permute-done | bytes 114720 | tf_op jit(solution)/shard_map/image_forward/ppermute | solution.py:27
  147.7 3.1 %multiply_reduce_fusion.4 = (f32[32]{0:T(128)S(1)}, f32[32,1152]{1,0:T(8,128)S(1)}) fusion(bf16[32,1792]{1,0:T(8,128)(2,1)S(1)} %reshape.156, bf16[1792,1152]{1,0:T(8,128)(2,1)} %bitcast.41), kind=kOutput, calls=%fused_computation.127 | convolution fusion | flops 132194272 | bytes 4391040 | tf_op jit(solution)/shard_map/image_forward/dot_general | solution.py:43
  152.5 3.0 %multiply_reduce_fusion.3 = (f32[32]{0:T(128)S(1)}, f32[32,1152]{1,0:T(8,128)S(1)}) fusion(f32[32,1152]{1,0:T(8,128)S(1)} %get-tuple-element.116, bf16[256,1152]{1,0:T(8,128)(2,1)S(1)} %collective-permute-done.28, bf16[256,1152]{1,0:T(8,128)(2,1)S(1)} %collective-permute-done.27, bf16[256,1152]{1,0:T(8,128)(2,1)} %collective-permute-done.21, ...), kind=kOutput, calls=%fused_computation.125 | convolution fusion | flops 170348512 | bytes 2658696 | tf_op jit(solution)/shard_map/image_loss/dot_general | solution.py:43
  155.8 3.4 %convolution_convert_fusion = bf16[32,1792]{1,0:T(8,128)(2,1)S(1)} fusion(bf16[32,1152]{1,0:T(8,128)(2,1)S(1)} %multiply_convert_fusion.5, bf16[1792,1152]{1,0:T(8,128)(2,1)} %bitcast.41), kind=kOutput, calls=%fused_computation.5 | convolution fusion | flops 132177920 | bytes 4317184 | tf_op jit(solution)/shard_map/image_loss/dot_general | solution.py:43
  159.6 2.9 %fusion = bf16[256,1152]{1,0:T(8,128)(2,1)} fusion(bf16[128,1152]{1,0:T(8,128)(2,1)S(1)} %bitcast.230, bf16[256,1152]{1,0:T(8,128)(2,1)} %bitcast.30, f32[]{:T(128)} %bitcast, s32[256]{0:T(256)S(1)} %get-tuple-element.122, f32[]{:T(128)} %bitcast.205, s32[128]{0:T(128)S(1)} %pad_add_fusion.2), kind=kOutput, calls=%fused_computation.2 | convolution fusion | flops 151879680 | bytes 1476104 | tf_op jit(solution)/shard_map/text_loss/dot_general | solution.py:43
  162.4 4.6 %all-to-all-start.2 = ((bf16[8,32,1152]{2,1,0:T(8,128)(2,1)}), bf16[8,32,1152]{2,1,0:T(8,128)(2,1)S(1)}, u32[]{:S(2)}, u32[]{:S(2)}) async-start(bf16[8,32,1152]{2,1,0:T(8,128)(2,1)} %bitcast.47), calls=%async_computation.2 | async-start | bytes 1179648 | tf_op jit(solution)/shard_map/text_loss/all_to_all | solution.py:444
  170.2 3.1 %collective-permute-done.30.refs_1_ = bf16[8,32,224]{2,1,0:T(8,128)(2,1)S(1)} collective-permute-done((bf16[8,32,224]{2,1,0:T(8,128)(2,1)S(1)}, bf16[8,32,224]{2,1,0:T(8,128)(2,1)S(1)}, u32[]{:S(2)}, u32[]{:S(2)}) %collective-permute-start.30) | collective-permute-done | bytes 114720 | tf_op jit(solution)/shard_map/image_backward/ppermute | solution.py:27
  177.2 7.8 %back.1 = (f32[2,2,256,256]{3,2,1,0:T(8,128)}, bf16[2,2,256,256]{3,2,1,0:T(8,128)(2,1)}) custom-call(s32[3]{0:T(128)} %pad_add_fusion.1.ids, bf16[8,32,224]{2,1,0:T(8,128)(2,1)} %bitcast.223, bf16[8,32,224]{2,1,0:T(8,128)(2,1)} %copy-done.21, bf16[8,32,224]{2,1,0:T(8,128)(2,1)} %copy-done.22, bf16[8,32,224]{2,1,0:T(8,128)(2,1)} %copy-done.23, ...), custom_call_target="tpu_custom_call" | custom-call | flops 1761607680 | bytes 29360128 | tf_op jit(solution)/shard_map/image_backward/back/pallas_call | solution.py:220
  201.1 2.7 %collective-permute-start.39 = (bf16[2,128,256]{2,1,0:T(8,128)(2,1)S(1)}, bf16[2,128,256]{2,1,0:T(8,128)(2,1)S(1)}, u32[]{:S(2)}, u32[]{:S(2)}) collective-permute-start(bf16[2,128,256]{2,1,0:T(8,128)(2,1)S(1)} %slice.209), channel_id=1, source_target_pairs={{0,16},{4,20},{8,24},{12,28},{16,0},{20,4},{24,8},{28,12},{1,17},{... | collective-permute-start | bytes 393224 | tf_op jit(solution)/shard_map/image_backward/ppermute | solution.py:27
  206.2 4.3 %collective-permute-done.39 = bf16[2,128,256]{2,1,0:T(8,128)(2,1)S(1)} collective-permute-done((bf16[2,128,256]{2,1,0:T(8,128)(2,1)S(1)}, bf16[2,128,256]{2,1,0:T(8,128)(2,1)S(1)}, u32[]{:S(2)}, u32[]{:S(2)}) %collective-permute-start.39) | collective-permute-done | bytes 131104 | tf_op jit(solution)/shard_map/image_backward/ppermute | solution.py:27
  (255 shorter events, 77.1 us)
Async XLA Ops:
  0.6 18.1 %collective-permute-start.3 = (bf16[128,288]{0,1:T(8,128)(2,1)}, bf16[128,288]{0,1:T(8,128)(2,1)S(1)}, u32[]{:S(2)}, u32[]{:S(2)}) collective-permute-start(bf16[128,288]{0,1:T(8,128)(2,1)} %param.12), channel_id=1, source_target_pairs={{0,2},{1,3},{2,0},{3,1},{4,6},{5,7},{6,4},{7,5},{8,10},{9,11},{10,... | collective-permute-start | bytes 221192 | tf_op jit(solution)/shard_map/first/ppermute | solution.py:27
  3.6 15.2 %collective-permute-start.4 = (bf16[128,288]{0,1:T(8,128)(2,1)}, bf16[128,288]{0,1:T(8,128)(2,1)S(1)}, u32[]{:S(2)}, u32[]{:S(2)}) collective-permute-start(bf16[128,288]{0,1:T(8,128)(2,1)} %param.12), channel_id=1, source_target_pairs={{0,1},{1,0},{2,3},{3,2},{4,5},{5,4},{6,7},{7,6},{8,9},{9,8},{10,11... | collective-permute-start | bytes 221192 | tf_op jit(solution)/shard_map/first/ppermute | solution.py:27
  8.2 36.3 %collective-permute-start.1 = (bf16[2,224,960]{2,1,0:T(8,128)(2,1)S(1)}, bf16[2,224,960]{2,1,0:T(8,128)(2,1)}, u32[]{:S(2)}, u32[]{:S(2)}) collective-permute-start(bf16[2,224,960]{2,1,0:T(8,128)(2,1)S(1)} %dynamic-slice_bitcast_fusion.refs_0_.refs_10_), channel_id=1, source_target_pairs={{0,8},{4,12},{8,0},{12,4},{16,24},{20,28},{24,16},{28,20},{1,9},{5... | collective-permute-start | bytes 2580488 | tf_op jit(solution)/shard_map/first/ppermute | solution.py:27
  9.9 55.0 %collective-permute-start = (bf16[2,224,960]{2,1,0:T(8,128)(2,1)S(1)}, bf16[2,224,960]{2,1,0:T(8,128)(2,1)}, u32[]{:S(2)}, u32[]{:S(2)}) collective-permute-start(bf16[2,224,960]{2,1,0:T(8,128)(2,1)S(1)} %dynamic-slice_bitcast_fusion.refs_0_.refs_10_), channel_id=1, source_target_pairs={{0,4},{4,0},{8,12},{12,8},{16,20},{20,16},{24,28},{28,24},{1,5},{5... | collective-permute-start | bytes 2580488 | tf_op jit(solution)/shard_map/first/ppermute | solution.py:27
  11.4 51.6 %all-to-all-start = ((bf16[2,2,224,960]{3,2,1,0:T(8,128)(2,1)}), bf16[2,2,224,960]{3,2,1,0:T(8,128)(2,1)}, u32[]{:S(2)}, u32[]{:S(2)}) async-start(bf16[2,2,224,960]{3,2,1,0:T(8,128)(2,1)} %pad_maximum_fusion.1), calls=%async_computation | async-start | bytes 3670016 | tf_op jit(solution)/shard_map/first/all_to_all | solution.py:53
  16.1 48.7 %collective-permute-start.9 = (bf16[448,1152]{1,0:T(8,128)(2,1)}, bf16[448,1152]{1,0:T(8,128)(2,1)}, u32[]{:S(2)}, u32[]{:S(2)}) collective-permute-start(bf16[448,1152]{1,0:T(8,128)(2,1)} %param.19), channel_id=1, source_target_pairs={{0,2},{1,3},{2,0},{3,1},{4,6},{5,7},{6,4},{7,5},{8,10},{9,11},{10,... | collective-permute-start | bytes 3096584 | tf_op jit(solution)/shard_map/first/ppermute | solution.py:27
  18.8 114.0 %collective-permute-start.24 = (bf16[448,1152]{1,0:T(8,128)(2,1)}, bf16[448,1152]{1,0:T(8,128)(2,1)}, u32[]{:S(2)}, u32[]{:S(2)}) collective-permute-start(bf16[448,1152]{1,0:T(8,128)(2,1)} %param.19), channel_id=1, source_target_pairs={{0,1},{1,0},{2,3},{3,2},{4,5},{5,4},{6,7},{7,6},{8,9},{9,8},{10,11... | collective-permute-start | bytes 3096584 | tf_op jit(solution)/shard_map/norm/ppermute | solution.py:27
  44.6 23.1 %collective-permute-start.2 = (bf16[2,224,960]{2,1,0:T(8,128)(2,1)}, bf16[2,224,960]{2,1,0:T(8,128)(2,1)}, u32[]{:S(2)}, u32[]{:S(2)}) collective-permute-start(bf16[2,224,960]{2,1,0:T(8,128)(2,1)} %collective-permute-done.1.refs_2_.refs_12_), channel_id=1, source_target_pairs={{0,4},{4,0},{8,12},{12,8},{16,20},{20,16},{24,28},{28,24},{1,5},{5... | collective-permute-start | bytes 2580488 | tf_op jit(solution)/shard_map/first/ppermute | solution.py:27
  51.7 13.2 %collective-permute-start.8 = (bf16[2,128,224]{2,1,0:T(8,128)(2,1)S(1)}, bf16[2,128,224]{2,1,0:T(8,128)(2,1)}, u32[]{:S(2)}, u32[]{:S(2)}) collective-permute-start(bf16[2,128,224]{2,1,0:T(8,128)(2,1)S(1)} %bitcast.216), channel_id=1, source_target_pairs={{0,16},{4,20},{8,24},{12,28},{16,0},{20,4},{24,8},{28,12},{1,17},{... | collective-permute-start | bytes 344072 | tf_op jit(solution)/shard_map/first/ppermute | solution.py:27
  69.3 7.7 %collective-permute-start.14 = (bf16[2,256,224]{2,1,0:T(8,128)(2,1)}, bf16[2,256,224]{2,1,0:T(8,128)(2,1)}, u32[]{:S(2)}, u32[]{:S(2)}) collective-permute-start(bf16[2,256,224]{2,1,0:T(8,128)(2,1)} %pad_maximum_fusion.7.refs_0_), channel_id=1, source_target_pairs={{0,2},{1,3},{2,0},{3,1},{4,6},{5,7},{6,4},{7,5},{8,10},{9,11},{10,... | collective-permute-start | bytes 688136 | tf_op jit(solution)/shard_map/second/ppermute | solution.py:27
  70.9 18.3 %collective-permute-start.10 = (bf16[224,960]{1,0:T(8,128)(2,1)}, bf16[224,960]{1,0:T(8,128)(2,1)S(1)}, u32[]{:S(2)}, u32[]{:S(2)}) collective-permute-start(bf16[224,960]{1,0:T(8,128)(2,1)} %get-tuple-element.48), channel_id=1, source_target_pairs={{0,4},{4,0},{8,12},{12,8},{16,20},{20,16},{24,28},{28,24},{1,5},{5... | collective-permute-start | bytes 1290248 | tf_op jit(solution)/shard_map/second/ppermute | solution.py:27
  72.6 19.7 %collective-permute-start.12 = (bf16[224,960]{1,0:T(8,128)(2,1)}, bf16[224,960]{1,0:T(8,128)(2,1)S(1)}, u32[]{:S(2)}, u32[]{:S(2)}) collective-permute-start(bf16[224,960]{1,0:T(8,128)(2,1)} %get-tuple-element.48), channel_id=1, source_target_pairs={{0,8},{4,12},{8,0},{12,4},{16,24},{20,28},{24,16},{28,20},{1,9},{5... | collective-permute-start | bytes 1290248 | tf_op jit(solution)/shard_map/second/ppermute | solution.py:27
  72.6 19.7 %collective-permute-start.11 = (bf16[224,960]{1,0:T(8,128)(2,1)}, bf16[224,960]{1,0:T(8,128)(2,1)}, u32[]{:S(2)}, u32[]{:S(2)}) collective-permute-start(bf16[224,960]{1,0:T(8,128)(2,1)} %get-tuple-element.49), channel_id=1, source_target_pairs={{0,4},{4,0},{8,12},{12,8},{16,20},{20,16},{24,28},{28,24},{1,5},{5... | collective-permute-start | bytes 1290248 | tf_op jit(solution)/shard_map/second/ppermute | solution.py:27
  77.0 19.6 %collective-permute-start.13 = (bf16[224,960]{1,0:T(8,128)(2,1)}, bf16[224,960]{1,0:T(8,128)(2,1)}, u32[]{:S(2)}, u32[]{:S(2)}) collective-permute-start(bf16[224,960]{1,0:T(8,128)(2,1)} %get-tuple-element.49), channel_id=1, source_target_pairs={{0,8},{4,12},{8,0},{12,4},{16,24},{20,28},{24,16},{28,20},{1,9},{5... | collective-permute-start | bytes 1290248 | tf_op jit(solution)/shard_map/second/ppermute | solution.py:27
  78.0 21.8 %all-to-all-start.1 = ((bf16[4,32,1152]{2,1,0:T(8,128)(2,1)}), bf16[4,32,1152]{2,1,0:T(8,128)(2,1)}, u32[]{:S(2)}, u32[]{:S(2)}) async-start(bf16[4,32,1152]{2,1,0:T(8,128)(2,1)} %broadcast_in_dim.83), calls=%async_computation.1 | async-start | bytes 589824 | tf_op jit(solution)/shard_map/third/all_to_all | solution.py:372
  96.6 6.8 %collective-permute-start.16 = (bf16[2,256,224]{2,1,0:T(8,128)(2,1)}, bf16[2,256,224]{2,1,0:T(8,128)(2,1)}, u32[]{:S(2)}, u32[]{:S(2)}) collective-permute-start(bf16[2,256,224]{2,1,0:T(8,128)(2,1)} %collective-permute-done.14.refs_1_), channel_id=1, source_target_pairs={{0,1},{1,0},{2,3},{3,2},{4,5},{5,4},{6,7},{7,6},{8,9},{9,8},{10,11... | collective-permute-start | bytes 688136 | tf_op jit(solution)/shard_map/second/ppermute | solution.py:27
  99.8 14.2 %collective-permute-start.17 = (bf16[4,32,1152]{2,1,0:T(8,128)(2,1)}, bf16[4,32,1152]{2,1,0:T(8,128)(2,1)}, u32[]{:S(2)}, u32[]{:S(2)}) collective-permute-start(bf16[4,32,1152]{2,1,0:T(8,128)(2,1)} %all-to-all-done.1), channel_id=1, source_target_pairs={{0,4},{4,0},{8,12},{12,8},{16,20},{20,16},{24,28},{28,24},{1,5},{5... | collective-permute-start | bytes 884744 | tf_op jit(solution)/shard_map/third/ppermute | solution.py:27
  101.8 39.2 %collective-permute-start.25 = (bf16[448,1152]{1,0:T(8,128)(2,1)}, bf16[448,1152]{1,0:T(8,128)(2,1)}, u32[]{:S(2)}, u32[]{:S(2)}) collective-permute-start(bf16[448,1152]{1,0:T(8,128)(2,1)} %collective-permute-done.9), channel_id=1, source_target_pairs={{0,1},{1,0},{2,3},{3,2},{4,5},{5,4},{6,7},{7,6},{8,9},{9,8},{10,11... | collective-permute-start | bytes 3096584 | tf_op jit(solution)/shard_map/norm/ppermute | solution.py:27
  101.9 15.4 %collective-permute-start.18 = (bf16[224,960]{1,0:T(8,128)(2,1)S(1)}, bf16[224,960]{1,0:T(8,128)(2,1)S(1)}, u32[]{:S(2)}, u32[]{:S(2)}) collective-permute-start(bf16[224,960]{1,0:T(8,128)(2,1)S(1)} %collective-permute-done.12.refs_6_.refs_7_.refs_8_.refs_9_.refs_10_.refs_16_), channel_id=1, source_target_pairs={{0,4},{4,0},{8,12},{12,8},{16,20},{20,16},{24,28},{28,24},{1,5},{5... | collective-permute-start | bytes 1290248 | tf_op jit(solution)/shard_map/third/ppermute | solution.py:27
  103.4 13.9 %collective-permute-start.19 = (bf16[224,960]{1,0:T(8,128)(2,1)}, bf16[224,960]{1,0:T(8,128)(2,1)S(1)}, u32[]{:S(2)}, u32[]{:S(2)}) collective-permute-start(bf16[224,960]{1,0:T(8,128)(2,1)} %collective-permute-done.11.refs_8_.refs_18_), channel_id=1, source_target_pairs={{0,8},{4,12},{8,0},{12,4},{16,24},{20,28},{24,16},{28,20},{1,9},{5... | collective-permute-start | bytes 1290248 | tf_op jit(solution)/shard_map/third/ppermute | solution.py:27
  115.9 15.4 %collective-permute-start.21 = (bf16[256,1152]{1,0:T(8,128)(2,1)}, bf16[256,1152]{1,0:T(8,128)(2,1)}, u32[]{:S(2)}, u32[]{:S(2)}) collective-permute-start(bf16[256,1152]{1,0:T(8,128)(2,1)} %bitcast.30), channel_id=1, source_target_pairs={{0,2},{1,3},{2,0},{3,1},{4,6},{5,7},{6,4},{7,5},{8,10},{9,11},{10,... | collective-permute-start | bytes 1769480 | tf_op jit(solution)/shard_map/norm/ppermute | solution.py:27
  131.4 7.2 %collective-permute-start.22 = (bf16[8,2,32,224]{3,2,0,1:T(8,128)(2,1)S(1)}, bf16[8,2,32,224]{3,2,0,1:T(8,128)(2,1)S(1)}, u32[]{:S(2)}, u32[]{:S(2)}) collective-permute-start(bf16[8,2,32,224]{3,2,0,1:T(8,128)(2,1)S(1)} %fusion.42), channel_id=1, source_target_pairs={{0,2},{1,3},{2,0},{3,1},{4,6},{5,7},{6,4},{7,5},{8,10},{9,11},{10,... | collective-permute-start | bytes 688136 | tf_op jit(solution)/shard_map/image_forward/ppermute | solution.py:27
  135.0 17.4 %collective-permute-start.27 = (bf16[256,1152]{1,0:T(8,128)(2,1)}, bf16[256,1152]{1,0:T(8,128)(2,1)S(1)}, u32[]{:S(2)}, u32[]{:S(2)}) collective-permute-start(bf16[256,1152]{1,0:T(8,128)(2,1)} %bitcast.30), channel_id=1, source_target_pairs={{0,1},{1,0},{2,3},{3,2},{4,5},{5,4},{6,7},{7,6},{8,9},{9,8},{10,11... | collective-permute-start | bytes 1769480 | tf_op jit(solution)/shard_map/norm/ppermute | solution.py:27
  138.7 8.7 %collective-permute-start.23 = (bf16[8,32,224]{2,1,0:T(8,128)(2,1)S(1)}, bf16[8,32,224]{2,1,0:T(8,128)(2,1)S(1)}, u32[]{:S(2)}, u32[]{:S(2)}) collective-permute-start(bf16[8,32,224]{2,1,0:T(8,128)(2,1)S(1)} %fusion.68), channel_id=1, source_target_pairs={{0,16},{4,20},{8,24},{12,28},{16,0},{20,4},{24,8},{28,12},{1,17},{... | collective-permute-start | bytes 344072 | tf_op jit(solution)/shard_map/image_forward/ppermute | solution.py:27
  143.3 9.2 %collective-permute-start.28 = (bf16[256,1152]{1,0:T(8,128)(2,1)}, bf16[256,1152]{1,0:T(8,128)(2,1)S(1)}, u32[]{:S(2)}, u32[]{:S(2)}) collective-permute-start(bf16[256,1152]{1,0:T(8,128)(2,1)} %collective-permute-done.21), channel_id=1, source_target_pairs={{0,1},{1,0},{2,3},{3,2},{4,5},{5,4},{6,7},{7,6},{8,9},{9,8},{10,11... | collective-permute-start | bytes 1769480 | tf_op jit(solution)/shard_map/norm/ppermute | solution.py:27
  159.4 9.7 %collective-permute-start.33 = (bf16[8,32,224]{2,1,0:T(8,128)(2,1)S(1)}, bf16[8,32,224]{2,1,0:T(8,128)(2,1)S(1)}, u32[]{:S(2)}, u32[]{:S(2)}) collective-permute-start(bf16[8,32,224]{2,1,0:T(8,128)(2,1)S(1)} %bitcast.220), channel_id=1, source_target_pairs={{0,16},{4,20},{8,24},{12,28},{16,0},{20,4},{24,8},{28,12},{1,17},{... | collective-permute-start | bytes 344072 | tf_op jit(solution)/shard_map/image_backward/ppermute | solution.py:27
  162.4 24.8 %all-to-all-start.2 = ((bf16[8,32,1152]{2,1,0:T(8,128)(2,1)}), bf16[8,32,1152]{2,1,0:T(8,128)(2,1)S(1)}, u32[]{:S(2)}, u32[]{:S(2)}) async-start(bf16[8,32,1152]{2,1,0:T(8,128)(2,1)} %bitcast.47), calls=%async_computation.2 | async-start | bytes 1179648 | tf_op jit(solution)/shard_map/text_loss/all_to_all | solution.py:444
  167.1 6.2 %collective-permute-start.30 = (bf16[8,32,224]{2,1,0:T(8,128)(2,1)S(1)}, bf16[8,32,224]{2,1,0:T(8,128)(2,1)S(1)}, u32[]{:S(2)}, u32[]{:S(2)}) collective-permute-start(bf16[8,32,224]{2,1,0:T(8,128)(2,1)S(1)} %bitcast.221), channel_id=1, source_target_pairs={{0,2},{1,3},{2,0},{3,1},{4,6},{5,7},{6,4},{7,5},{8,10},{9,11},{10,... | collective-permute-start | bytes 344072 | tf_op jit(solution)/shard_map/image_backward/ppermute | solution.py:27
  169.1 6.1 %collective-permute-start.34 = (bf16[8,32,224]{2,1,0:T(8,128)(2,1)S(1)}, bf16[8,32,224]{2,1,0:T(8,128)(2,1)S(1)}, u32[]{:S(2)}, u32[]{:S(2)}) collective-permute-start(bf16[8,32,224]{2,1,0:T(8,128)(2,1)S(1)} %collective-permute-done.33.refs_4_), channel_id=1, source_target_pairs={{0,2},{1,3},{2,0},{3,1},{4,6},{5,7},{6,4},{7,5},{8,10},{9,11},{10,... | collective-permute-start | bytes 344072 | tf_op jit(solution)/shard_map/image_backward/ppermute | solution.py:27
  190.9 9.0 %collective-permute-start.38 = (bf16[2,256,256]{2,1,0:T(8,128)(2,1)}, bf16[2,256,256]{2,1,0:T(8,128)(2,1)}, u32[]{:S(2)}, u32[]{:S(2)}) collective-permute-start(bf16[2,256,256]{2,1,0:T(8,128)(2,1)} %fusion.41), channel_id=1, source_target_pairs={{0,2},{1,3},{2,0},{3,1},{4,6},{5,7},{6,4},{7,5},{8,10},{9,11},{10,... | collective-permute-start | bytes 786440 | tf_op jit(solution)/shard_map/image_backward/ppermute | solution.py:27
  201.1 9.5 %collective-permute-start.39 = (bf16[2,128,256]{2,1,0:T(8,128)(2,1)S(1)}, bf16[2,128,256]{2,1,0:T(8,128)(2,1)S(1)}, u32[]{:S(2)}, u32[]{:S(2)}) collective-permute-start(bf16[2,128,256]{2,1,0:T(8,128)(2,1)S(1)} %slice.209), channel_id=1, source_target_pairs={{0,16},{4,20},{8,24},{12,28},{16,0},{20,4},{24,8},{28,12},{1,17},{... | collective-permute-start | bytes 393224 | tf_op jit(solution)/shard_map/image_backward/ppermute | solution.py:27
  205.0 7.7 %collective-permute-start.43 = (bf16[1,128,292]{1,2,0:T(8,128)(2,1)S(1)}, bf16[1,128,292]{1,2,0:T(8,128)(2,1)S(1)}, u32[]{:S(2)}, u32[]{:S(2)}) collective-permute-start(bf16[1,128,292]{1,2,0:T(8,128)(2,1)S(1)} %maximum_bitcast_fusion), channel_id=1, source_target_pairs={{0,2},{1,3},{2,0},{3,1},{4,6},{5,7},{6,4},{7,5},{8,10},{9,11},{10,... | collective-permute-start | bytes 224264 | tf_op jit(solution)/shard_map/text_backward/ppermute | solution.py:27
  (55 other events, 369.9 us)

commit v6 on v5

--- a/solution.py
+++ b/solution.py
@@ -20,7 +20,7 @@
 SLOTS = (0, 1, 2, 4, 3, 5, 6, 7)
 PAIRED = 5
 MEBIBYTES = {"norm": 12, "up": 18, "forward": 28, "back": 28}
-PARAMS = pltpu.CompilerParams(vmem_limit_bytes=60 * 1024 * 1024)
+PARAMS = pltpu.CompilerParams(vmem_limit_bytes=63 * 1024 * 1024)
 
 
 def swap(value, axis, flip):
@@ -332,11 +332,11 @@
         gain = image_gain.reshape(members, 1, width)
         text_gains = jnp.sum(text_up.astype(F32) * text_gain[:, None], axis=0)
         own_gain = lax.dynamic_slice_in_dim(text_gain, grp * text_cols, text_cols, 0)
-        ready = (ids, gain, text_gains, own_gain)
+        ready = (ids, gain, text_gains, own_gain, scale, shift)
         far, near_y, near_z, near_last, total, far_in, head_x, ready = gate(
             (far, near_y, near_z, near_last, total, far_in, head_x, ready)
         )
-        ids, gain, text_gains, own_gain = ready
+        ids, gain, text_gains, own_gain, scale, shift = ready
 
     with jax.named_scope("second"):
         far_parts, total = gate(([far[0], far[1]], total))
@@ -496,7 +496,7 @@
         own_grad = place(own_grad, grp, FLIPS).transpose(1, 0, 2, 3)
         own_grad = own_grad.reshape(share_count, rows, width)
         image_grad = (own_grad.astype(F32) + back).astype(BF16)
-        image_grad = image_grad.transpose(1, 0, 2).reshape(rows, image_cols)
+        image_grad = jnp.concatenate([image_grad[at] for at in range(share_count)], 1)
 
     with jax.named_scope("text_sum"):
         grad_text_unit = jnp.sum(text_parts.astype(F32), axis=0)

time: 216 us -> 207 us (0.958)
  other arithmetic: 20.3 us -> 14.4 us
  matrix products: 15.9 us -> 13.7 us
    dynamic_update_slice x15, local copies, waits for them, and re-layouts: 12.4 us -> 15.5 us  [place(): whole = lax.dynamic_update_index_in_dim(whole, part, index ^ flip, 0)]
    add x2, other arithmetic: 2.73 us -> 0.09 us  [shards(): total = take(total, x) + swap(send, 'grp', 2).astype(F32)]
    ppermute x44, waiting for transfers between devices: 58.2 us -> 55.8 us  [swap(): lax.ppermute(value, axis, [(i, i ^ flip) for i in range(lax.axis_size(axi...]
    dot_general x11, matrix products: 15.9 us -> 13.7 us  [dot(): return lax.dot_general(left, right, dims, preferred_element_type=F32)]
    unnamed x83 -> x76, local copies, waits for them, and re-layouts: 5.79 us -> 6.02 us
  transfers between devices with their start and end apart: 47 -> 47, of which waited for: 21 -> 21; matrix products, arithmetic and copies ran while one was open for 28% -> 25% of each run, Pallas kernels for 11% -> 12%
where the time goes in v6:
time: 207 us; the launch traced here: 206 us
  waiting for transfers between devices  67.1 us (32%)
  starting transfers between devices  51.7 us (25%)
  local copies, waits for them, and re-layouts  32 us (15%)
  Pallas kernels  24.2 us (12%)
  other arithmetic  14.4 us (7%)
  matrix products  13.7 us (7%)
  between operations  2.91 us (1%)
    ppermute x44, waiting for transfers between devices, swap(): lax.ppermute(value, axis, [(i, i ^ flip) for i in range(lax.axis_size(axi...  55.8 us
    ppermute x44, starting transfers between devices, swap(): lax.ppermute(value, axis, [(i, i ^ flip) for i in range(lax.axis_size(axi...  36.6 us
    pallas_call x4, Pallas kernels, call(): pl.pallas_call(kernel, out_shape=shapes, in_specs=[SMEM] + [VMEM] * (len(...  24.2 us
    dynamic_update_slice x15, local copies, waits for them, and re-layouts, place(): whole = lax.dynamic_update_index_in_dim(whole, part, index ^ flip, 0)  15.5 us
    dot_general x11, matrix products, dot(): return lax.dot_general(left, right, dims, preferred_element_type=F32)  13.7 us
    all_to_all x1, waiting for transfers between devices, exchange(): lax.all_to_all(halves, 'img', split_axis=0, concat_axis=0, tiled=True, ax...  8.84 us
    unnamed x76, local copies, waits for them, and re-layouts  6.02 us
    all_to_all x1, starting transfers between devices, shards(): lax.all_to_all(copies, 'img', split_axis=0, concat_axis=0, tiled=True, ax...  5.91 us
  transfers between devices with their start and end apart: 47, of which 21 were waited for; matrix products, arithmetic and copies ran while one was open for 25% of the time, Pallas kernels for 12%

profile of v6, /device:TPU:0, one launch (start us, length us, event | category | flops | bytes accessed | tf_op | source)
XLA Modules:
  0.0 206.0 jit_solution(13729079023316265758)
XLA Ops:
  0.6 3.0 %collective-permute-start.3 = (bf16[128,288]{0,1:T(8,128)(2,1)}, bf16[128,288]{0,1:T(8,128)(2,1)}, u32[]{:S(2)}, u32[]{:S(2)}) collective-permute-start(bf16[128,288]{0,1:T(8,128)(2,1)} %param.12), channel_id=1, source_target_pairs={{0,2},{1,3},{2,0},{3,1},{4,6},{5,7},{6,4},{7,5},{8,10},{9,11},{10,... | collective-permute-start | bytes 221192 | tf_op jit(solution)/shard_map/first/ppermute | solution.py:27
  10.2 4.7 %all-to-all-start = ((bf16[2,2,224,960]{3,2,1,0:T(8,128)(2,1)}), bf16[2,2,224,960]{3,2,1,0:T(8,128)(2,1)}, u32[]{:S(2)}, u32[]{:S(2)}) async-start(bf16[2,2,224,960]{3,2,1,0:T(8,128)(2,1)} %copy-done.4), calls=%async_computation | async-start | bytes 3670016 | tf_op jit(solution)/shard_map/first/all_to_all | solution.py:53
  29.0 14.3 %collective-permute-done.1.refs_2_.refs_12_ = bf16[2,224,960]{2,1,0:T(8,128)(2,1)S(1)} collective-permute-done((bf16[2,224,960]{2,1,0:T(8,128)(2,1)S(1)}, bf16[2,224,960]{2,1,0:T(8,128)(2,1)S(1)}, u32[]{:S(2)}, u32[]{:S(2)}) %collective-permute-start.1) | collective-permute-done | bytes 860192 | tf_op jit(solution)/shard_map/first/ppermute | solution.py:27
  43.3 2.5 %collective-permute-start.2 = (bf16[2,224,960]{2,1,0:T(8,128)(2,1)S(1)}, bf16[2,224,960]{2,1,0:T(8,128)(2,1)}, u32[]{:S(2)}, u32[]{:S(2)}) collective-permute-start(bf16[2,224,960]{2,1,0:T(8,128)(2,1)S(1)} %collective-permute-done.1.refs_2_.refs_12_), channel_id=1, source_target_pairs={{0,4},{4,0},{8,12},{12,8},{16,20},{20,16},{24,28},{28,24},{1,5},{5... | collective-permute-start | bytes 2580488 | tf_op jit(solution)/shard_map/first/ppermute | solution.py:27
  47.9 2.3 %collective-permute-done.7 = bf16[32,1152]{1,0:T(8,128)(2,1)S(1)} collective-permute-done((bf16[32,1152]{1,0:T(8,128)(2,1)S(1)}, bf16[32,1152]{1,0:T(8,128)(2,1)S(1)}, u32[]{:S(2)}, u32[]{:S(2)}) %collective-permute-start.7) | collective-permute-done | bytes 73760 | tf_op jit(solution)/shard_map/first/ppermute | solution.py:27
  50.2 2.7 %collective-permute-start.8 = (bf16[2,128,224]{2,1,0:T(8,128)(2,1)S(1)}, bf16[2,128,224]{2,1,0:T(8,128)(2,1)S(1)}, u32[]{:S(2)}, u32[]{:S(2)}) collective-permute-start(bf16[2,128,224]{2,1,0:T(8,128)(2,1)S(1)} %bitcast.218), channel_id=1, source_target_pairs={{0,16},{4,20},{8,24},{12,28},{16,0},{20,4},{24,8},{28,12},{1,17},{... | collective-permute-start | bytes 344072 | tf_op jit(solution)/shard_map/first/ppermute | solution.py:27
  53.0 8.8 %all-to-all-done = bf16[2,2,224,960]{3,2,1,0:T(8,128)(2,1)} async-done(((bf16[2,2,224,960]{3,2,1,0:T(8,128)(2,1)}), bf16[2,2,224,960]{3,2,1,0:T(8,128)(2,1)}, u32[]{:S(2)}, u32[]{:S(2)}) %all-to-all-start) | async-done | bytes 1720352 | tf_op jit(solution)/shard_map/first/all_to_all | solution.py:53
  63.6 2.7 %collective-permute-done.2.refs_4_.refs_14_ = bf16[2,224,960]{2,1,0:T(8,128)(2,1)} collective-permute-done((bf16[2,224,960]{2,1,0:T(8,128)(2,1)S(1)}, bf16[2,224,960]{2,1,0:T(8,128)(2,1)}, u32[]{:S(2)}, u32[]{:S(2)}) %collective-permute-start.2) | collective-permute-done | bytes 860192 | tf_op jit(solution)/shard_map/first/ppermute | solution.py:27
  70.0 4.8 %collective-permute-done.14.refs_1_ = bf16[2,256,224]{2,1,0:T(8,128)(2,1)S(1)} collective-permute-done((bf16[2,256,224]{2,1,0:T(8,128)(2,1)S(1)}, bf16[2,256,224]{2,1,0:T(8,128)(2,1)S(1)}, u32[]{:S(2)}, u32[]{:S(2)}) %collective-permute-start.14) | collective-permute-done | bytes 229408 | tf_op jit(solution)/shard_map/second/ppermute | solution.py:27
  76.3 5.9 %all-to-all-start.1 = ((bf16[4,32,1152]{2,1,0:T(8,128)(2,1)}), bf16[4,32,1152]{2,1,0:T(8,128)(2,1)}, u32[]{:S(2)}, u32[]{:S(2)}) async-start(bf16[4,32,1152]{2,1,0:T(8,128)(2,1)} %broadcast_in_dim.83), calls=%async_computation.1 | async-start | bytes 589824 | tf_op jit(solution)/shard_map/third/all_to_all | solution.py:372
  82.3 2.3 %broadcast_in_dim.84 = bf16[4,448,1152]{2,1,0:T(8,128)(2,1)} broadcast(bf16[]{:T(256)} %constant.207.clone.1), dimensions={} | broadcast | bytes 4128770 | tf_op jit(solution)/shard_map/norm/broadcast_in_dim | solution.py:31
  85.6 3.7 %collective-permute-done.11.refs_8_.refs_18_ = bf16[224,960]{1,0:T(8,128)(2,1)} collective-permute-done((bf16[224,960]{1,0:T(8,128)(2,1)S(1)}, bf16[224,960]{1,0:T(8,128)(2,1)}, u32[]{:S(2)}, u32[]{:S(2)}) %collective-permute-start.11) | collective-permute-done | bytes 430112 | tf_op jit(solution)/shard_map/second/ppermute | solution.py:27
  89.3 4.3 %collective-permute-done.13.refs_9_.refs_19_ = bf16[224,960]{1,0:T(8,128)(2,1)} collective-permute-done((bf16[224,960]{1,0:T(8,128)(2,1)S(1)}, bf16[224,960]{1,0:T(8,128)(2,1)}, u32[]{:S(2)}, u32[]{:S(2)}) %collective-permute-start.13) | collective-permute-done | bytes 430112 | tf_op jit(solution)/shard_map/second/ppermute | solution.py:27
  94.1 2.5 %all-to-all-done.1 = bf16[4,32,1152]{2,1,0:T(8,128)(2,1)} async-done(((bf16[4,32,1152]{2,1,0:T(8,128)(2,1)}), bf16[4,32,1152]{2,1,0:T(8,128)(2,1)}, u32[]{:S(2)}, u32[]{:S(2)}) %all-to-all-start.1) | async-done | bytes 294944 | tf_op jit(solution)/shard_map/third/all_to_all | solution.py:372
  100.3 2.1 %collective-permute-start.19 = (bf16[224,960]{1,0:T(8,128)(2,1)}, bf16[224,960]{1,0:T(8,128)(2,1)}, u32[]{:S(2)}, u32[]{:S(2)}) collective-permute-start(bf16[224,960]{1,0:T(8,128)(2,1)} %collective-permute-done.11.refs_8_.refs_18_), channel_id=1, source_target_pairs={{0,8},{4,12},{8,0},{12,4},{16,24},{20,28},{24,16},{28,20},{1,9},{5... | collective-permute-start | bytes 1290248 | tf_op jit(solution)/shard_map/third/ppermute | solution.py:27
  102.4 3.4 %norm.1 = (bf16[8,272,224]{2,1,0:T(8,128)(2,1)}, bf16[8,32,224]{2,1,0:T(8,128)(2,1)}, f32[256,1]{1,0:T(8,128)}, f32[256,1]{1,0:T(8,128)}) custom-call(s32[3]{0:T(128)} %pad_add_fusion.1.ids, bf16[2,256,224]{2,1,0:T(8,128)(2,1)} %copy-done.15, bf16[2,256,224]{2,1,0:T(8,128)(2,1)} %copy-done.20, bf16[2,256,224]{2,1,0:T(8,128)(2,1)} %copy-done.22, ...), custom_call_target="tpu_custom_call" | custom-call | bytes 12582912 | tf_op jit(solution)/shard_map/second/norm/pallas_call | solution.py:220
  105.8 5.0 %up.1.partial = f32[272,960]{1,0:T(8,128)} custom-call(s32[3]{0:T(128)} %pad_add_fusion.1.ids, bf16[8,272,224]{2,1,0:T(8,128)(2,1)} %get-tuple-element.58.scaled, bf16[2,224,960]{2,1,0:T(8,128)(2,1)} %copy-done.1, bf16[2,224,960]{2,1,0:T(8,128)(2,1)} %collective-permute-done.refs_1_.refs_11_, bf16[2,224,960]{2,1,0:T(8,128)(2,1)} %copy-done.5, ...), custom_call_target="tpu_custom_call" | custom-call | flops 1761607680 | bytes 18874368 | tf_op jit(solution)/shard_map/image_forward/up/pallas_call | solution.py:220
  113.6 8.0 %forward.1 = (f32[256,960]{1,0:T(8,128)}, f32[1,960]{1,0:T(1,128)}, f32[8,4,32,224]{3,2,1,0:T(8,128)}, bf16[8,4,32,224]{3,2,1,0:T(8,128)(2,1)}) custom-call(s32[3]{0:T(128)} %pad_add_fusion.1.ids, bf16[8,272,224]{2,1,0:T(8,128)(2,1)} %get-tuple-element.58.scaled, f32[272,960]{1,0:T(8,128)} %up.1.partial, bf16[2,224,960]{2,1,0:T(8,128)(2,1)} %copy-done.1, ...), custom_call_target="tpu_custom_call" | custom-call | flops 1761607680 | bytes 29360128 | tf_op jit(solution)/shard_map/image_forward/forward/pallas_call | solution.py:220
  121.7 2.4 %bitcast_dynamic-update-slice_fusion.2 = bf16[4,448,1152]{2,1,0:T(8,128)(2,1)} fusion(bf16[4,448,1152]{2,1,0:T(8,128)(2,1)} %bitcast_dynamic-update-slice_fusion.3, s32[]{:T(128)S(6)} %select_n.145, bf16[448,1152]{1,0:T(8,128)(2,1)} %collective-permute-done.9), kind=kLoop, calls=%fused_computation.14 | loop fusion | bytes 2064388 | tf_op jit(solution)/shard_map/norm/jit(dynamic_update_index_in_dim)/dynamic_update_slice | solution.py:33
  124.3 3.0 %collective-permute-done.21 = bf16[256,1152]{1,0:T(8,128)(2,1)} collective-permute-done((bf16[256,1152]{1,0:T(8,128)(2,1)S(1)}, bf16[256,1152]{1,0:T(8,128)(2,1)}, u32[]{:S(2)}, u32[]{:S(2)}) %collective-permute-start.21) | collective-permute-done | bytes 589856 | tf_op jit(solution)/shard_map/norm/ppermute | solution.py:27
  128.7 2.3 %bitcast_dynamic-update-slice_fusion.1 = bf16[4,448,1152]{2,1,0:T(8,128)(2,1)} fusion(bf16[4,448,1152]{2,1,0:T(8,128)(2,1)} %bitcast_dynamic-update-slice_fusion.2, s32[]{:T(128)S(6)} %select_n.146, bf16[448,1152]{1,0:T(8,128)(2,1)} %collective-permute-done.24), kind=kLoop, calls=%fused_computation.13 | loop fusion | bytes 2064388 | tf_op jit(solution)/shard_map/norm/jit(dynamic_update_index_in_dim)/dynamic_update_slice | solution.py:33
  131.0 3.5 %collective-permute-done.22 = bf16[8,2,32,224]{3,2,0,1:T(8,128)(2,1)S(1)} collective-permute-done((bf16[8,2,32,224]{3,2,0,1:T(8,128)(2,1)S(1)}, bf16[8,2,32,224]{3,2,0,1:T(8,128)(2,1)S(1)}, u32[]{:S(2)}, u32[]{:S(2)}) %collective-permute-start.22) | collective-permute-done | bytes 229408 | tf_op jit(solution)/shard_map/image_forward/ppermute | solution.py:27
  136.4 2.3 %bitcast_dynamic-update-slice_fusion = bf16[4,448,1152]{2,1,0:T(8,128)(2,1)} fusion(bf16[4,448,1152]{2,1,0:T(8,128)(2,1)} %bitcast_dynamic-update-slice_fusion.1, s32[]{:T(128)S(6)} %select_n.147, bf16[448,1152]{1,0:T(8,128)(2,1)} %collective-permute-done.25), kind=kLoop, calls=%fused_computation.12 | loop fusion | bytes 2064388 | tf_op jit(solution)/shard_map/norm/jit(dynamic_update_index_in_dim)/dynamic_update_slice | solution.py:33
  138.7 4.5 %collective-permute-done.23 = bf16[8,32,224]{2,1,0:T(8,128)(2,1)S(1)} collective-permute-done((bf16[8,32,224]{2,1,0:T(8,128)(2,1)S(1)}, bf16[8,32,224]{2,1,0:T(8,128)(2,1)S(1)}, u32[]{:S(2)}, u32[]{:S(2)}) %collective-permute-start.23) | collective-permute-done | bytes 114720 | tf_op jit(solution)/shard_map/image_forward/ppermute | solution.py:27
  143.5 3.1 %multiply_reduce_fusion.4 = (f32[32]{0:T(128)S(1)}, f32[32,1152]{1,0:T(8,128)S(1)}) fusion(bf16[32,1792]{1,0:T(8,128)(2,1)S(1)} %reshape.153, bf16[1792,1152]{1,0:T(8,128)(2,1)} %bitcast.42), kind=kOutput, calls=%fused_computation.111 | convolution fusion | flops 132194272 | bytes 4391040 | tf_op jit(solution)/shard_map/image_forward/dot_general | solution.py:43
  148.2 2.6 %multiply_reduce_fusion.3 = (f32[32]{0:T(128)S(1)}, f32[32,1152]{1,0:T(8,128)S(1)}) fusion(f32[32,1152]{1,0:T(8,128)S(1)} %get-tuple-element.128, f32[]{:T(128)} %bitcast.23, bf16[256,1152]{1,0:T(8,128)(2,1)S(1)} %collective-permute-done.28, bf16[256,1152]{1,0:T(8,128)(2,1)S(1)} %collective-permute-done.27, bf16[256,1152]{1,0:T(8,128)(2,1)} %collective-permute-done.21, ...), kind=kOutput, calls=%fused_computation.109 | convolution fusion | flops 170348512 | bytes 2658696 | tf_op jit(solution)/shard_map/image_loss/dot_general | solution.py:43
  151.2 3.4 %convolution_convert_fusion = bf16[32,1792]{1,0:T(8,128)(2,1)S(1)} fusion(bf16[32,1152]{1,0:T(8,128)(2,1)S(1)} %multiply_convert_fusion.6, bf16[1792,1152]{1,0:T(8,128)(2,1)} %bitcast.42), kind=kOutput, calls=%fused_computation.2 | convolution fusion | flops 132177920 | bytes 4317184 | tf_op jit(solution)/shard_map/image_loss/dot_general | solution.py:43
  156.8 4.5 %all-to-all-start.2 = ((bf16[8,32,1152]{2,1,0:T(8,128)(2,1)}), bf16[8,32,1152]{2,1,0:T(8,128)(2,1)S(1)}, u32[]{:S(2)}, u32[]{:S(2)}) async-start(bf16[8,32,1152]{2,1,0:T(8,128)(2,1)} %bitcast.47), calls=%async_computation.2 | async-start | bytes 1179648 | tf_op jit(solution)/shard_map/text_loss/all_to_all | solution.py:444
  167.2 2.9 %collective-permute-done.34.refs_5_ = bf16[8,32,224]{2,1,0:T(8,128)(2,1)S(1)} collective-permute-done((bf16[8,32,224]{2,1,0:T(8,128)(2,1)S(1)}, bf16[8,32,224]{2,1,0:T(8,128)(2,1)S(1)}, u32[]{:S(2)}, u32[]{:S(2)}) %collective-permute-start.34) | collective-permute-done | bytes 114720 | tf_op jit(solution)/shard_map/image_backward/ppermute | solution.py:27
  172.1 7.8 %back.1 = (f32[2,2,256,256]{3,2,1,0:T(8,128)}, bf16[2,2,256,256]{3,2,1,0:T(8,128)(2,1)}) custom-call(s32[3]{0:T(128)} %pad_add_fusion.1.ids, bf16[8,32,224]{2,1,0:T(8,128)(2,1)} %bitcast.225, bf16[8,32,224]{2,1,0:T(8,128)(2,1)} %copy-done.24, bf16[8,32,224]{2,1,0:T(8,128)(2,1)} %copy-done.25, bf16[8,32,224]{2,1,0:T(8,128)(2,1)} %copy-done.26, ...), custom_call_target="tpu_custom_call" | custom-call | flops 1761607680 | bytes 29360128 | tf_op jit(solution)/shard_map/image_backward/back/pallas_call | solution.py:220
  195.0 2.1 %collective-permute-start.39 = (bf16[2,128,256]{2,1,0:T(8,128)(2,1)S(1)}, bf16[2,128,256]{2,1,0:T(8,128)(2,1)S(1)}, u32[]{:S(2)}, u32[]{:S(2)}) collective-permute-start(bf16[2,128,256]{2,1,0:T(8,128)(2,1)S(1)} %slice.221), channel_id=1, source_target_pairs={{0,16},{4,20},{8,24},{12,28},{16,0},{20,4},{24,8},{28,12},{1,17},{... | collective-permute-start | bytes 393224 | tf_op jit(solution)/shard_map/image_backward/ppermute | solution.py:27
  199.7 4.0 %collective-permute-done.39 = bf16[2,128,256]{2,1,0:T(8,128)(2,1)S(1)} collective-permute-done((bf16[2,128,256]{2,1,0:T(8,128)(2,1)S(1)}, bf16[2,128,256]{2,1,0:T(8,128)(2,1)S(1)}, u32[]{:S(2)}, u32[]{:S(2)}) %collective-permute-start.39) | collective-permute-done | bytes 131104 | tf_op jit(solution)/shard_map/image_backward/ppermute | solution.py:27
  (249 shorter events, 71.7 us)
Async XLA Ops:
  0.6 16.7 %collective-permute-start.3 = (bf16[128,288]{0,1:T(8,128)(2,1)}, bf16[128,288]{0,1:T(8,128)(2,1)}, u32[]{:S(2)}, u32[]{:S(2)}) collective-permute-start(bf16[128,288]{0,1:T(8,128)(2,1)} %param.12), channel_id=1, source_target_pairs={{0,2},{1,3},{2,0},{3,1},{4,6},{5,7},{6,4},{7,5},{8,10},{9,11},{10,... | collective-permute-start | bytes 221192 | tf_op jit(solution)/shard_map/first/ppermute | solution.py:27
  3.6 15.4 %collective-permute-start.4 = (bf16[128,288]{0,1:T(8,128)(2,1)}, bf16[128,288]{0,1:T(8,128)(2,1)}, u32[]{:S(2)}, u32[]{:S(2)}) collective-permute-start(bf16[128,288]{0,1:T(8,128)(2,1)} %param.12), channel_id=1, source_target_pairs={{0,1},{1,0},{2,3},{3,2},{4,5},{5,4},{6,7},{7,6},{8,9},{9,8},{10,11... | collective-permute-start | bytes 221192 | tf_op jit(solution)/shard_map/first/ppermute | solution.py:27
  7.1 36.2 %collective-permute-start.1 = (bf16[2,224,960]{2,1,0:T(8,128)(2,1)S(1)}, bf16[2,224,960]{2,1,0:T(8,128)(2,1)S(1)}, u32[]{:S(2)}, u32[]{:S(2)}) collective-permute-start(bf16[2,224,960]{2,1,0:T(8,128)(2,1)S(1)} %dynamic-slice_bitcast_fusion.refs_0_.refs_10_), channel_id=1, source_target_pairs={{0,8},{4,12},{8,0},{12,4},{16,24},{20,28},{24,16},{28,20},{1,9},{5... | collective-permute-start | bytes 2580488 | tf_op jit(solution)/shard_map/first/ppermute | solution.py:27
  8.7 54.9 %collective-permute-start = (bf16[2,224,960]{2,1,0:T(8,128)(2,1)S(1)}, bf16[2,224,960]{2,1,0:T(8,128)(2,1)}, u32[]{:S(2)}, u32[]{:S(2)}) collective-permute-start(bf16[2,224,960]{2,1,0:T(8,128)(2,1)S(1)} %dynamic-slice_bitcast_fusion.refs_0_.refs_10_), channel_id=1, source_target_pairs={{0,4},{4,0},{8,12},{12,8},{16,20},{20,16},{24,28},{28,24},{1,5},{5... | collective-permute-start | bytes 2580488 | tf_op jit(solution)/shard_map/first/ppermute | solution.py:27
  10.2 51.6 %all-to-all-start = ((bf16[2,2,224,960]{3,2,1,0:T(8,128)(2,1)}), bf16[2,2,224,960]{3,2,1,0:T(8,128)(2,1)}, u32[]{:S(2)}, u32[]{:S(2)}) async-start(bf16[2,2,224,960]{3,2,1,0:T(8,128)(2,1)} %copy-done.4), calls=%async_computation | async-start | bytes 3670016 | tf_op jit(solution)/shard_map/first/all_to_all | solution.py:53
  14.9 48.6 %collective-permute-start.9 = (bf16[448,1152]{1,0:T(8,128)(2,1)}, bf16[448,1152]{1,0:T(8,128)(2,1)}, u32[]{:S(2)}, u32[]{:S(2)}) collective-permute-start(bf16[448,1152]{1,0:T(8,128)(2,1)} %param.19), channel_id=1, source_target_pairs={{0,2},{1,3},{2,0},{3,1},{4,6},{5,7},{6,4},{7,5},{8,10},{9,11},{10,... | collective-permute-start | bytes 3096584 | tf_op jit(solution)/shard_map/first/ppermute | solution.py:27
  17.4 111.3 %collective-permute-start.24 = (bf16[448,1152]{1,0:T(8,128)(2,1)}, bf16[448,1152]{1,0:T(8,128)(2,1)}, u32[]{:S(2)}, u32[]{:S(2)}) collective-permute-start(bf16[448,1152]{1,0:T(8,128)(2,1)} %param.19), channel_id=1, source_target_pairs={{0,1},{1,0},{2,3},{3,2},{4,5},{5,4},{6,7},{7,6},{8,9},{9,8},{10,11... | collective-permute-start | bytes 3096584 | tf_op jit(solution)/shard_map/norm/ppermute | solution.py:27
  43.3 23.0 %collective-permute-start.2 = (bf16[2,224,960]{2,1,0:T(8,128)(2,1)S(1)}, bf16[2,224,960]{2,1,0:T(8,128)(2,1)}, u32[]{:S(2)}, u32[]{:S(2)}) collective-permute-start(bf16[2,224,960]{2,1,0:T(8,128)(2,1)S(1)} %collective-permute-done.1.refs_2_.refs_12_), channel_id=1, source_target_pairs={{0,4},{4,0},{8,12},{12,8},{16,20},{20,16},{24,28},{28,24},{1,5},{5... | collective-permute-start | bytes 2580488 | tf_op jit(solution)/shard_map/first/ppermute | solution.py:27
  50.2 13.3 %collective-permute-start.8 = (bf16[2,128,224]{2,1,0:T(8,128)(2,1)S(1)}, bf16[2,128,224]{2,1,0:T(8,128)(2,1)S(1)}, u32[]{:S(2)}, u32[]{:S(2)}) collective-permute-start(bf16[2,128,224]{2,1,0:T(8,128)(2,1)S(1)} %bitcast.218), channel_id=1, source_target_pairs={{0,16},{4,20},{8,24},{12,28},{16,0},{20,4},{24,8},{28,12},{1,17},{... | collective-permute-start | bytes 344072 | tf_op jit(solution)/shard_map/first/ppermute | solution.py:27
  67.2 7.6 %collective-permute-start.14 = (bf16[2,256,224]{2,1,0:T(8,128)(2,1)S(1)}, bf16[2,256,224]{2,1,0:T(8,128)(2,1)S(1)}, u32[]{:S(2)}, u32[]{:S(2)}) collective-permute-start(bf16[2,256,224]{2,1,0:T(8,128)(2,1)S(1)} %pad_maximum_fusion.7.refs_0_), channel_id=1, source_target_pairs={{0,2},{1,3},{2,0},{3,1},{4,6},{5,7},{6,4},{7,5},{8,10},{9,11},{10,... | collective-permute-start | bytes 688136 | tf_op jit(solution)/shard_map/second/ppermute | solution.py:27
  67.9 17.7 %collective-permute-start.10 = (bf16[224,960]{1,0:T(8,128)(2,1)S(1)}, bf16[224,960]{1,0:T(8,128)(2,1)S(1)}, u32[]{:S(2)}, u32[]{:S(2)}) collective-permute-start(bf16[224,960]{1,0:T(8,128)(2,1)S(1)} %get-tuple-element.51), channel_id=1, source_target_pairs={{0,4},{4,0},{8,12},{12,8},{16,20},{20,16},{24,28},{28,24},{1,5},{5... | collective-permute-start | bytes 1290248 | tf_op jit(solution)/shard_map/second/ppermute | solution.py:27
  69.7 19.6 %collective-permute-start.12 = (bf16[224,960]{1,0:T(8,128)(2,1)S(1)}, bf16[224,960]{1,0:T(8,128)(2,1)}, u32[]{:S(2)}, u32[]{:S(2)}) collective-permute-start(bf16[224,960]{1,0:T(8,128)(2,1)S(1)} %get-tuple-element.51), channel_id=1, source_target_pairs={{0,8},{4,12},{8,0},{12,4},{16,24},{20,28},{24,16},{28,20},{1,9},{5... | collective-permute-start | bytes 1290248 | tf_op jit(solution)/shard_map/second/ppermute | solution.py:27
  69.7 19.6 %collective-permute-start.11 = (bf16[224,960]{1,0:T(8,128)(2,1)S(1)}, bf16[224,960]{1,0:T(8,128)(2,1)}, u32[]{:S(2)}, u32[]{:S(2)}) collective-permute-start(bf16[224,960]{1,0:T(8,128)(2,1)S(1)} %get-tuple-element.52), channel_id=1, source_target_pairs={{0,4},{4,0},{8,12},{12,8},{16,20},{20,16},{24,28},{28,24},{1,5},{5... | collective-permute-start | bytes 1290248 | tf_op jit(solution)/shard_map/second/ppermute | solution.py:27
  74.8 18.8 %collective-permute-start.13 = (bf16[224,960]{1,0:T(8,128)(2,1)S(1)}, bf16[224,960]{1,0:T(8,128)(2,1)}, u32[]{:S(2)}, u32[]{:S(2)}) collective-permute-start(bf16[224,960]{1,0:T(8,128)(2,1)S(1)} %get-tuple-element.52), channel_id=1, source_target_pairs={{0,8},{4,12},{8,0},{12,4},{16,24},{20,28},{24,16},{28,20},{1,9},{5... | collective-permute-start | bytes 1290248 | tf_op jit(solution)/shard_map/second/ppermute | solution.py:27
  76.3 20.3 %all-to-all-start.1 = ((bf16[4,32,1152]{2,1,0:T(8,128)(2,1)}), bf16[4,32,1152]{2,1,0:T(8,128)(2,1)}, u32[]{:S(2)}, u32[]{:S(2)}) async-start(bf16[4,32,1152]{2,1,0:T(8,128)(2,1)} %broadcast_in_dim.83), calls=%async_computation.1 | async-start | bytes 589824 | tf_op jit(solution)/shard_map/third/all_to_all | solution.py:372
  93.6 5.9 %collective-permute-start.16 = (bf16[2,256,224]{2,1,0:T(8,128)(2,1)S(1)}, bf16[2,256,224]{2,1,0:T(8,128)(2,1)S(1)}, u32[]{:S(2)}, u32[]{:S(2)}) collective-permute-start(bf16[2,256,224]{2,1,0:T(8,128)(2,1)S(1)} %copy-done.21), channel_id=1, source_target_pairs={{0,1},{1,0},{2,3},{3,2},{4,5},{5,4},{6,7},{7,6},{8,9},{9,8},{10,11... | collective-permute-start | bytes 688136 | tf_op jit(solution)/shard_map/second/ppermute | solution.py:27
  96.6 14.2 %collective-permute-start.17 = (bf16[4,32,1152]{2,1,0:T(8,128)(2,1)}, bf16[4,32,1152]{2,1,0:T(8,128)(2,1)}, u32[]{:S(2)}, u32[]{:S(2)}) collective-permute-start(bf16[4,32,1152]{2,1,0:T(8,128)(2,1)} %all-to-all-done.1), channel_id=1, source_target_pairs={{0,4},{4,0},{8,12},{12,8},{16,20},{20,16},{24,28},{28,24},{1,5},{5... | collective-permute-start | bytes 884744 | tf_op jit(solution)/shard_map/third/ppermute | solution.py:27
  98.0 38.5 %collective-permute-start.25 = (bf16[448,1152]{1,0:T(8,128)(2,1)}, bf16[448,1152]{1,0:T(8,128)(2,1)}, u32[]{:S(2)}, u32[]{:S(2)}) collective-permute-start(bf16[448,1152]{1,0:T(8,128)(2,1)} %collective-permute-done.9), channel_id=1, source_target_pairs={{0,1},{1,0},{2,3},{3,2},{4,5},{5,4},{6,7},{7,6},{8,9},{9,8},{10,11... | collective-permute-start | bytes 3096584 | tf_op jit(solution)/shard_map/norm/ppermute | solution.py:27
  98.1 15.4 %collective-permute-start.18 = (bf16[224,960]{1,0:T(8,128)(2,1)}, bf16[224,960]{1,0:T(8,128)(2,1)}, u32[]{:S(2)}, u32[]{:S(2)}) collective-permute-start(bf16[224,960]{1,0:T(8,128)(2,1)} %collective-permute-done.12.refs_6_.refs_7_.refs_8_.refs_9_.refs_10_.refs_16_), channel_id=1, source_target_pairs={{0,4},{4,0},{8,12},{12,8},{16,20},{20,16},{24,28},{28,24},{1,5},{5... | collective-permute-start | bytes 1290248 | tf_op jit(solution)/shard_map/third/ppermute | solution.py:27
  100.3 13.3 %collective-permute-start.19 = (bf16[224,960]{1,0:T(8,128)(2,1)}, bf16[224,960]{1,0:T(8,128)(2,1)}, u32[]{:S(2)}, u32[]{:S(2)}) collective-permute-start(bf16[224,960]{1,0:T(8,128)(2,1)} %collective-permute-done.11.refs_8_.refs_18_), channel_id=1, source_target_pairs={{0,8},{4,12},{8,0},{12,4},{16,24},{20,28},{24,16},{28,20},{1,9},{5... | collective-permute-start | bytes 1290248 | tf_op jit(solution)/shard_map/third/ppermute | solution.py:27
  112.0 15.3 %collective-permute-start.21 = (bf16[256,1152]{1,0:T(8,128)(2,1)S(1)}, bf16[256,1152]{1,0:T(8,128)(2,1)}, u32[]{:S(2)}, u32[]{:S(2)}) collective-permute-start(bf16[256,1152]{1,0:T(8,128)(2,1)S(1)} %bitcast.227), channel_id=1, source_target_pairs={{0,2},{1,3},{2,0},{3,1},{4,6},{5,7},{6,4},{7,5},{8,10},{9,11},{10,... | collective-permute-start | bytes 1769480 | tf_op jit(solution)/shard_map/norm/ppermute | solution.py:27
  127.3 7.2 %collective-permute-start.22 = (bf16[8,2,32,224]{3,2,0,1:T(8,128)(2,1)S(1)}, bf16[8,2,32,224]{3,2,0,1:T(8,128)(2,1)S(1)}, u32[]{:S(2)}, u32[]{:S(2)}) collective-permute-start(bf16[8,2,32,224]{3,2,0,1:T(8,128)(2,1)S(1)} %fusion.29), channel_id=1, source_target_pairs={{0,2},{1,3},{2,0},{3,1},{4,6},{5,7},{6,4},{7,5},{8,10},{9,11},{10,... | collective-permute-start | bytes 688136 | tf_op jit(solution)/shard_map/image_forward/ppermute | solution.py:27
  131.0 17.2 %collective-permute-start.27 = (bf16[256,1152]{1,0:T(8,128)(2,1)S(1)}, bf16[256,1152]{1,0:T(8,128)(2,1)S(1)}, u32[]{:S(2)}, u32[]{:S(2)}) collective-permute-start(bf16[256,1152]{1,0:T(8,128)(2,1)S(1)} %bitcast.228), channel_id=1, source_target_pairs={{0,1},{1,0},{2,3},{3,2},{4,5},{5,4},{6,7},{7,6},{8,9},{9,8},{10,11... | collective-permute-start | bytes 1769480 | tf_op jit(solution)/shard_map/norm/ppermute | solution.py:27
  134.6 8.6 %collective-permute-start.23 = (bf16[8,32,224]{2,1,0:T(8,128)(2,1)S(1)}, bf16[8,32,224]{2,1,0:T(8,128)(2,1)S(1)}, u32[]{:S(2)}, u32[]{:S(2)}) collective-permute-start(bf16[8,32,224]{2,1,0:T(8,128)(2,1)S(1)} %fusion.55), channel_id=1, source_target_pairs={{0,16},{4,20},{8,24},{12,28},{16,0},{20,4},{24,8},{28,12},{1,17},{... | collective-permute-start | bytes 344072 | tf_op jit(solution)/shard_map/image_forward/ppermute | solution.py:27
  138.7 9.5 %collective-permute-start.28 = (bf16[256,1152]{1,0:T(8,128)(2,1)}, bf16[256,1152]{1,0:T(8,128)(2,1)S(1)}, u32[]{:S(2)}, u32[]{:S(2)}) collective-permute-start(bf16[256,1152]{1,0:T(8,128)(2,1)} %collective-permute-done.21), channel_id=1, source_target_pairs={{0,1},{1,0},{2,3},{3,2},{4,5},{5,4},{6,7},{7,6},{8,9},{9,8},{10,11... | collective-permute-start | bytes 1769480 | tf_op jit(solution)/shard_map/norm/ppermute | solution.py:27
  154.9 9.7 %collective-permute-start.33 = (bf16[8,32,224]{2,1,0:T(8,128)(2,1)S(1)}, bf16[8,32,224]{2,1,0:T(8,128)(2,1)S(1)}, u32[]{:S(2)}, u32[]{:S(2)}) collective-permute-start(bf16[8,32,224]{2,1,0:T(8,128)(2,1)S(1)} %bitcast.222), channel_id=1, source_target_pairs={{0,16},{4,20},{8,24},{12,28},{16,0},{20,4},{24,8},{28,12},{1,17},{... | collective-permute-start | bytes 344072 | tf_op jit(solution)/shard_map/image_backward/ppermute | solution.py:27
  156.8 25.3 %all-to-all-start.2 = ((bf16[8,32,1152]{2,1,0:T(8,128)(2,1)}), bf16[8,32,1152]{2,1,0:T(8,128)(2,1)S(1)}, u32[]{:S(2)}, u32[]{:S(2)}) async-start(bf16[8,32,1152]{2,1,0:T(8,128)(2,1)} %bitcast.47), calls=%async_computation.2 | async-start | bytes 1179648 | tf_op jit(solution)/shard_map/text_loss/all_to_all | solution.py:444
  161.3 5.4 %collective-permute-start.30 = (bf16[8,32,224]{2,1,0:T(8,128)(2,1)S(1)}, bf16[8,32,224]{2,1,0:T(8,128)(2,1)S(1)}, u32[]{:S(2)}, u32[]{:S(2)}) collective-permute-start(bf16[8,32,224]{2,1,0:T(8,128)(2,1)S(1)} %bitcast.223), channel_id=1, source_target_pairs={{0,2},{1,3},{2,0},{3,1},{4,6},{5,7},{6,4},{7,5},{8,10},{9,11},{10,... | collective-permute-start | bytes 344072 | tf_op jit(solution)/shard_map/image_backward/ppermute | solution.py:27
  164.6 5.5 %collective-permute-start.34 = (bf16[8,32,224]{2,1,0:T(8,128)(2,1)S(1)}, bf16[8,32,224]{2,1,0:T(8,128)(2,1)S(1)}, u32[]{:S(2)}, u32[]{:S(2)}) collective-permute-start(bf16[8,32,224]{2,1,0:T(8,128)(2,1)S(1)} %collective-permute-done.33.refs_4_), channel_id=1, source_target_pairs={{0,2},{1,3},{2,0},{3,1},{4,6},{5,7},{6,4},{7,5},{8,10},{9,11},{10,... | collective-permute-start | bytes 344072 | tf_op jit(solution)/shard_map/image_backward/ppermute | solution.py:27
  186.0 8.9 %collective-permute-start.38 = (bf16[2,256,256]{2,1,0:T(8,128)(2,1)}, bf16[2,256,256]{2,1,0:T(8,128)(2,1)S(1)}, u32[]{:S(2)}, u32[]{:S(2)}) collective-permute-start(bf16[2,256,256]{2,1,0:T(8,128)(2,1)} %fusion.28), channel_id=1, source_target_pairs={{0,2},{1,3},{2,0},{3,1},{4,6},{5,7},{6,4},{7,5},{8,10},{9,11},{10,... | collective-permute-start | bytes 786440 | tf_op jit(solution)/shard_map/image_backward/ppermute | solution.py:27
  195.0 8.8 %collective-permute-start.39 = (bf16[2,128,256]{2,1,0:T(8,128)(2,1)S(1)}, bf16[2,128,256]{2,1,0:T(8,128)(2,1)S(1)}, u32[]{:S(2)}, u32[]{:S(2)}) collective-permute-start(bf16[2,128,256]{2,1,0:T(8,128)(2,1)S(1)} %slice.221), channel_id=1, source_target_pairs={{0,16},{4,20},{8,24},{12,28},{16,0},{20,4},{24,8},{28,12},{1,17},{... | collective-permute-start | bytes 393224 | tf_op jit(solution)/shard_map/image_backward/ppermute | solution.py:27
  198.3 6.8 %collective-permute-start.43 = (bf16[1,128,292]{1,2,0:T(8,128)(2,1)S(1)}, bf16[1,128,292]{1,2,0:T(8,128)(2,1)S(1)}, u32[]{:S(2)}, u32[]{:S(2)}) collective-permute-start(bf16[1,128,292]{1,2,0:T(8,128)(2,1)S(1)} %maximum_bitcast_fusion), channel_id=1, source_target_pairs={{0,2},{1,3},{2,0},{3,1},{4,6},{5,7},{6,4},{7,5},{8,10},{9,11},{10,... | collective-permute-start | bytes 224264 | tf_op jit(solution)/shard_map/text_backward/ppermute | solution.py:27
  (51 other events, 352.7 us)

commit v7 on v6

--- a/solution.py
+++ b/solution.py
@@ -166,16 +166,20 @@
 
 def back_kernel(split, ids, *refs):
     parts, (before, gains), refs = refs[:8], refs[8:10], refs[10:]
-    outs, others, buffer, sems, upstreams = refs[11:]
+    outs, others, buffer, sems, upstreams, more = refs[11:]
     downs = fetch(1, refs[:11], buffer, sems)
     ups = fetch(0, refs[:11], buffer, sems)
     for copy in downs.values():
         copy.start()
     rows, hidden = before.shape
     width = buffer.shape[1]
-    for side in range(2):
-        for at, flip in enumerate(FLIPS):
-            upstreams[:, side * 4 + (ids[2] ^ flip)] = parts[side * 4 + at][...]
+    loads = []
+    for at in range(8):
+        row = at // 4 * 4 + (ids[2] ^ FLIPS[at % 4])
+        loads.append(pltpu.make_async_copy(parts[at], upstreams.at[:, row], more.at[at]))
+        loads[-1].start()
+    for copy in loads:
+        copy.wait()
     total = jnp.zeros((rows, hidden), F32)
     for at in range(8):
         downs[at].wait()
@@ -210,7 +214,7 @@
             ref[at // 2, at % 2, :, width:] = tail.astype(ref.dtype)
 
 
-def call(kernel, name, shapes, operands, weights=(), more=()):
+def call(kernel, name, shapes, operands, weights=(), more=(), places=None):
     scratch = []
     if weights:
         scratch.append(pltpu.VMEM((16,) + weights[0].shape[1:], BF16))
@@ -220,7 +224,7 @@
     return pl.pallas_call(
         kernel,
         out_shape=shapes,
-        in_specs=[SMEM] + [VMEM] * (len(operands) - 1) + [ANY] * len(weights),
+        in_specs=[SMEM] + (places or [VMEM] * (len(operands) - 1)) + [ANY] * len(weights),
         out_specs=tuple(VMEM for _ in shapes),
         scratch_shapes=scratch,
         compiler_params=PARAMS,
@@ -384,8 +388,6 @@
         share_x = swap(share, "grp", 2)
         every = [share, share_x, swap(share, "grp", 1), swap(share_x, "grp", 1)]
         every_text = jnp.concatenate(every)
-        heads = [image_head, head_x, swap(image_head, "grp", 1), swap(head_x, "grp", 1)]
-        head = place(heads, grp, FLIPS).reshape(members, width, embed_width)
 
     with jax.named_scope("image_forward"):
         shape = (8, 4, quarter, image_features // 8)
@@ -396,6 +398,9 @@
             (ids, scaled),
             weights[:7] + [weights[6]] * 4,
         )
+        head_x = tie(head_x, partial)
+        heads = [image_head, head_x, swap(image_head, "grp", 1), swap(head_x, "grp", 1)]
+        head = place(heads, grp, FLIPS).reshape(members, width, embed_width)
         before, gains, keep, send = call(
             forward_kernel,
             "forward",
@@ -405,7 +410,7 @@
                 jax.ShapeDtypeStruct(shape, F32),
                 jax.ShapeDtypeStruct(shape, BF16),
             ),
-            (ids, scaled, tie(partial, share, head)),
+            (ids, scaled, tie(partial, share)),
             weights,
         )
         total = (keep + swap(send, "grp", 1).astype(F32)).reshape(8, 2, 2, quarter, -1)
@@ -466,7 +471,11 @@
             shapes,
             (ids, *sides, before, gains),
             weights,
-            [pltpu.VMEM((8, 8, quarter, image_features // 8), BF16)],
+            [
+                pltpu.VMEM((8, 8, quarter, image_features // 8), BF16),
+                pltpu.SemaphoreType.DMA((8,)),
+            ],
+            [ANY] * 8 + [VMEM, VMEM],
         )
         if not split:
             tail = jnp.broadcast_to(send, (members,) + send.shape)

time: 207 us -> 209 us (level)
    unnamed x76 -> x74, local copies, waits for them, and re-layouts: 6.02 us -> 5.99 us
  transfers between devices with their start and end apart: 47 -> 47, of which waited for: 21 -> 20; matrix products, arithmetic and copies ran while one was open for 25% -> 25% of each run, Pallas kernels for 12% -> 12%
where the time goes in v7:
time: 209 us; the launch traced here: 207 us
  waiting for transfers between devices  66.7 us (32%)
  starting transfers between devices  52.8 us (25%)
  local copies, waits for them, and re-layouts  32 us (15%)
  Pallas kernels  25 us (12%)
  other arithmetic  14.4 us (7%)
  matrix products  13.7 us (7%)
  between operations  2.89 us (1%)
    ppermute x44, waiting for transfers between devices, swap(): lax.ppermute(value, axis, [(i, i ^ flip) for i in range(lax.axis_size(axi...  55.4 us
    ppermute x44, starting transfers between devices, swap(): lax.ppermute(value, axis, [(i, i ^ flip) for i in range(lax.axis_size(axi...  37.7 us
    pallas_call x4, Pallas kernels, call(): pl.pallas_call(kernel, out_shape=shapes, in_specs=[SMEM] + (places or [VM...  25 us
    dynamic_update_slice x15, local copies, waits for them, and re-layouts, place(): whole = lax.dynamic_update_index_in_dim(whole, part, index ^ flip, 0)  15.5 us
    dot_general x11, matrix products, dot(): return lax.dot_general(left, right, dims, preferred_element_type=F32)  13.7 us
    all_to_all x1, waiting for transfers between devices, exchange(): lax.all_to_all(halves, 'img', split_axis=0, concat_axis=0, tiled=True, ax...  8.83 us
    unnamed x74, local copies, waits for them, and re-layouts  5.99 us
    all_to_all x1, starting transfers between devices, shards(): lax.all_to_all(copies, 'img', split_axis=0, concat_axis=0, tiled=True, ax...  5.91 us
  transfers between devices with their start and end apart: 47, of which 20 were waited for; matrix products, arithmetic and copies ran while one was open for 25% of the time, Pallas kernels for 12%

profile of v7, /device:TPU:0, one launch (start us, length us, event | category | flops | bytes accessed | tf_op | source)
XLA Modules:
  0.0 207.4 jit_solution(7910382515034880233)
XLA Ops:
  0.6 3.0 %collective-permute-start.3 = (bf16[128,288]{0,1:T(8,128)(2,1)}, bf16[128,288]{0,1:T(8,128)(2,1)}, u32[]{:S(2)}, u32[]{:S(2)}) collective-permute-start(bf16[128,288]{0,1:T(8,128)(2,1)} %param.12), channel_id=1, source_target_pairs={{0,2},{1,3},{2,0},{3,1},{4,6},{5,7},{6,4},{7,5},{8,10},{9,11},{10,... | collective-permute-start | bytes 221192 | tf_op jit(solution)/shard_map/first/ppermute | solution.py:27
  10.2 4.7 %all-to-all-start = ((bf16[2,2,224,960]{3,2,1,0:T(8,128)(2,1)}), bf16[2,2,224,960]{3,2,1,0:T(8,128)(2,1)}, u32[]{:S(2)}, u32[]{:S(2)}) async-start(bf16[2,2,224,960]{3,2,1,0:T(8,128)(2,1)} %copy-done.4), calls=%async_computation | async-start | bytes 3670016 | tf_op jit(solution)/shard_map/first/all_to_all | solution.py:53
  29.1 14.2 %collective-permute-done.1.refs_2_.refs_12_ = bf16[2,224,960]{2,1,0:T(8,128)(2,1)S(1)} collective-permute-done((bf16[2,224,960]{2,1,0:T(8,128)(2,1)S(1)}, bf16[2,224,960]{2,1,0:T(8,128)(2,1)S(1)}, u32[]{:S(2)}, u32[]{:S(2)}) %collective-permute-start.1) | collective-permute-done | bytes 860192 | tf_op jit(solution)/shard_map/first/ppermute | solution.py:27
  43.3 2.5 %collective-permute-start.2 = (bf16[2,224,960]{2,1,0:T(8,128)(2,1)S(1)}, bf16[2,224,960]{2,1,0:T(8,128)(2,1)}, u32[]{:S(2)}, u32[]{:S(2)}) collective-permute-start(bf16[2,224,960]{2,1,0:T(8,128)(2,1)S(1)} %collective-permute-done.1.refs_2_.refs_12_), channel_id=1, source_target_pairs={{0,4},{4,0},{8,12},{12,8},{16,20},{20,16},{24,28},{28,24},{1,5},{5... | collective-permute-start | bytes 2580488 | tf_op jit(solution)/shard_map/first/ppermute | solution.py:27
  47.9 2.3 %collective-permute-done.7 = bf16[32,1152]{1,0:T(8,128)(2,1)S(1)} collective-permute-done((bf16[32,1152]{1,0:T(8,128)(2,1)S(1)}, bf16[32,1152]{1,0:T(8,128)(2,1)S(1)}, u32[]{:S(2)}, u32[]{:S(2)}) %collective-permute-start.7) | collective-permute-done | bytes 73760 | tf_op jit(solution)/shard_map/first/ppermute | solution.py:27
  50.3 2.7 %collective-permute-start.8 = (bf16[2,128,224]{2,1,0:T(8,128)(2,1)S(1)}, bf16[2,128,224]{2,1,0:T(8,128)(2,1)S(1)}, u32[]{:S(2)}, u32[]{:S(2)}) collective-permute-start(bf16[2,128,224]{2,1,0:T(8,128)(2,1)S(1)} %bitcast.218), channel_id=1, source_target_pairs={{0,16},{4,20},{8,24},{12,28},{16,0},{20,4},{24,8},{28,12},{1,17},{... | collective-permute-start | bytes 344072 | tf_op jit(solution)/shard_map/first/ppermute | solution.py:27
  53.0 8.8 %all-to-all-done = bf16[2,2,224,960]{3,2,1,0:T(8,128)(2,1)} async-done(((bf16[2,2,224,960]{3,2,1,0:T(8,128)(2,1)}), bf16[2,2,224,960]{3,2,1,0:T(8,128)(2,1)}, u32[]{:S(2)}, u32[]{:S(2)}) %all-to-all-start) | async-done | bytes 1720352 | tf_op jit(solution)/shard_map/first/all_to_all | solution.py:53
  63.6 2.7 %collective-permute-done.2.refs_4_.refs_14_ = bf16[2,224,960]{2,1,0:T(8,128)(2,1)} collective-permute-done((bf16[2,224,960]{2,1,0:T(8,128)(2,1)S(1)}, bf16[2,224,960]{2,1,0:T(8,128)(2,1)}, u32[]{:S(2)}, u32[]{:S(2)}) %collective-permute-start.2) | collective-permute-done | bytes 860192 | tf_op jit(solution)/shard_map/first/ppermute | solution.py:27
  70.0 4.8 %collective-permute-done.14.refs_1_ = bf16[2,256,224]{2,1,0:T(8,128)(2,1)S(1)} collective-permute-done((bf16[2,256,224]{2,1,0:T(8,128)(2,1)S(1)}, bf16[2,256,224]{2,1,0:T(8,128)(2,1)S(1)}, u32[]{:S(2)}, u32[]{:S(2)}) %collective-permute-start.14) | collective-permute-done | bytes 229408 | tf_op jit(solution)/shard_map/second/ppermute | solution.py:27
  76.3 5.9 %all-to-all-start.1 = ((bf16[4,32,1152]{2,1,0:T(8,128)(2,1)}), bf16[4,32,1152]{2,1,0:T(8,128)(2,1)}, u32[]{:S(2)}, u32[]{:S(2)}) async-start(bf16[4,32,1152]{2,1,0:T(8,128)(2,1)} %broadcast_in_dim.83), calls=%async_computation.1 | async-start | bytes 589824 | tf_op jit(solution)/shard_map/third/all_to_all | solution.py:376
  82.3 2.3 %broadcast_in_dim.84 = bf16[4,448,1152]{2,1,0:T(8,128)(2,1)} broadcast(bf16[]{:T(256)} %constant.207.clone.1), dimensions={} | broadcast | bytes 4128770 | tf_op jit(solution)/shard_map/image_forward/broadcast_in_dim | solution.py:31
  85.7 3.7 %collective-permute-done.11.refs_8_.refs_18_ = bf16[224,960]{1,0:T(8,128)(2,1)} collective-permute-done((bf16[224,960]{1,0:T(8,128)(2,1)S(1)}, bf16[224,960]{1,0:T(8,128)(2,1)}, u32[]{:S(2)}, u32[]{:S(2)}) %collective-permute-start.11) | collective-permute-done | bytes 430112 | tf_op jit(solution)/shard_map/second/ppermute | solution.py:27
  89.3 4.3 %collective-permute-done.13.refs_9_.refs_19_ = bf16[224,960]{1,0:T(8,128)(2,1)} collective-permute-done((bf16[224,960]{1,0:T(8,128)(2,1)S(1)}, bf16[224,960]{1,0:T(8,128)(2,1)}, u32[]{:S(2)}, u32[]{:S(2)}) %collective-permute-start.13) | collective-permute-done | bytes 430112 | tf_op jit(solution)/shard_map/second/ppermute | solution.py:27
  94.2 2.5 %all-to-all-done.1 = bf16[4,32,1152]{2,1,0:T(8,128)(2,1)} async-done(((bf16[4,32,1152]{2,1,0:T(8,128)(2,1)}), bf16[4,32,1152]{2,1,0:T(8,128)(2,1)}, u32[]{:S(2)}, u32[]{:S(2)}) %all-to-all-start.1) | async-done | bytes 294944 | tf_op jit(solution)/shard_map/third/all_to_all | solution.py:376
  100.2 2.1 %collective-permute-start.19 = (bf16[224,960]{1,0:T(8,128)(2,1)}, bf16[224,960]{1,0:T(8,128)(2,1)}, u32[]{:S(2)}, u32[]{:S(2)}) collective-permute-start(bf16[224,960]{1,0:T(8,128)(2,1)} %collective-permute-done.11.refs_8_.refs_18_), channel_id=1, source_target_pairs={{0,8},{4,12},{8,0},{12,4},{16,24},{20,28},{24,16},{28,20},{1,9},{5... | collective-permute-start | bytes 1290248 | tf_op jit(solution)/shard_map/third/ppermute | solution.py:27
  102.3 3.4 %norm.1 = (bf16[8,272,224]{2,1,0:T(8,128)(2,1)}, bf16[8,32,224]{2,1,0:T(8,128)(2,1)}, f32[256,1]{1,0:T(8,128)}, f32[256,1]{1,0:T(8,128)}) custom-call(s32[3]{0:T(128)} %pad_add_fusion.1.ids, bf16[2,256,224]{2,1,0:T(8,128)(2,1)} %copy-done.15, bf16[2,256,224]{2,1,0:T(8,128)(2,1)} %copy-done.20, bf16[2,256,224]{2,1,0:T(8,128)(2,1)} %copy-done.22, ...), custom_call_target="tpu_custom_call" | custom-call | bytes 12582912 | tf_op jit(solution)/shard_map/second/norm/pallas_call | solution.py:224
  105.7 5.0 %up.1.partial = f32[272,960]{1,0:T(8,128)} custom-call(s32[3]{0:T(128)} %pad_add_fusion.1.ids, bf16[8,272,224]{2,1,0:T(8,128)(2,1)} %get-tuple-element.59.scaled, bf16[2,224,960]{2,1,0:T(8,128)(2,1)} %copy-done.1, bf16[2,224,960]{2,1,0:T(8,128)(2,1)} %collective-permute-done.refs_1_.refs_11_, bf16[2,224,960]{2,1,0:T(8,128)(2,1)} %copy-done.5, ...), custom_call_target="tpu_custom_call" | custom-call | flops 1761607680 | bytes 18874368 | tf_op jit(solution)/shard_map/image_forward/up/pallas_call | solution.py:224
  113.5 8.0 %forward.1 = (f32[256,960]{1,0:T(8,128)}, f32[1,960]{1,0:T(1,128)}, f32[8,4,32,224]{3,2,1,0:T(8,128)}, bf16[8,4,32,224]{3,2,1,0:T(8,128)(2,1)}) custom-call(s32[3]{0:T(128)} %pad_add_fusion.1.ids, bf16[8,272,224]{2,1,0:T(8,128)(2,1)} %get-tuple-element.59.scaled, f32[272,960]{1,0:T(8,128)} %up.1.partial, bf16[2,224,960]{2,1,0:T(8,128)(2,1)} %copy-done.1, ...), custom_call_target="tpu_custom_call" | custom-call | flops 1761607680 | bytes 29360128 | tf_op jit(solution)/shard_map/image_forward/forward/pallas_call | solution.py:224
  121.8 2.3 %bitcast_dynamic-update-slice_fusion.2 = bf16[4,448,1152]{2,1,0:T(8,128)(2,1)} fusion(bf16[4,448,1152]{2,1,0:T(8,128)(2,1)} %bitcast_dynamic-update-slice_fusion.3, s32[]{:T(128)S(6)} %select_n.145, bf16[448,1152]{1,0:T(8,128)(2,1)} %collective-permute-done.9), kind=kLoop, calls=%fused_computation.14 | loop fusion | bytes 2064388 | tf_op jit(solution)/shard_map/image_forward/jit(dynamic_update_index_in_dim)/dynamic_update_slice | solution.py:33
  124.4 3.5 %collective-permute-done.21 = bf16[256,1152]{1,0:T(8,128)(2,1)} collective-permute-done((bf16[256,1152]{1,0:T(8,128)(2,1)S(1)}, bf16[256,1152]{1,0:T(8,128)(2,1)}, u32[]{:S(2)}, u32[]{:S(2)}) %collective-permute-start.21) | collective-permute-done | bytes 589856 | tf_op jit(solution)/shard_map/norm/ppermute | solution.py:27
  129.3 2.3 %bitcast_dynamic-update-slice_fusion.1 = bf16[4,448,1152]{2,1,0:T(8,128)(2,1)} fusion(bf16[4,448,1152]{2,1,0:T(8,128)(2,1)} %bitcast_dynamic-update-slice_fusion.2, s32[]{:T(128)S(6)} %select_n.146, bf16[448,1152]{1,0:T(8,128)(2,1)} %collective-permute-done.24), kind=kLoop, calls=%fused_computation.13 | loop fusion | bytes 2064388 | tf_op jit(solution)/shard_map/image_forward/jit(dynamic_update_index_in_dim)/dynamic_update_slice | solution.py:33
  132.1 3.7 %collective-permute-done.22 = bf16[8,2,32,224]{3,2,0,1:T(8,128)(2,1)S(1)} collective-permute-done((bf16[8,2,32,224]{3,2,0,1:T(8,128)(2,1)S(1)}, bf16[8,2,32,224]{3,2,0,1:T(8,128)(2,1)S(1)}, u32[]{:S(2)}, u32[]{:S(2)}) %collective-permute-start.22) | collective-permute-done | bytes 229408 | tf_op jit(solution)/shard_map/image_forward/ppermute | solution.py:27
  137.7 2.3 %bitcast_dynamic-update-slice_fusion = bf16[4,448,1152]{2,1,0:T(8,128)(2,1)} fusion(bf16[4,448,1152]{2,1,0:T(8,128)(2,1)} %bitcast_dynamic-update-slice_fusion.1, s32[]{:T(128)S(6)} %select_n.147, bf16[448,1152]{1,0:T(8,128)(2,1)} %collective-permute-done.25), kind=kLoop, calls=%fused_computation.12 | loop fusion | bytes 2064388 | tf_op jit(solution)/shard_map/image_forward/jit(dynamic_update_index_in_dim)/dynamic_update_slice | solution.py:33
  140.0 3.9 %collective-permute-done.23 = bf16[8,32,224]{2,1,0:T(8,128)(2,1)S(1)} collective-permute-done((bf16[8,32,224]{2,1,0:T(8,128)(2,1)S(1)}, bf16[8,32,224]{2,1,0:T(8,128)(2,1)S(1)}, u32[]{:S(2)}, u32[]{:S(2)}) %collective-permute-start.23) | collective-permute-done | bytes 114720 | tf_op jit(solution)/shard_map/image_forward/ppermute | solution.py:27
  144.2 3.1 %multiply_reduce_fusion.4 = (f32[32]{0:T(128)S(1)}, f32[32,1152]{1,0:T(8,128)S(1)}) fusion(bf16[32,1792]{1,0:T(8,128)(2,1)S(1)} %reshape.152, bf16[1792,1152]{1,0:T(8,128)(2,1)} %bitcast.42), kind=kOutput, calls=%fused_computation.111 | convolution fusion | flops 132194272 | bytes 4391040 | tf_op jit(solution)/shard_map/image_forward/dot_general | solution.py:43
  149.0 2.6 %multiply_reduce_fusion.3 = (f32[32]{0:T(128)S(1)}, f32[32,1152]{1,0:T(8,128)S(1)}) fusion(f32[32,1152]{1,0:T(8,128)S(1)} %get-tuple-element.130, f32[]{:T(128)} %bitcast.23, bf16[256,1152]{1,0:T(8,128)(2,1)S(1)} %collective-permute-done.28, bf16[256,1152]{1,0:T(8,128)(2,1)S(1)} %collective-permute-done.27, bf16[256,1152]{1,0:T(8,128)(2,1)} %collective-permute-done.21, ...), kind=kOutput, calls=%fused_computation.109 | convolution fusion | flops 170348512 | bytes 2658696 | tf_op jit(solution)/shard_map/image_loss/dot_general | solution.py:43
  151.9 3.4 %convolution_convert_fusion = bf16[32,1792]{1,0:T(8,128)(2,1)S(1)} fusion(bf16[32,1152]{1,0:T(8,128)(2,1)S(1)} %multiply_convert_fusion.6, bf16[1792,1152]{1,0:T(8,128)(2,1)} %bitcast.42), kind=kOutput, calls=%fused_computation.2 | convolution fusion | flops 132177920 | bytes 4317184 | tf_op jit(solution)/shard_map/image_loss/dot_general | solution.py:43
  157.6 4.5 %all-to-all-start.2 = ((bf16[8,32,1152]{2,1,0:T(8,128)(2,1)}), bf16[8,32,1152]{2,1,0:T(8,128)(2,1)S(1)}, u32[]{:S(2)}, u32[]{:S(2)}) async-start(bf16[8,32,1152]{2,1,0:T(8,128)(2,1)} %bitcast.47), calls=%async_computation.2 | async-start | bytes 1179648 | tf_op jit(solution)/shard_map/text_loss/all_to_all | solution.py:449
  167.9 2.8 %collective-permute-done.34.refs_5_ = bf16[8,32,224]{2,1,0:T(8,128)(2,1)S(1)} collective-permute-done((bf16[8,32,224]{2,1,0:T(8,128)(2,1)S(1)}, bf16[8,32,224]{2,1,0:T(8,128)(2,1)S(1)}, u32[]{:S(2)}, u32[]{:S(2)}) %collective-permute-start.34) | collective-permute-done | bytes 114720 | tf_op jit(solution)/shard_map/image_backward/ppermute | solution.py:27
  172.8 8.6 %back.1 = (f32[2,2,256,256]{3,2,1,0:T(8,128)}, bf16[2,2,256,256]{3,2,1,0:T(8,128)(2,1)}) custom-call(s32[3]{0:T(128)} %pad_add_fusion.1.ids, bf16[8,32,224]{2,1,0:T(8,128)(2,1)} %bitcast.225, bf16[8,32,224]{2,1,0:T(8,128)(2,1)} %copy-done.23, bf16[8,32,224]{2,1,0:T(8,128)(2,1)} %copy-done.24, bf16[8,32,224]{2,1,0:T(8,128)(2,1)} %copy-done.25, ...), custom_call_target="tpu_custom_call" | custom-call | flops 1761607680 | bytes 29360128 | tf_op jit(solution)/shard_map/image_backward/back/pallas_call | solution.py:224
  196.5 2.2 %collective-permute-start.39 = (bf16[2,128,256]{2,1,0:T(8,128)(2,1)S(1)}, bf16[2,128,256]{2,1,0:T(8,128)(2,1)S(1)}, u32[]{:S(2)}, u32[]{:S(2)}) collective-permute-start(bf16[2,128,256]{2,1,0:T(8,128)(2,1)S(1)} %slice.221), channel_id=1, source_target_pairs={{0,16},{4,20},{8,24},{12,28},{16,0},{20,4},{24,8},{28,12},{1,17},{... | collective-permute-start | bytes 393224 | tf_op jit(solution)/shard_map/image_backward/ppermute | solution.py:27
  201.4 3.9 %collective-permute-done.39 = bf16[2,128,256]{2,1,0:T(8,128)(2,1)S(1)} collective-permute-done((bf16[2,128,256]{2,1,0:T(8,128)(2,1)S(1)}, bf16[2,128,256]{2,1,0:T(8,128)(2,1)S(1)}, u32[]{:S(2)}, u32[]{:S(2)}) %collective-permute-start.39) | collective-permute-done | bytes 131104 | tf_op jit(solution)/shard_map/image_backward/ppermute | solution.py:27
  (247 shorter events, 72.5 us)
Async XLA Ops:
  0.6 16.7 %collective-permute-start.3 = (bf16[128,288]{0,1:T(8,128)(2,1)}, bf16[128,288]{0,1:T(8,128)(2,1)}, u32[]{:S(2)}, u32[]{:S(2)}) collective-permute-start(bf16[128,288]{0,1:T(8,128)(2,1)} %param.12), channel_id=1, source_target_pairs={{0,2},{1,3},{2,0},{3,1},{4,6},{5,7},{6,4},{7,5},{8,10},{9,11},{10,... | collective-permute-start | bytes 221192 | tf_op jit(solution)/shard_map/first/ppermute | solution.py:27
  3.6 15.4 %collective-permute-start.4 = (bf16[128,288]{0,1:T(8,128)(2,1)}, bf16[128,288]{0,1:T(8,128)(2,1)}, u32[]{:S(2)}, u32[]{:S(2)}) collective-permute-start(bf16[128,288]{0,1:T(8,128)(2,1)} %param.12), channel_id=1, source_target_pairs={{0,1},{1,0},{2,3},{3,2},{4,5},{5,4},{6,7},{7,6},{8,9},{9,8},{10,11... | collective-permute-start | bytes 221192 | tf_op jit(solution)/shard_map/first/ppermute | solution.py:27
  7.1 36.2 %collective-permute-start.1 = (bf16[2,224,960]{2,1,0:T(8,128)(2,1)S(1)}, bf16[2,224,960]{2,1,0:T(8,128)(2,1)S(1)}, u32[]{:S(2)}, u32[]{:S(2)}) collective-permute-start(bf16[2,224,960]{2,1,0:T(8,128)(2,1)S(1)} %dynamic-slice_bitcast_fusion.refs_0_.refs_10_), channel_id=1, source_target_pairs={{0,8},{4,12},{8,0},{12,4},{16,24},{20,28},{24,16},{28,20},{1,9},{5... | collective-permute-start | bytes 2580488 | tf_op jit(solution)/shard_map/first/ppermute | solution.py:27
  8.7 54.9 %collective-permute-start = (bf16[2,224,960]{2,1,0:T(8,128)(2,1)S(1)}, bf16[2,224,960]{2,1,0:T(8,128)(2,1)}, u32[]{:S(2)}, u32[]{:S(2)}) collective-permute-start(bf16[2,224,960]{2,1,0:T(8,128)(2,1)S(1)} %dynamic-slice_bitcast_fusion.refs_0_.refs_10_), channel_id=1, source_target_pairs={{0,4},{4,0},{8,12},{12,8},{16,20},{20,16},{24,28},{28,24},{1,5},{5... | collective-permute-start | bytes 2580488 | tf_op jit(solution)/shard_map/first/ppermute | solution.py:27
  10.2 51.6 %all-to-all-start = ((bf16[2,2,224,960]{3,2,1,0:T(8,128)(2,1)}), bf16[2,2,224,960]{3,2,1,0:T(8,128)(2,1)}, u32[]{:S(2)}, u32[]{:S(2)}) async-start(bf16[2,2,224,960]{3,2,1,0:T(8,128)(2,1)} %copy-done.4), calls=%async_computation | async-start | bytes 3670016 | tf_op jit(solution)/shard_map/first/all_to_all | solution.py:53
  14.9 48.6 %collective-permute-start.9 = (bf16[448,1152]{1,0:T(8,128)(2,1)}, bf16[448,1152]{1,0:T(8,128)(2,1)}, u32[]{:S(2)}, u32[]{:S(2)}) collective-permute-start(bf16[448,1152]{1,0:T(8,128)(2,1)} %param.19), channel_id=1, source_target_pairs={{0,2},{1,3},{2,0},{3,1},{4,6},{5,7},{6,4},{7,5},{8,10},{9,11},{10,... | collective-permute-start | bytes 3096584 | tf_op jit(solution)/shard_map/first/ppermute | solution.py:27
  17.4 111.9 %collective-permute-start.24 = (bf16[448,1152]{1,0:T(8,128)(2,1)}, bf16[448,1152]{1,0:T(8,128)(2,1)}, u32[]{:S(2)}, u32[]{:S(2)}) collective-permute-start(bf16[448,1152]{1,0:T(8,128)(2,1)} %param.19), channel_id=1, source_target_pairs={{0,1},{1,0},{2,3},{3,2},{4,5},{5,4},{6,7},{7,6},{8,9},{9,8},{10,11... | collective-permute-start | bytes 3096584 | tf_op jit(solution)/shard_map/image_forward/ppermute | solution.py:27
  43.3 23.0 %collective-permute-start.2 = (bf16[2,224,960]{2,1,0:T(8,128)(2,1)S(1)}, bf16[2,224,960]{2,1,0:T(8,128)(2,1)}, u32[]{:S(2)}, u32[]{:S(2)}) collective-permute-start(bf16[2,224,960]{2,1,0:T(8,128)(2,1)S(1)} %collective-permute-done.1.refs_2_.refs_12_), channel_id=1, source_target_pairs={{0,4},{4,0},{8,12},{12,8},{16,20},{20,16},{24,28},{28,24},{1,5},{5... | collective-permute-start | bytes 2580488 | tf_op jit(solution)/shard_map/first/ppermute | solution.py:27
  50.3 13.3 %collective-permute-start.8 = (bf16[2,128,224]{2,1,0:T(8,128)(2,1)S(1)}, bf16[2,128,224]{2,1,0:T(8,128)(2,1)S(1)}, u32[]{:S(2)}, u32[]{:S(2)}) collective-permute-start(bf16[2,128,224]{2,1,0:T(8,128)(2,1)S(1)} %bitcast.218), channel_id=1, source_target_pairs={{0,16},{4,20},{8,24},{12,28},{16,0},{20,4},{24,8},{28,12},{1,17},{... | collective-permute-start | bytes 344072 | tf_op jit(solution)/shard_map/first/ppermute | solution.py:27
  67.2 7.6 %collective-permute-start.14 = (bf16[2,256,224]{2,1,0:T(8,128)(2,1)S(1)}, bf16[2,256,224]{2,1,0:T(8,128)(2,1)S(1)}, u32[]{:S(2)}, u32[]{:S(2)}) collective-permute-start(bf16[2,256,224]{2,1,0:T(8,128)(2,1)S(1)} %pad_maximum_fusion.7.refs_0_), channel_id=1, source_target_pairs={{0,2},{1,3},{2,0},{3,1},{4,6},{5,7},{6,4},{7,5},{8,10},{9,11},{10,... | collective-permute-start | bytes 688136 | tf_op jit(solution)/shard_map/second/ppermute | solution.py:27
  67.9 17.7 %collective-permute-start.10 = (bf16[224,960]{1,0:T(8,128)(2,1)S(1)}, bf16[224,960]{1,0:T(8,128)(2,1)S(1)}, u32[]{:S(2)}, u32[]{:S(2)}) collective-permute-start(bf16[224,960]{1,0:T(8,128)(2,1)S(1)} %get-tuple-element.52), channel_id=1, source_target_pairs={{0,4},{4,0},{8,12},{12,8},{16,20},{20,16},{24,28},{28,24},{1,5},{5... | collective-permute-start | bytes 1290248 | tf_op jit(solution)/shard_map/second/ppermute | solution.py:27
  69.7 19.6 %collective-permute-start.12 = (bf16[224,960]{1,0:T(8,128)(2,1)S(1)}, bf16[224,960]{1,0:T(8,128)(2,1)}, u32[]{:S(2)}, u32[]{:S(2)}) collective-permute-start(bf16[224,960]{1,0:T(8,128)(2,1)S(1)} %get-tuple-element.52), channel_id=1, source_target_pairs={{0,8},{4,12},{8,0},{12,4},{16,24},{20,28},{24,16},{28,20},{1,9},{5... | collective-permute-start | bytes 1290248 | tf_op jit(solution)/shard_map/second/ppermute | solution.py:27
  69.7 19.6 %collective-permute-start.11 = (bf16[224,960]{1,0:T(8,128)(2,1)S(1)}, bf16[224,960]{1,0:T(8,128)(2,1)}, u32[]{:S(2)}, u32[]{:S(2)}) collective-permute-start(bf16[224,960]{1,0:T(8,128)(2,1)S(1)} %get-tuple-element.53), channel_id=1, source_target_pairs={{0,4},{4,0},{8,12},{12,8},{16,20},{20,16},{24,28},{28,24},{1,5},{5... | collective-permute-start | bytes 1290248 | tf_op jit(solution)/shard_map/second/ppermute | solution.py:27
  74.8 18.8 %collective-permute-start.13 = (bf16[224,960]{1,0:T(8,128)(2,1)S(1)}, bf16[224,960]{1,0:T(8,128)(2,1)}, u32[]{:S(2)}, u32[]{:S(2)}) collective-permute-start(bf16[224,960]{1,0:T(8,128)(2,1)S(1)} %get-tuple-element.53), channel_id=1, source_target_pairs={{0,8},{4,12},{8,0},{12,4},{16,24},{20,28},{24,16},{28,20},{1,9},{5... | collective-permute-start | bytes 1290248 | tf_op jit(solution)/shard_map/second/ppermute | solution.py:27
  76.3 20.3 %all-to-all-start.1 = ((bf16[4,32,1152]{2,1,0:T(8,128)(2,1)}), bf16[4,32,1152]{2,1,0:T(8,128)(2,1)}, u32[]{:S(2)}, u32[]{:S(2)}) async-start(bf16[4,32,1152]{2,1,0:T(8,128)(2,1)} %broadcast_in_dim.83), calls=%async_computation.1 | async-start | bytes 589824 | tf_op jit(solution)/shard_map/third/all_to_all | solution.py:376
  93.6 5.8 %collective-permute-start.15 = (bf16[2,256,224]{2,1,0:T(8,128)(2,1)S(1)}, bf16[2,256,224]{2,1,0:T(8,128)(2,1)S(1)}, u32[]{:S(2)}, u32[]{:S(2)}) collective-permute-start(bf16[2,256,224]{2,1,0:T(8,128)(2,1)S(1)} %pad_maximum_fusion.7.refs_0_), channel_id=1, source_target_pairs={{0,1},{1,0},{2,3},{3,2},{4,5},{5,4},{6,7},{7,6},{8,9},{9,8},{10,11... | collective-permute-start | bytes 688136 | tf_op jit(solution)/shard_map/second/ppermute | solution.py:27
  93.6 8.7 %collective-permute-start.16 = (bf16[2,256,224]{2,1,0:T(8,128)(2,1)S(1)}, bf16[2,256,224]{2,1,0:T(8,128)(2,1)}, u32[]{:S(2)}, u32[]{:S(2)}) collective-permute-start(bf16[2,256,224]{2,1,0:T(8,128)(2,1)S(1)} %copy-done.21), channel_id=1, source_target_pairs={{0,1},{1,0},{2,3},{3,2},{4,5},{5,4},{6,7},{7,6},{8,9},{9,8},{10,11... | collective-permute-start | bytes 688136 | tf_op jit(solution)/shard_map/second/ppermute | solution.py:27
  96.6 14.2 %collective-permute-start.17 = (bf16[4,32,1152]{2,1,0:T(8,128)(2,1)}, bf16[4,32,1152]{2,1,0:T(8,128)(2,1)}, u32[]{:S(2)}, u32[]{:S(2)}) collective-permute-start(bf16[4,32,1152]{2,1,0:T(8,128)(2,1)} %all-to-all-done.1), channel_id=1, source_target_pairs={{0,4},{4,0},{8,12},{12,8},{16,20},{20,16},{24,28},{28,24},{1,5},{5... | collective-permute-start | bytes 884744 | tf_op jit(solution)/shard_map/third/ppermute | solution.py:27
  98.0 15.5 %collective-permute-start.18 = (bf16[224,960]{1,0:T(8,128)(2,1)}, bf16[224,960]{1,0:T(8,128)(2,1)}, u32[]{:S(2)}, u32[]{:S(2)}) collective-permute-start(bf16[224,960]{1,0:T(8,128)(2,1)} %collective-permute-done.12.refs_6_.refs_7_.refs_8_.refs_9_.refs_10_.refs_16_), channel_id=1, source_target_pairs={{0,4},{4,0},{8,12},{12,8},{16,20},{20,16},{24,28},{28,24},{1,5},{5... | collective-permute-start | bytes 1290248 | tf_op jit(solution)/shard_map/third/ppermute | solution.py:27
  100.2 13.3 %collective-permute-start.19 = (bf16[224,960]{1,0:T(8,128)(2,1)}, bf16[224,960]{1,0:T(8,128)(2,1)}, u32[]{:S(2)}, u32[]{:S(2)}) collective-permute-start(bf16[224,960]{1,0:T(8,128)(2,1)} %collective-permute-done.11.refs_8_.refs_18_), channel_id=1, source_target_pairs={{0,8},{4,12},{8,0},{12,4},{16,24},{20,28},{24,16},{28,20},{1,9},{5... | collective-permute-start | bytes 1290248 | tf_op jit(solution)/shard_map/third/ppermute | solution.py:27
  110.7 27.0 %collective-permute-start.25 = (bf16[448,1152]{1,0:T(8,128)(2,1)}, bf16[448,1152]{1,0:T(8,128)(2,1)}, u32[]{:S(2)}, u32[]{:S(2)}) collective-permute-start(bf16[448,1152]{1,0:T(8,128)(2,1)} %collective-permute-done.9), channel_id=1, source_target_pairs={{0,1},{1,0},{2,3},{3,2},{4,5},{5,4},{6,7},{7,6},{8,9},{9,8},{10,11... | collective-permute-start | bytes 3096584 | tf_op jit(solution)/shard_map/image_forward/ppermute | solution.py:27
  112.0 15.9 %collective-permute-start.21 = (bf16[256,1152]{1,0:T(8,128)(2,1)S(1)}, bf16[256,1152]{1,0:T(8,128)(2,1)}, u32[]{:S(2)}, u32[]{:S(2)}) collective-permute-start(bf16[256,1152]{1,0:T(8,128)(2,1)S(1)} %bitcast.227), channel_id=1, source_target_pairs={{0,2},{1,3},{2,0},{3,1},{4,6},{5,7},{6,4},{7,5},{8,10},{9,11},{10,... | collective-permute-start | bytes 1769480 | tf_op jit(solution)/shard_map/norm/ppermute | solution.py:27
  127.9 7.9 %collective-permute-start.22 = (bf16[8,2,32,224]{3,2,0,1:T(8,128)(2,1)S(1)}, bf16[8,2,32,224]{3,2,0,1:T(8,128)(2,1)S(1)}, u32[]{:S(2)}, u32[]{:S(2)}) collective-permute-start(bf16[8,2,32,224]{3,2,0,1:T(8,128)(2,1)S(1)} %fusion.29), channel_id=1, source_target_pairs={{0,2},{1,3},{2,0},{3,1},{4,6},{5,7},{6,4},{7,5},{8,10},{9,11},{10,... | collective-permute-start | bytes 688136 | tf_op jit(solution)/shard_map/image_forward/ppermute | solution.py:27
  131.6 17.4 %collective-permute-start.27 = (bf16[256,1152]{1,0:T(8,128)(2,1)S(1)}, bf16[256,1152]{1,0:T(8,128)(2,1)S(1)}, u32[]{:S(2)}, u32[]{:S(2)}) collective-permute-start(bf16[256,1152]{1,0:T(8,128)(2,1)S(1)} %bitcast.228), channel_id=1, source_target_pairs={{0,1},{1,0},{2,3},{3,2},{4,5},{5,4},{6,7},{7,6},{8,9},{9,8},{10,11... | collective-permute-start | bytes 1769480 | tf_op jit(solution)/shard_map/norm/ppermute | solution.py:27
  131.6 17.4 %collective-permute-start.28 = (bf16[256,1152]{1,0:T(8,128)(2,1)}, bf16[256,1152]{1,0:T(8,128)(2,1)S(1)}, u32[]{:S(2)}, u32[]{:S(2)}) collective-permute-start(bf16[256,1152]{1,0:T(8,128)(2,1)} %collective-permute-done.21), channel_id=1, source_target_pairs={{0,1},{1,0},{2,3},{3,2},{4,5},{5,4},{6,7},{7,6},{8,9},{9,8},{10,11... | collective-permute-start | bytes 1769480 | tf_op jit(solution)/shard_map/norm/ppermute | solution.py:27
  135.9 8.0 %collective-permute-start.23 = (bf16[8,32,224]{2,1,0:T(8,128)(2,1)S(1)}, bf16[8,32,224]{2,1,0:T(8,128)(2,1)S(1)}, u32[]{:S(2)}, u32[]{:S(2)}) collective-permute-start(bf16[8,32,224]{2,1,0:T(8,128)(2,1)S(1)} %fusion.55), channel_id=1, source_target_pairs={{0,16},{4,20},{8,24},{12,28},{16,0},{20,4},{24,8},{28,12},{1,17},{... | collective-permute-start | bytes 344072 | tf_op jit(solution)/shard_map/image_forward/ppermute | solution.py:27
  155.6 9.7 %collective-permute-start.33 = (bf16[8,32,224]{2,1,0:T(8,128)(2,1)S(1)}, bf16[8,32,224]{2,1,0:T(8,128)(2,1)S(1)}, u32[]{:S(2)}, u32[]{:S(2)}) collective-permute-start(bf16[8,32,224]{2,1,0:T(8,128)(2,1)S(1)} %bitcast.222), channel_id=1, source_target_pairs={{0,16},{4,20},{8,24},{12,28},{16,0},{20,4},{24,8},{28,12},{1,17},{... | collective-permute-start | bytes 344072 | tf_op jit(solution)/shard_map/image_backward/ppermute | solution.py:27
  157.6 26.1 %all-to-all-start.2 = ((bf16[8,32,1152]{2,1,0:T(8,128)(2,1)}), bf16[8,32,1152]{2,1,0:T(8,128)(2,1)S(1)}, u32[]{:S(2)}, u32[]{:S(2)}) async-start(bf16[8,32,1152]{2,1,0:T(8,128)(2,1)} %bitcast.47), calls=%async_computation.2 | async-start | bytes 1179648 | tf_op jit(solution)/shard_map/text_loss/all_to_all | solution.py:449
  165.3 5.5 %collective-permute-start.34 = (bf16[8,32,224]{2,1,0:T(8,128)(2,1)S(1)}, bf16[8,32,224]{2,1,0:T(8,128)(2,1)S(1)}, u32[]{:S(2)}, u32[]{:S(2)}) collective-permute-start(bf16[8,32,224]{2,1,0:T(8,128)(2,1)S(1)} %collective-permute-done.33.refs_4_), channel_id=1, source_target_pairs={{0,2},{1,3},{2,0},{3,1},{4,6},{5,7},{6,4},{7,5},{8,10},{9,11},{10,... | collective-permute-start | bytes 344072 | tf_op jit(solution)/shard_map/image_backward/ppermute | solution.py:27
  187.6 8.8 %collective-permute-start.38 = (bf16[2,256,256]{2,1,0:T(8,128)(2,1)}, bf16[2,256,256]{2,1,0:T(8,128)(2,1)S(1)}, u32[]{:S(2)}, u32[]{:S(2)}) collective-permute-start(bf16[2,256,256]{2,1,0:T(8,128)(2,1)} %fusion.28), channel_id=1, source_target_pairs={{0,2},{1,3},{2,0},{3,1},{4,6},{5,7},{6,4},{7,5},{8,10},{9,11},{10,... | collective-permute-start | bytes 786440 | tf_op jit(solution)/shard_map/image_backward/ppermute | solution.py:27
  196.5 8.7 %collective-permute-start.39 = (bf16[2,128,256]{2,1,0:T(8,128)(2,1)S(1)}, bf16[2,128,256]{2,1,0:T(8,128)(2,1)S(1)}, u32[]{:S(2)}, u32[]{:S(2)}) collective-permute-start(bf16[2,128,256]{2,1,0:T(8,128)(2,1)S(1)} %slice.221), channel_id=1, source_target_pairs={{0,16},{4,20},{8,24},{12,28},{16,0},{20,4},{24,8},{28,12},{1,17},{... | collective-permute-start | bytes 393224 | tf_op jit(solution)/shard_map/image_backward/ppermute | solution.py:27
  199.9 6.7 %collective-permute-start.43 = (bf16[1,128,292]{1,2,0:T(8,128)(2,1)S(1)}, bf16[1,128,292]{1,2,0:T(8,128)(2,1)S(1)}, u32[]{:S(2)}, u32[]{:S(2)}) collective-permute-start(bf16[1,128,292]{1,2,0:T(8,128)(2,1)S(1)} %maximum_bitcast_fusion), channel_id=1, source_target_pairs={{0,2},{1,3},{2,0},{3,1},{4,6},{5,7},{6,4},{7,5},{8,10},{9,11},{10,... | collective-permute-start | bytes 224264 | tf_op jit(solution)/shard_map/text_backward/ppermute | solution.py:27
  (50 other events, 352.9 us)
